TPU v7x, 512 devices: a whole 4x8x8 slice. The times are simulated.
512 devices in a mesh: dp: 8 (over z), cells: 64 (over y, x, core).
Axes of the slice: x: 4, y: 8, z: 8, core: 2. Of those that a mesh axis runs over, the one named last changes fastest.
Arguments:
- vectors: bfloat16 [262144, 768], P(('dp', 'cells')), may hold values from -7 to 7
- cell_of: int32 [262144], P(('dp', 'cells')), may hold values from 0 to 2047, as said below
- cell_slot: int32 [2048], replicated, may hold values from 0 to 2047, as said below
- coarse: bfloat16 [2048, 768], P('cells'), may hold values from -6 to 6
- fine_book: bfloat16 [2048, 256, 768], P(('dp', 'cells')), may hold values from -8.375 to 8.375
Outputs:
- coarse_share: float32 [2048], replicated
- fine_next: bfloat16 [2048, 256, 768], P(('dp', 'cells'))
- distortion: float32 [262144], P(('dp', 'cells'))
Inputs may be any that keep to these rules, and one draw needn't show every extreme that they name: `cell_slot`: A permutation: every slot holds exactly one cell. The slots s with s // 4 = g lie on the device of flat index g over dp then cells. `cell_of`: every vector's slot lies on a device of the vector's own dp index. Of the vectors of one device, at most 16 have slots on any one device, and some devices receive exactly 16 from every device of their dp index.
All inputs are finite; a program needn't handle non-finite values.
Results may differ from a plain program's by a relative error of at most 0.0026.
Values may be sent and summed in bfloat16 or wider, within the bound.
No kernel may reach another device: no remote copies, remote signals or barrier semaphores. Data moves between devices by JAX's collectives and lax.ppermute only.
A program may use at most 64 MiB of HBM per device.

v0:
```python
import jax
import jax.numpy as jnp
from jax import lax
from jax.sharding import PartitionSpec as P

sharpness = 0.0625


def distance_block(points, point_squares, centres):
    wide = centres.astype(jnp.float32)
    centre_squares = jnp.sum(wide * wide, axis=1)
    products = lax.dot_general(
        points, centres, (((1,), (1,)), ((), ())), preferred_element_type=jnp.float32
    )
    return point_squares[:, None] + centre_squares[None, :] - 2.0 * products


def fine_owner(residual, local_cell, book):
    cells_here, fine_count, feature_count = book.shape
    flat_book = book.reshape(cells_here * fine_count, feature_count)
    present = (local_cell >= 0).astype(jnp.float32)
    chosen = jnp.maximum(local_cell, 0)
    residual_wide = residual.astype(jnp.float32)
    distance = distance_block(residual, jnp.sum(residual_wide * residual_wide, axis=1), flat_book)
    column_cell = jnp.arange(cells_here * fine_count, dtype=jnp.int32) // fine_count
    inside = column_cell[None, :] == chosen[:, None]
    scores = jnp.where(inside, -sharpness * distance, -jnp.inf)
    weights = jax.nn.softmax(scores, axis=1) * present[:, None]
    spread = jnp.sum(jnp.where(inside, weights * distance, 0.0), axis=1) / feature_count
    fine_mass = jnp.sum(weights, axis=0)
    totals = lax.dot_general(
        weights.astype(jnp.bfloat16),
        residual,
        (((0,), (0,)), ((), ())),
        preferred_element_type=jnp.float32,
    )
    updated = (flat_book.astype(jnp.float32) + totals) / (1.0 + fine_mass[:, None])
    return (spread, updated.astype(jnp.bfloat16).reshape(book.shape))


def on_device(vectors, cell_of, cell_slot, coarse, fine_book):
    cells_axis = lax.axis_size("cells")
    row_count, feature_count = vectors.shape
    cells_here = fine_book.shape[0]
    capacity = 2 * row_count // cells_axis
    vector_wide = vectors.astype(jnp.float32)
    vector_squares = jnp.sum(vector_wide * vector_wide, axis=1)
    my_slot = cell_slot[cell_of]
    dest_column = my_slot // cells_here % cells_axis
    local_cell = my_slot % cells_here
    onehot = (dest_column[:, None] == jnp.arange(cells_axis, dtype=jnp.int32)[None, :]).astype(
        jnp.int32
    )
    earlier = jnp.cumsum(onehot, axis=0) - onehot
    position = dest_column * capacity + jnp.sum(earlier * onehot, axis=1)
    centres = lax.all_gather(coarse, "cells", axis=0, tiled=True)
    distance = distance_block(vectors, vector_squares, centres)
    picked = centres[cell_of]
    payload = (vector_wide - picked.astype(jnp.float32)).astype(jnp.bfloat16)
    send_rows = (
        jnp.zeros((cells_axis * capacity, feature_count), jnp.bfloat16).at[position].set(payload)
    )
    send_cells = jnp.full((cells_axis * capacity,), -1, jnp.int32).at[position].set(local_cell)
    got_rows, got_cells = (
        lax.all_to_all(
            send_rows.reshape(cells_axis, capacity, feature_count),
            "cells",
            split_axis=0,
            concat_axis=0,
            tiled=True,
        ),
        lax.all_to_all(
            send_cells.reshape(cells_axis, capacity),
            "cells",
            split_axis=0,
            concat_axis=0,
            tiled=True,
        ),
    )
    probs = jax.nn.softmax(-sharpness * distance, axis=1)
    share_local = jnp.sum(probs, axis=0)
    coarse_share = lax.psum(share_local, ("dp", "cells")) * (cells_here / row_count)
    got_rows = got_rows.reshape(cells_axis * capacity, feature_count)
    got_cells = got_cells.reshape(cells_axis * capacity)
    spread, fine_next = fine_owner(got_rows, got_cells, fine_book)
    returned = lax.all_to_all(
        spread.reshape(cells_axis, capacity), "cells", split_axis=0, concat_axis=0, tiled=True
    )
    distortion = returned.reshape(cells_axis * capacity)[position]
    return (coarse_share, fine_next, distortion)


def solution(mesh):
    return jax.shard_map(
        on_device,
        mesh=mesh,
        in_specs=(
            P(("dp", "cells"), None),
            P(("dp", "cells")),
            P(),
            P("cells", None),
            P(("dp", "cells"), None, None),
        ),
        out_specs=(P(), P(("dp", "cells"), None, None), P(("dp", "cells"))),
        check_vma=False,
    )
```

profile of v0, /device:TPU:1, one launch (start us, length us, event | category | flops | bytes accessed | tf_op | source)
XLA Modules:
  0.0 283.5 jit_solution(4195400880622908779)
XLA Ops:
  7.2 0.0 copy-start
  7.2 0.0 all-gather.2.cloned.1.call-start
  7.2 0.7 all-gather.2.cloned.1.call-update
  7.9 0.7 compare_select_fusion.5
  8.6 0.0 copy-done
  8.6 3.1 %gather_fusion = s32[512]{0:T(512)S(1)} fusion(s32[2048]{0:T(1024)S(1)} %copy-done, s32[1024]{0:T(1024)S(1)} %pad_clamp_fusion.1), kind=kCustom, calls=%fused_computation | custom fusion | bytes 6144 | tf_op jit(solution)/shard_map/gather | solution.py:48
  11.8 1.2 reduce-window.6
  13.0 0.2 slice_reduce_fusion
  13.3 0.1 fusion.14
  13.5 2.4 scatter_custom_fusion
  15.9 0.7 all_to_all.13
  16.6 11.6 %all-to-all-start = ((s32[64,1,16]{2,1,0:T(1,128)}), s32[64,1,16]{2,1,0:T(1,128)S(1)}, u32[]{:S(2)}, u32[]{:S(2)}) async-start(s32[64,1,16]{2,1,0:T(1,128)} %bitcast.6), calls=%async_computation | async-start | bytes 65536 | tf_op jit(solution)/shard_map/all_to_all | solution.py:72
  28.2 72.6 %all-gather.2.cloned.1.call-done = bf16[2048,768]{1,0:T(8,128)(2,1)} async-done(((bf16[32,768]{1,0:T(8,128)(2,1)}), bf16[2048,768]{1,0:T(8,128)(2,1)}) %all-gather.2.cloned.1.call-update) | async-done | bytes 3145744 | tf_op jit(solution)/shard_map/all_gather | solution.py:56
  100.8 8.3 %scatter_custom_fusion.1 = bf16[1024,768]{1,0:T(8,128)(2,1)} fusion(s32[512]{0:T(512)S(1)} %bitcast.64, bf16[512,768]{1,0:T(8,128)(2,1)} %param.5, bf16[]{:T(256)} %constant.86.clone.1, bf16[2048,768]{1,0:T(8,128)(2,1)} %all-gather.2.cloned.1.call-done, s32[1024]{0:T(1024)S(1)} %pad_clamp_fusion.1), kind=kCustom, calls=%fused_computation.26 | custom fusion | flops 1572864 | bytes 5509122 | tf_op jit(solution)/shard_map/scatter | solution.py:61
  109.1 0.0 copy-start.2
  109.1 0.0 all-to-all-done
  109.1 6.8 %all-to-all-start.1 = ((bf16[64,16,768]{2,1,0:T(8,128)(2,1)}), bf16[64,16,768]{2,1,0:T(8,128)(2,1)}, u32[]{:S(2)}, u32[]{:S(2)}) async-start(bf16[64,16,768]{2,1,0:T(8,128)(2,1)} %bitcast.53), calls=%async_computation.1 | async-start | bytes 3145728 | tf_op jit(solution)/shard_map/all_to_all | solution.py:65
  116.0 1.8 multiply_reduce_fusion.1
  117.8 1.4 fusion.7
  119.2 0.1 maximum_reduce_fusion
  119.3 0.1 max.15
  119.3 0.1 fusion.16
  119.4 0.1 reshape.217
  119.5 0.0 copy-done.2
  119.5 0.7 multiply_reduce_fusion
  120.2 3.2 %fusion.34 = (f32[512]{0:T(512)S(1)}, f32[512,2048]{1,0:T(8,128)S(1)}) fusion(bf16[512,768]{1,0:T(8,128)(2,1)} %param.5, bf16[2048,768]{1,0:T(8,128)(2,1)S(1)} %copy-done.2, f32[2048]{0:T(1024)S(1)} %multiply_reduce_fusion, f32[512]{0:T(512)S(1)} %fusion.7), kind=kOutput, calls=%fused_computation.94 | convolution fusion | flops 1615855104 | bytes 8138752 | tf_op jit(solution)/shard_map/dot_general | solution.py:12
  123.4 0.0 copy-start.3
  123.5 0.7 fusion.1
  124.2 1.0 divide_reduce_fusion
  125.2 117.3 %psum.7 = f32[2048]{0:T(1024)S(1)} all-reduce(f32[2048]{0:T(1024)S(1)} %divide_reduce_fusion), channel_id=1, replica_groups=mesh['dp'=8,'cells'=64] {'dp','cells'}, use_global_device_ids=true, to_apply=%region_5.6 | all-reduce | flops 2048 | bytes 16384 | tf_op jit(solution)/shard_map/psum | solution.py:82
  242.5 0.6 broadcast_multiply_fusion
  243.1 0.0 all-to-all-done.1
  243.1 1.8 multiply_reduce_fusion.2
  244.9 0.1 add.124
  245.0 0.0 copy-done.3
  245.0 3.5 %fusion.33 = (f32[1024]{0:T(1024)S(1)}, f32[1024,1024]{0,1:T(8,128)S(1)}) fusion(f32[1024]{0:T(1024)S(1)} %bitcast.56, f32[1024]{0:T(1024)S(1)} %add.124, s32[1024]{0:T(1024)S(1)} %max.15, s32[1024]{0:T(1024)S(1)} %add_select_fusion, bf16[1024,768]{1,0:T(8,128)(2,1)} %bitcast.8, bf16[1024,768]{1,0:T(8,128)(2,1)S(1)} %bitcast.54), kind=kOutput, calls=%fused_computation.93 | convolution fusion | flops 1617951744 | bytes 7360512 | tf_op jit(solution)/shard_map/dot_general | solution.py:12
  248.5 0.0 copy-start.1
  248.5 1.8 fusion.2
  250.3 2.8 fusion
  253.1 0.0 copy-done.1
  253.1 0.7 div.90
  253.8 8.7 %all-to-all-start.2 = ((f32[64,1,16]{2,1,0:T(1,128)}), f32[64,1,16]{2,1,0:T(1,128)S(1)}, u32[]{:S(2)}, u32[]{:S(2)}) async-start(f32[64,1,16]{2,1,0:T(1,128)} %bitcast.10), calls=%async_computation.2 | async-start | bytes 65536 | tf_op jit(solution)/shard_map/all_to_all | solution.py:86
  262.5 6.2 %divide_convert_fusion = bf16[1024,768]{1,0:T(8,128)(2,1)} fusion(bf16[1024,768]{1,0:T(8,128)(2,1)S(1)} %bitcast.55, bf16[1024,768]{1,0:T(8,128)(2,1)} %bitcast.8, f32[1024]{0:T(1024)S(1)} %get-tuple-element.12, f32[1024]{0:T(1024)S(1)} %reshape.217, f32[1024]{0:T(1024)S(1)} %fusion.2, f32[1024]{0:T(1024)S(1)} %get-tuple-element.9, ...), kind=kOutput, calls=%fused_computation.17 | convolution fusion | flops 1624244224 | bytes 8945664 | tf_op jit(solution)/shard_map/dot_general | solution.py:31
  268.7 3.2 %all-to-all-done.2 = f32[64,1,16]{2,1,0:T(1,128)S(1)} async-done(((f32[64,1,16]{2,1,0:T(1,128)}), f32[64,1,16]{2,1,0:T(1,128)S(1)}, u32[]{:S(2)}, u32[]{:S(2)}) %all-to-all-start.2) | async-done | bytes 4128 | tf_op jit(solution)/shard_map/all_to_all | solution.py:86
  271.9 0.5 broadcast.290
  272.4 0.7 reduce.15
  273.1 0.1 reshape.216
  273.2 3.4 %gather_fusion.1 = f32[512]{0:T(512)} fusion(f32[1024]{0:T(1024)S(1)} %reshape.216, s32[1024]{0:T(1024)S(1)} %pad_clamp_fusion), kind=kCustom, calls=%fused_computation.2 | custom fusion | bytes 6144 | tf_op jit(solution)/shard_map/gather | solution.py:89
  (11 shorter events, 0.1 us)
Async XLA Ops:
  7.2 1.4 copy-start
  7.2 93.7 %all-gather.2.cloned.1.call-start = ((), (), s32[]{:S(2)}) async-start(), calls=%async_computation.3 | async-start | bytes 3194880 | tf_op jit(solution)/shard_map/all_gather | solution.py:56
  16.6 92.5 %all-to-all-start = ((s32[64,1,16]{2,1,0:T(1,128)}), s32[64,1,16]{2,1,0:T(1,128)S(1)}, u32[]{:S(2)}, u32[]{:S(2)}) async-start(s32[64,1,16]{2,1,0:T(1,128)} %bitcast.6), calls=%async_computation | async-start | bytes 65536 | tf_op jit(solution)/shard_map/all_to_all | solution.py:72
  109.1 10.4 %copy-start.2 = (bf16[2048,768]{1,0:T(8,128)(2,1)S(1)}, bf16[2048,768]{1,0:T(8,128)(2,1)}, u32[]{:S(2)}) copy-start(bf16[2048,768]{1,0:T(8,128)(2,1)} %all-gather.2.cloned.1.call-done) | copy-start | bytes 9437188
  109.1 134.0 %all-to-all-start.1 = ((bf16[64,16,768]{2,1,0:T(8,128)(2,1)}), bf16[64,16,768]{2,1,0:T(8,128)(2,1)}, u32[]{:S(2)}, u32[]{:S(2)}) async-start(bf16[64,16,768]{2,1,0:T(8,128)(2,1)} %bitcast.53), calls=%async_computation.1 | async-start | bytes 3145728 | tf_op jit(solution)/shard_map/all_to_all | solution.py:65
  123.4 121.5 %copy-start.3 = (bf16[4,256,768]{2,1,0:T(8,128)(2,1)S(1)}, bf16[4,256,768]{2,1,0:T(8,128)(2,1)}, u32[]{:S(2)}) copy-start(bf16[4,256,768]{2,1,0:T(8,128)(2,1)} %param.9) | copy-start | bytes 4718596
  248.5 4.6 %copy-start.1 = (f32[1024,1024]{0,1:T(8,128)}, f32[1024,1024]{0,1:T(8,128)S(1)}, u32[]{:S(2)}) copy-start(f32[1024,1024]{0,1:T(8,128)S(1)} %get-tuple-element.10) | copy-start | bytes 12582916
  253.8 18.1 %all-to-all-start.2 = ((f32[64,1,16]{2,1,0:T(1,128)}), f32[64,1,16]{2,1,0:T(1,128)S(1)}, u32[]{:S(2)}, u32[]{:S(2)}) async-start(f32[64,1,16]{2,1,0:T(1,128)} %bitcast.10), calls=%async_computation.2 | async-start | bytes 65536 | tf_op jit(solution)/shard_map/all_to_all | solution.py:86
Sparse Core Ops, SparseCore 0:
  11.4 89.4 all-gather.1
where the time goes:
time: 284 us; the launch traced here: 283 us
  blocking collectives  117 us (41%)
  waiting for transfers between devices  76.5 us (27%)
  starting transfers between devices  27.2 us (10%)
  other arithmetic  23.8 us (8%)
  between operations  14.2 us (5%)
  matrix products  13 us (5%)
  local copies, waits for them, and re-layouts  11.4 us (4%)
    psum x1, blocking collectives, on_device(): lax.psum(share_local, ('dp', 'cells')) * (cells_here / row_count)  117 us
    all_gather x1, waiting for transfers between devices, on_device(): centres = lax.all_gather(coarse, 'cells', axis=0, tiled=True)  72.6 us
    all_to_all x1, starting transfers between devices, on_device(): lax.all_to_all(send_cells.reshape(cells_axis, capacity), 'cells', split_a...  11.6 us
    all_to_all x1, starting transfers between devices, on_device(): lax.all_to_all(spread.reshape(cells_axis, capacity), 'cells', split_axis=...  8.72 us
    scatter x1, other arithmetic, on_device(): jnp.zeros((cells_axis * capacity, feature_count), jnp.bfloat16).at[position]  8.28 us
    all_to_all x1, starting transfers between devices, on_device(): lax.all_to_all(send_rows.reshape(cells_axis, capacity, feature_count), 'c...  6.83 us
    dot_general x2, matrix products, distance_block(): lax.dot_general(points, centres, (((1,), (1,)), ((), ())), preferred_elem...  6.76 us
    dot_general x1, matrix products, fine_owner(): lax.dot_general(weights.astype(jnp.bfloat16), residual, (((0,), (0,)), ((...  6.21 us
  transfers between devices with their start and end apart: 4, of which 2 were waited for; matrix products, arithmetic and copies ran while one was open for 11% of the time, Pallas kernels for 0%

commit v1 on v0

v1 whole, which is shorter than its diff:
```python
import functools

import jax
import jax.numpy as jnp
from jax import lax
from jax.experimental import pallas as pl
from jax.experimental.pallas import tpu as pltpu
from jax.sharding import Mesh, PartitionSpec as P

sharpness = 0.0625
Z, Y, X, CORES = 8, 8, 4, 2
PLANE = ("y", "x", "c")
EVERY = ("z", "y", "x", "c")
SETS = 4
f32, bf16, i32 = jnp.float32, jnp.bfloat16, jnp.int32
VMEM = pl.BlockSpec(memory_space=pltpu.VMEM)
SMEM = pl.BlockSpec(memory_space=pltpu.SMEM)


def params(cost):
    return dict(
        compiler_params=pltpu.CompilerParams(vmem_limit_bytes=48 * 2**20),
        cost_estimate=pl.CostEstimate(flops=cost, bytes_accessed=4 * 2**20, transcendentals=0),
    )


def iota(shape, axis):
    return lax.broadcasted_iota(i32, shape, axis)


def dot(a, b, ca, cb, precision=None):
    return lax.dot_general(
        a, b, (((ca,), (cb,)), ((), ())), preferred_element_type=f32, precision=precision
    )


def as_row(column):
    return jnp.transpose(jnp.broadcast_to(column, (column.shape[0], 128)))[0:1, :]


def route_kernel(owned, cell, table, vectors, send, meta, place):
    owners, cap, _ = send.shape
    rows = vectors.shape[0]
    high, low = table.shape
    cell_of = cell[...]
    slots = table[...]
    in_high = (iota((high, rows), 0) == cell_of // low).astype(bf16)
    in_low = iota((low, rows), 0) == cell_of % low
    owner_table = ((slots // owned) % owners).astype(bf16)
    local_table = (slots % owned).astype(bf16)
    owner = jnp.sum(jnp.where(in_low, dot(owner_table, in_high, 0, 0), 0.0), axis=0, keepdims=True)
    local = jnp.sum(jnp.where(in_low, dot(local_table, in_high, 0, 0), 0.0), axis=0, keepdims=True)
    at_owner = iota((owners, rows), 0) == owner.astype(i32)
    before = (iota((rows, rows), 0) < iota((rows, rows), 1)).astype(bf16)
    earlier = dot(at_owner.astype(bf16), before, 1, 0)
    rank = jnp.sum(jnp.where(at_owner, earlier, 0.0), axis=0, keepdims=True).astype(i32)
    position = owner.astype(i32) * cap + rank
    place[...] = position
    at_rank = (iota((cap, rows), 0) == rank).astype(bf16)
    found = dot(jnp.where(at_owner, local + 1.0, 0.0).astype(bf16), at_rank, 1, 1) - 1.0
    meta[...] = found.reshape(owners, 1, cap)
    block = 256
    for b in range(owners * cap // block):
        pick = (iota((block, rows), 0) + b * block == position).astype(bf16)
        moved = dot(pick, vectors[...], 1, 0).astype(bf16)
        send[b * block // cap : (b + 1) * block // cap] = moved.reshape(block // cap, cap, -1)


def route(vectors, cell_of, cell_slot, owners, cap, owned):
    rows, features = vectors.shape
    return pl.pallas_call(
        functools.partial(route_kernel, owned),
        out_shape=(
            jax.ShapeDtypeStruct((owners, cap, features), bf16),
            jax.ShapeDtypeStruct((owners, 1, cap), f32),
            jax.ShapeDtypeStruct((1, rows), i32),
        ),
        in_specs=[VMEM] * 3,
        out_specs=(VMEM,) * 3,
        name="route",
        **params(2 * 10**9),
    )(cell_of.reshape(1, rows), cell_slot.reshape(-1, 64), vectors)


def squares_kernel(book, vectors, book_squares, vector_squares):
    block = 256
    for b in range(book.shape[0] // block):
        at = slice(b * block, (b + 1) * block)
        wide = book[at].astype(f32)
        book_squares[at] = jnp.sum(wide * wide, axis=1, keepdims=True)
    for b in range(vectors.shape[0] // block):
        at = slice(b * block, (b + 1) * block)
        wide = vectors[at].astype(f32)
        vector_squares[:, at] = as_row(jnp.sum(wide * wide, axis=1, keepdims=True))


def squares(book, vectors):
    return pl.pallas_call(
        squares_kernel,
        out_shape=(
            jax.ShapeDtypeStruct((book.shape[0], 1), f32),
            jax.ShapeDtypeStruct((1, vectors.shape[0]), f32),
        ),
        in_specs=[VMEM] * 2,
        out_specs=(VMEM,) * 2,
        name="squares",
        **params(10**9),
    )(book, vectors)


def coarse_kernel(
    where, vectors, vector_squares, slots, own, right, left, far_a, far_b, own2, right2, left2, far_a2, far_b2,
    share, mine, scores,
):
    base, quarter, core = where[0], where[1], where[2]
    rows = vectors.shape[0]
    groups = scores.shape[0]
    picked = jnp.zeros((8, vectors.shape[1]), f32)
    top = jnp.full((1, rows), -jnp.inf, f32)
    half = groups // 2
    for side, chunks in ((core, (own, right, left, far_a, far_b)), (1 - core, (own2, right2, left2, far_a2, far_b2))):
        for chunk, step, start in zip(chunks, (0, 1, 3, 2, 2), (0, 0, 0, 0, half), strict=True):
            count = chunk.shape[0] // 8
            at = side * SETS + (quarter + step) % SETS
            points = chunk[...]
            wide = points.astype(f32)
            distance = (
                vector_squares[...] + jnp.sum(wide * wide, axis=1, keepdims=True) - 2.0 * dot(points, vectors[...], 1, 1)
            )
            score = -sharpness * distance
            top = jnp.maximum(top, jnp.max(score, axis=0, keepdims=True))
            scores[start : start + count, at] = score.reshape(count, 8, rows)
            held = slots[at][:, start * 8 : (start + count) * 8]
            inside = (iota((8, count * 8), 0) + base == held) & (iota((8, count * 8), 0) < SETS)
            picked = picked + dot(inside.astype(bf16), points, 1, 0)
    mine[...] = picked.astype(bf16)
    total = jnp.zeros((1, rows), f32)
    blocks = groups // 2
    for b in range(blocks):
        e = jnp.exp(scores[2 * b : 2 * b + 2].reshape(128, rows) - top)
        total = total + jnp.sum(e, axis=0, keepdims=True)
        scores[2 * b : 2 * b + 2] = e.reshape(2, 8, 8, rows)
    inverse = 1.0 / total
    for b in range(blocks):
        probs = scores[2 * b : 2 * b + 2].reshape(128, rows) * inverse
        lanes = probs[:, 0:128]
        for j in range(1, rows // 128):
            lanes = lanes + probs[:, j * 128 : (j + 1) * 128]
        share[b : b + 1, :] = jnp.sum(jnp.transpose(lanes), axis=0, keepdims=True)


def coarse_part(where, vectors, vector_squares, slots, chunks):
    rows, features = vectors.shape
    groups = Y * X
    return pl.pallas_call(
        coarse_kernel,
        out_shape=(
            jax.ShapeDtypeStruct((groups // 2, 128), f32),
            jax.ShapeDtypeStruct((8, features), bf16),
        ),
        in_specs=[SMEM] + [VMEM] * (3 + len(chunks)),
        out_specs=(VMEM,) * 2,
        scratch_shapes=[pltpu.VMEM((groups, CORES * SETS, 8, rows), f32)],
        name="coarse_part",
        **params(2 * 10**9),
    )(where, vectors, vector_squares, slots, *chunks)


def fine_kernel(got, meta, mine, book, book_squares, spread, weights, residual, mass):
    owners, _, cap = meta.shape
    rows, features = got.shape
    count = book.shape[0]
    fine = count // SETS
    spread_places = (iota((cap, rows), 1) % cap == iota((cap, rows), 0)).astype(bf16)
    at_owner = iota((owners, rows), 1) // cap == iota((owners, rows), 0)
    across = dot(meta[...].reshape(owners, cap).astype(bf16), spread_places, 1, 0)
    local = jnp.sum(jnp.where(at_owner, across, 0.0), axis=0, keepdims=True)
    block = 256
    parts = []
    for b in range(rows // block):
        at = slice(b * block, (b + 1) * block)
        slot = local[:, at]
        inside = [slot == s for s in range(SETS)]
        chosen = (iota((8, block), 0).astype(f32) == slot).astype(bf16)
        base = dot(chosen, mine[...], 0, 0)
        moved = (got[at].astype(f32) - base).astype(bf16)
        residual[at] = moved
        wide = moved.astype(f32)
        moved_squares = as_row(jnp.sum(wide * wide, axis=1, keepdims=True))
        distance = jnp.zeros((fine, block), f32)
        for s in range(SETS):
            of = slice(s * fine, (s + 1) * fine)
            here = moved_squares + book_squares[of] - 2.0 * dot(book[of], moved, 1, 1)
            distance = jnp.where(inside[s], here, distance)
        score = -sharpness * distance
        e = jnp.exp(score - jnp.max(score, axis=0, keepdims=True))
        weight = e * ((slot >= 0.0).astype(f32) / jnp.sum(e, axis=0, keepdims=True))
        parts.append(jnp.sum(weight * distance, axis=0, keepdims=True) / features)
        for s in range(SETS):
            of = slice(s * fine, (s + 1) * fine)
            only = jnp.where(inside[s], weight, 0.0)
            weights[of, at] = only.astype(bf16)
            part = jnp.sum(only, axis=1, keepdims=True)
            mass[of] = part if b == 0 else mass[of] + part
    row = jnp.concatenate(parts, axis=1)
    spread[...] = dot(
        jnp.where(at_owner, row, 0.0), spread_places.astype(f32), 1, 1, lax.Precision.HIGHEST
    ).reshape(owners, 1, cap)


def fine_part(got, meta, mine, book, book_squares):
    owners, _, cap = meta.shape
    rows, features = got.shape
    count = book.shape[0]
    return pl.pallas_call(
        fine_kernel,
        out_shape=(
            jax.ShapeDtypeStruct((owners, 1, cap), f32),
            jax.ShapeDtypeStruct((count, rows), bf16),
            jax.ShapeDtypeStruct((rows, features), bf16),
            jax.ShapeDtypeStruct((count, 1), f32),
        ),
        in_specs=[VMEM] * 5,
        out_specs=(VMEM,) * 4,
        name="fine_part",
        **params(3 * 10**9),
    )(got, meta, mine, book, book_squares)


def update_kernel(book, weights, residual, mass, out):
    block = 256
    for b in range(book.shape[0] // block):
        at = slice(b * block, (b + 1) * block)
        total = dot(weights[at], residual[...], 1, 0)
        out[at] = ((book[at].astype(f32) + total) * (1.0 / (1.0 + mass[at]))).astype(bf16)


def update(book, weights, residual, mass):
    return pl.pallas_call(
        update_kernel,
        out_shape=jax.ShapeDtypeStruct(book.shape, bf16),
        in_specs=[VMEM] * 4,
        out_specs=VMEM,
        name="update",
        **params(3 * 10**9),
    )(book, weights, residual, mass)


def pick_kernel(returned, place, out):
    owners, _, cap = returned.shape
    rows = place.shape[1]
    position = place[...]
    at_owner = (iota((owners, rows), 0) == position // cap).astype(f32)
    at_rank = iota((cap, rows), 0) == position % cap
    across = dot(returned[...].reshape(owners, cap), at_owner, 0, 0, lax.Precision.HIGHEST)
    out[...] = jnp.sum(jnp.where(at_rank, across, 0.0), axis=0, keepdims=True)


def pick(returned, place):
    return pl.pallas_call(
        pick_kernel,
        out_shape=jax.ShapeDtypeStruct(place.shape, f32),
        in_specs=[VMEM] * 2,
        out_specs=VMEM,
        name="pick",
        **params(10**8),
    )(returned, place)


def exchange(x, axes):
    return lax.all_to_all(x, axes, 0, 0, tiled=True)


def add_over(x, axes, count):
    return jnp.sum(exchange(jnp.broadcast_to(x[None], (count, *x.shape)), axes), axis=0)


def gather_coarse(coarse, quarter):
    features = coarse.shape[1]
    rows = coarse.shape[0] // SETS
    part = lax.dynamic_slice_in_dim(coarse, quarter * rows, rows, 0)
    groups = Y * X
    own = exchange(jnp.broadcast_to(part[None], (groups, rows, features)), ("y", "x"))
    own = own.reshape(groups * rows, features)
    up = [(i, (i + 1) % Z) for i in range(Z)]
    down = [(i, (i - 1) % Z) for i in range(Z)]
    right = lax.ppermute(own, "z", down)
    left = lax.ppermute(own, "z", up)
    half = groups * rows // 2
    far_a = lax.ppermute(right[:half], "z", down)
    far_b = lax.ppermute(left[half:], "z", up)
    chunks = (own, right, left, far_a, far_b)
    return chunks + tuple(lax.ppermute(chunk, "c", [(0, 1), (1, 0)]) for chunk in chunks)


def on_device(vectors, cell_of, cell_slot, coarse, fine_book):
    rows, features = vectors.shape
    owned, fine, _ = fine_book.shape
    owners = Y * X * CORES
    cap = 2 * rows // owners
    cells = cell_slot.shape[0]
    z, c = lax.axis_index("z"), lax.axis_index("c")
    base = lax.axis_index(EVERY) * owned
    where = jnp.stack([base, z % SETS, c]).astype(i32)
    book = fine_book.reshape(owned * fine, features)

    send, meta, place = route(vectors, cell_of, cell_slot, owners, cap, owned)
    got = exchange(send, PLANE).reshape(owners * cap, features)
    got_meta = exchange(meta, PLANE)
    chunks = gather_coarse(coarse, z % SETS)
    book_squares, vector_squares = squares(book, vectors)
    slots = cell_slot.reshape(Y * X, CORES, SETS, 8).transpose(1, 2, 0, 3).reshape(CORES * SETS, 1, Y * X * 8)
    share, mine = coarse_part(where, vectors, vector_squares, slots, chunks)
    share = add_over(share, ("z", "c"), Z * CORES)
    share = add_over(share, ("y", "x"), Y * X)
    coarse_share = (share * (owned / rows)).reshape(cells)

    spread, weights, residual, mass = fine_part(got, got_meta, mine, book, book_squares)
    returned = exchange(spread, PLANE)
    fine_next = update(book, weights, residual, mass).reshape(fine_book.shape)
    distortion = pick(returned, place).reshape(rows)
    return (coarse_share, fine_next, distortion)


def solution(mesh):
    grid = Mesh(mesh.devices.reshape(Z, Y, X, CORES), EVERY)
    return jax.shard_map(
        on_device,
        mesh=grid,
        in_specs=(P(EVERY, None), P(EVERY), P(), P(PLANE, None), P(EVERY, None, None)),
        out_specs=(P(), P(EVERY, None, None), P(EVERY)),
        check_vma=False,
    )
```

time: 284 us -> 191 us (0.67)
  blocking collectives: 117 us -> 39.3 us
  starting transfers between devices: 27.2 us -> 56.3 us
  other arithmetic: 23.8 us -> 1.69 us
  Pallas kernels: 0 us -> 17.5 us
  waiting for transfers between devices: 76.5 us -> 59.6 us
  between operations: 14.2 us -> 0.91 us
  matrix products: 13 us -> 0 us
  local copies, waits for them, and re-layouts: 11.4 us -> 15 us
    psum x1 -> x0, blocking collectives: 117 us -> none  [on_device(): lax.psum(share_local, ('dp', 'cells')) * (cells_here / row_count)]
    all_gather x1 -> x0, waiting for transfers between devices: 72.6 us -> none  [on_device(): centres = lax.all_gather(coarse, 'cells', axis=0, tiled=True)]
    all_to_all x3 -> x4, waiting for transfers between devices: 3.18 us -> 54.6 us  [exchange(): return lax.all_to_all(x, axes, 0, 0, tiled=True)]
    all_to_all x0 -> x2, blocking collectives: none -> 39.3 us  [exchange(): return lax.all_to_all(x, axes, 0, 0, tiled=True)]
    ppermute x0 -> x9, starting transfers between devices: none -> 33.3 us  [the longest x5 14.3 us: gather_coarse(): lax.ppermute(chunk, 'c', [(0, 1), (1, 0)])]
    pallas_call x0 -> x6, Pallas kernels: none -> 17.5 us  [the longest x1 5.28 us: coarse_part(): pl.pallas_call(coarse_kernel, out_shape=(jax.ShapeDtypeStruct((groups //...]
    dot_general x3 -> x0, matrix products: 13 us -> none  [the longest x2 6.76 us: distance_block(): lax.dot_general(points, centres, (((1,), (1,)), ((), ())), preferred_elem...]
    reduce_sum x9 -> x2, other arithmetic: 12 us -> 1.01 us  [add_over(): jnp.sum(exchange(jnp.broadcast_to(x[None], (count, *x.shape)), axes), axi...]
  transfers between devices with their start and end apart: 4 -> 13, of which waited for: 2 -> 5; matrix products, arithmetic and copies ran while one was open for 11% -> 3% of each run, Pallas kernels for 0% -> 3%
where the time goes in v1:
time: 191 us; the launch traced here: 190 us
  waiting for transfers between devices  59.6 us (31%)
  starting transfers between devices  56.3 us (29%)
  blocking collectives  39.3 us (21%)
  Pallas kernels  17.5 us (9%)
  local copies, waits for them, and re-layouts  15 us (8%)
    all_to_all x4, waiting for transfers between devices, exchange(): return lax.all_to_all(x, axes, 0, 0, tiled=True)  54.6 us
    all_to_all x2, blocking collectives, exchange(): return lax.all_to_all(x, axes, 0, 0, tiled=True)  39.3 us
    all_to_all x4, starting transfers between devices, exchange(): return lax.all_to_all(x, axes, 0, 0, tiled=True)  23 us
    ppermute x5, starting transfers between devices, gather_coarse(): lax.ppermute(chunk, 'c', [(0, 1), (1, 0)])  14.3 us
    unnamed x26, local copies, waits for them, and re-layouts  10.9 us
    ppermute x1, starting transfers between devices, gather_coarse(): right = lax.ppermute(own, 'z', down)  8.59 us
    pallas_call x1, Pallas kernels, coarse_part(): pl.pallas_call(coarse_kernel, out_shape=(jax.ShapeDtypeStruct((groups //...  5.28 us
    pallas_call x1, Pallas kernels, fine_part(): pl.pallas_call(fine_kernel, out_shape=(jax.ShapeDtypeStruct((owners, 1, c...  5.26 us
  transfers between devices with their start and end apart: 13, of which 5 were waited for; matrix products, arithmetic and copies ran while one was open for 3% of the time, Pallas kernels for 3%

profile of v1, /device:TPU:1, one launch (start us, length us, event | category | flops | bytes accessed | tf_op | source)
XLA Modules:
  0.0 190.2 jit_solution(10165200040128796595)
XLA Ops:
  0.6 0.0 copy-start
  0.6 0.0 copy-start.12
  0.7 0.0 copy-start.1
  0.7 0.7 copy-done
  1.5 24.1 %all_to_all.30 = bf16[32,8,768]{2,1,0:T(8,128)(2,1)S(1)} all-to-all(bf16[32,8,768]{2,1,0:T(8,128)(2,1)S(1)} %broadcast_in_dim.6), channel_id=1, replica_groups=mesh['z'=8,'y'=8,'x'=4,'c'=2] {'y','x'}, dimensions={0} | all-to-all | bytes 786432 | tf_op jit(solution)/shard_map/all_to_all | solution.py:271
  25.6 4.0 %collective-permute-start.1 = (bf16[256,768]{1,0:T(8,128)(2,1)S(1)}, bf16[256,768]{1,0:T(8,128)(2,1)S(1)}, u32[]{:S(2)}, u32[]{:S(2)}) collective-permute-start(bf16[256,768]{1,0:T(8,128)(2,1)S(1)} %bitcast.15), channel_id=1, source_target_pairs={{0,64},{64,128},{128,192},{192,256},{256,320},{320,384},{384,448},... | collective-permute-start | bytes 1179656 | tf_op jit(solution)/shard_map/ppermute | solution.py:288
  29.6 8.6 %collective-permute-start = (bf16[256,768]{1,0:T(8,128)(2,1)S(1)}, bf16[256,768]{1,0:T(8,128)(2,1)S(1)}, u32[]{:S(2)}, u32[]{:S(2)}) collective-permute-start(bf16[256,768]{1,0:T(8,128)(2,1)S(1)} %bitcast.16), channel_id=1, source_target_pairs={{0,448},{64,0},{128,64},{192,128},{256,192},{320,256},{384,320},{4... | collective-permute-start | bytes 1179656 | tf_op jit(solution)/shard_map/ppermute | solution.py:287
  38.2 5.0 %collective-permute-done.1.left = bf16[256,768]{1,0:T(8,128)(2,1)S(1)} collective-permute-done((bf16[256,768]{1,0:T(8,128)(2,1)S(1)}, bf16[256,768]{1,0:T(8,128)(2,1)S(1)}, u32[]{:S(2)}, u32[]{:S(2)}) %collective-permute-start.1) | collective-permute-done | bytes 393248 | tf_op jit(solution)/shard_map/ppermute | solution.py:288
  43.2 0.7 slice.9
  43.9 1.9 %collective-permute-start.3 = (bf16[128,768]{1,0:T(8,128)(2,1)}, bf16[128,768]{1,0:T(8,128)(2,1)S(1)}, u32[]{:S(2)}, u32[]{:S(2)}) collective-permute-start(bf16[128,768]{1,0:T(8,128)(2,1)} %slice.9), channel_id=1, source_target_pairs={{0,64},{64,128},{128,192},{192,256},{256,320},{320,384},{384,448},... | collective-permute-start | bytes 589832 | tf_op jit(solution)/shard_map/ppermute | solution.py:291
  45.8 0.0 collective-permute-done.right
  45.8 0.7 slice.8
  46.5 4.6 %collective-permute-start.2 = (bf16[128,768]{1,0:T(8,128)(2,1)}, bf16[128,768]{1,0:T(8,128)(2,1)}, u32[]{:S(2)}, u32[]{:S(2)}) collective-permute-start(bf16[128,768]{1,0:T(8,128)(2,1)} %slice.8), channel_id=1, source_target_pairs={{0,448},{64,0},{128,64},{192,128},{256,192},{320,256},{384,320},{4... | collective-permute-start | bytes 589832 | tf_op jit(solution)/shard_map/ppermute | solution.py:290
  51.1 5.6 %collective-permute-start.4 = (bf16[256,768]{1,0:T(8,128)(2,1)S(1)}, bf16[256,768]{1,0:T(8,128)(2,1)S(1)}, u32[]{:S(2)}, u32[]{:S(2)}) collective-permute-start(bf16[256,768]{1,0:T(8,128)(2,1)S(1)} %bitcast.17), channel_id=1, source_target_pairs={{0,1},{1,0},{2,3},{3,2},{4,5},{5,4},{6,7},{7,6},{8,9},{9,8},{10,11... | collective-permute-start | bytes 1179656 | tf_op jit(solution)/shard_map/ppermute | solution.py:293
  56.7 1.9 %collective-permute-start.6 = (bf16[256,768]{1,0:T(8,128)(2,1)S(1)}, bf16[256,768]{1,0:T(8,128)(2,1)}, u32[]{:S(2)}, u32[]{:S(2)}) collective-permute-start(bf16[256,768]{1,0:T(8,128)(2,1)S(1)} %collective-permute-done.1.left), channel_id=1, source_target_pairs={{0,1},{1,0},{2,3},{3,2},{4,5},{5,4},{6,7},{7,6},{8,9},{9,8},{10,11... | collective-permute-start | bytes 1179656 | tf_op jit(solution)/shard_map/ppermute | solution.py:293
  58.6 2.4 %collective-permute-start.5 = (bf16[256,768]{1,0:T(8,128)(2,1)S(1)}, bf16[256,768]{1,0:T(8,128)(2,1)}, u32[]{:S(2)}, u32[]{:S(2)}) collective-permute-start(bf16[256,768]{1,0:T(8,128)(2,1)S(1)} %collective-permute-done.right), channel_id=1, source_target_pairs={{0,1},{1,0},{2,3},{3,2},{4,5},{5,4},{6,7},{7,6},{8,9},{9,8},{10,11... | collective-permute-start | bytes 1179656 | tf_op jit(solution)/shard_map/ppermute | solution.py:293
  61.0 0.0 copy-done.12
  61.0 0.8 reshape.41
  61.9 0.9 copy.10
  62.8 0.1 reshape.49.slots
  62.9 0.0 collective-permute-done.3.far_b
  62.9 1.9 %collective-permute-start.8 = (bf16[128,768]{1,0:T(8,128)(2,1)S(1)}, bf16[128,768]{1,0:T(8,128)(2,1)S(1)}, u32[]{:S(2)}, u32[]{:S(2)}) collective-permute-start(bf16[128,768]{1,0:T(8,128)(2,1)S(1)} %collective-permute-done.3.far_b), channel_id=1, source_target_pairs={{0,1},{1,0},{2,3},{3,2},{4,5},{5,4},{6,7},{7,6},{8,9},{9,8},{10,11... | collective-permute-start | bytes 589832 | tf_op jit(solution)/shard_map/ppermute | solution.py:293
  64.9 0.0 collective-permute-done.2.far_a
  64.9 2.4 %collective-permute-start.7 = (bf16[128,768]{1,0:T(8,128)(2,1)}, bf16[128,768]{1,0:T(8,128)(2,1)S(1)}, u32[]{:S(2)}, u32[]{:S(2)}) collective-permute-start(bf16[128,768]{1,0:T(8,128)(2,1)} %collective-permute-done.2.far_a), channel_id=1, source_target_pairs={{0,1},{1,0},{2,3},{3,2},{4,5},{5,4},{6,7},{7,6},{8,9},{9,8},{10,11... | collective-permute-start | bytes 589832 | tf_op jit(solution)/shard_map/ppermute | solution.py:293
  67.3 0.0 copy-done.1
  67.3 0.0 copy-start.2
  67.3 1.1 copy-done.2
  68.4 0.6 squares.1
  69.0 0.0 copy-start.5
  69.0 0.8 copy-done.5
  69.8 0.1 pad_add_fusion.where
  69.9 0.0 collective-permute-done.4.own2
  69.9 0.0 collective-permute-done.8.far_b2
  69.9 0.0 collective-permute-done.6.left2
  69.9 0.0 collective-permute-done.7.far_a2
  69.9 0.0 collective-permute-done.5.right2
  69.9 0.0 copy-start.4
  69.9 5.3 %coarse_part.1 = (f32[16,128]{1,0:T(8,128)S(1)}, bf16[8,768]{1,0:T(8,128)(2,1)S(1)}) custom-call(s32[3]{0:T(128)S(1)} %pad_add_fusion.where, bf16[512,768]{1,0:T(8,128)(2,1)S(1)} %copy-done.2, f32[1,512]{1,0:T(1,128)S(1)} %get-tuple-element.14.vector_squares, s32[8,1,256]{2,1,0:T(1,128)S(1)} %reshape.49.slots, bf16[256,768]{1,0:T(8,128)(2,1)S(1)} %bitcast.18, ...), custom_call_target="tpu_custom_call" | custom-call | flops 2000000000 | bytes 4194304 | tf_op jit(solution)/shard_map/coarse_part/pallas_call | solution.py:155
  75.2 0.7 broadcast_in_dim.7
  75.9 4.3 %all-to-all-start.1 = ((f32[16,16,128]{2,1,0:T(8,128)}), f32[16,16,128]{2,1,0:T(8,128)S(1)}, u32[]{:S(2)}, u32[]{:S(2)}) async-start(f32[16,16,128]{2,1,0:T(8,128)} %broadcast_in_dim.7), calls=%async_computation.1 | async-start | bytes 262144 | tf_op jit(solution)/shard_map/all_to_all | solution.py:271
  80.2 0.1 reshape.45.table
  80.3 0.0 copy-done.4
  80.3 1.1 copy-done.3
  81.4 2.6 %route.1 = (bf16[64,16,768]{2,1,0:T(8,128)(2,1)}, f32[64,1,16]{2,1,0:T(1,128)}, s32[1,512]{1,0:T(1,128)S(1)}) custom-call(s32[1,512]{1,0:T(1,128)S(1)} %bitcast.22, s32[32,64]{1,0:T(8,128)S(1)} %reshape.45.table, bf16[512,768]{1,0:T(8,128)(2,1)S(1)} %copy-done.3), custom_call_target="tpu_custom_call" | custom-call | flops 2000000000 | bytes 4194304 | tf_op jit(solution)/shard_map/route/pallas_call | solution.py:71
  84.0 5.4 %all-to-all-done.1 = f32[16,16,128]{2,1,0:T(8,128)S(1)} async-done(((f32[16,16,128]{2,1,0:T(8,128)}), f32[16,16,128]{2,1,0:T(8,128)S(1)}, u32[]{:S(2)}, u32[]{:S(2)}) %all-to-all-start.1) | async-done | bytes 131104 | tf_op jit(solution)/shard_map/all_to_all | solution.py:271
  89.4 5.6 %all-to-all-start.4 = ((f32[64,1,16]{2,1,0:T(1,128)}), f32[64,1,16]{2,1,0:T(1,128)S(1)}, u32[]{:S(2)}, u32[]{:S(2)}) async-start(f32[64,1,16]{2,1,0:T(1,128)} %get-tuple-element.17), calls=%async_computation.4 | async-start | bytes 65536 | tf_op jit(solution)/shard_map/all_to_all | solution.py:271
  95.0 9.3 %all-to-all-done.4.meta = f32[64,1,16]{2,1,0:T(1,128)S(1)} async-done(((f32[64,1,16]{2,1,0:T(1,128)}), f32[64,1,16]{2,1,0:T(1,128)S(1)}, u32[]{:S(2)}, u32[]{:S(2)}) %all-to-all-start.4) | async-done | bytes 4128 | tf_op jit(solution)/shard_map/all_to_all | solution.py:271
  104.4 15.2 %all_to_all.31 = f32[32,16,128]{2,1,0:T(8,128)} all-to-all(f32[32,16,128]{2,1,0:T(8,128)S(1)} %broadcast_in_dim.8), channel_id=1, replica_groups=mesh['z'=8,'y'=8,'x'=4,'c'=2] {'y','x'}, dimensions={0} | all-to-all | bytes 524288 | tf_op jit(solution)/shard_map/all_to_all | solution.py:271
  119.5 6.6 %all-to-all-start.3 = ((bf16[64,16,768]{2,1,0:T(8,128)(2,1)}), bf16[64,16,768]{2,1,0:T(8,128)(2,1)S(1)}, u32[]{:S(2)}, u32[]{:S(2)}) async-start(bf16[64,16,768]{2,1,0:T(8,128)(2,1)} %get-tuple-element.16), calls=%async_computation.3 | async-start | bytes 3145728 | tf_op jit(solution)/shard_map/all_to_all | solution.py:271
  126.2 1.0 reduce_sum.19
  127.1 0.6 multiply_bitcast_fusion
  127.7 37.5 %all-to-all-done.3 = bf16[64,16,768]{2,1,0:T(8,128)(2,1)S(1)} async-done(((bf16[64,16,768]{2,1,0:T(8,128)(2,1)}), bf16[64,16,768]{2,1,0:T(8,128)(2,1)S(1)}, u32[]{:S(2)}, u32[]{:S(2)}) %all-to-all-start.3) | async-done | bytes 1572896 | tf_op jit(solution)/shard_map/all_to_all | solution.py:271
  165.3 1.0 copy-done.6
  166.3 5.3 %fine_part.1 = (f32[64,1,16]{2,1,0:T(1,128)}, bf16[1024,1024]{1,0:T(8,128)(2,1)}, bf16[1024,768]{1,0:T(8,128)(2,1)S(1)}, f32[1024,1]{1,0:T(8,128)S(1)}) custom-call(bf16[1024,768]{1,0:T(8,128)(2,1)S(1)} %bitcast.14, f32[64,1,16]{2,1,0:T(1,128)S(1)} %all-to-all-done.4.meta, bf16[8,768]{1,0:T(8,128)(2,1)S(1)} %get-tuple-element.18.mine, ...), custom_call_target="tpu_custom_call" | custom-call | flops 3000000000 | bytes 4194304 | tf_op jit(solution)/shard_map/fine_part/pallas_call | solution.py:215
  171.6 1.1 copy-done.8
  172.7 0.8 copy-done.10
  173.5 6.5 %all-to-all-start.5 = ((f32[64,1,16]{2,1,0:T(1,128)}), f32[64,1,16]{2,1,0:T(1,128)S(1)}, u32[]{:S(2)}, u32[]{:S(2)}) async-start(f32[64,1,16]{2,1,0:T(1,128)} %get-tuple-element.23), calls=%async_computation.5 | async-start | bytes 65536 | tf_op jit(solution)/shard_map/all_to_all | solution.py:271
  180.0 0.0 copy-start.7
  180.0 1.6 copy-done.7
  181.6 1.4 copy-done.9
  183.0 1.0 copy-done.11
  184.0 2.9 %update.1 = bf16[1024,768]{1,0:T(8,128)(2,1)} custom-call(bf16[1024,768]{1,0:T(8,128)(2,1)S(1)} %bitcast.21, bf16[1024,1024]{1,0:T(8,128)(2,1)S(1)} %copy-done.7, bf16[1024,768]{1,0:T(8,128)(2,1)S(1)} %copy-done.9, f32[1024,1]{1,0:T(8,128)S(1)} %copy-done.11), custom_call_target="tpu_custom_call" | custom-call | flops 3000000000 | bytes 4194304 | tf_op jit(solution)/shard_map/update/pallas_call | solution.py:239
  187.0 2.4 %all-to-all-done.5.returned = f32[64,1,16]{2,1,0:T(1,128)S(1)} async-done(((f32[64,1,16]{2,1,0:T(1,128)}), f32[64,1,16]{2,1,0:T(1,128)S(1)}, u32[]{:S(2)}, u32[]{:S(2)}) %all-to-all-start.5) | async-done | bytes 4128 | tf_op jit(solution)/shard_map/all_to_all | solution.py:271
  189.4 0.8 pick.1
  (10 shorter events, 0.1 us)
Async XLA Ops:
  0.6 0.8 copy-start
  0.6 60.4 %copy-start.12 = (s32[2048]{0:T(1024)S(1)}, s32[2048]{0:T(1024)}, u32[]{:S(2)}) copy-start(s32[2048]{0:T(1024)} %param.7) | copy-start | bytes 24580
  0.7 66.6 %copy-start.1 = (bf16[4,256,768]{2,1,0:T(8,128)(2,1)S(1)}, bf16[4,256,768]{2,1,0:T(8,128)(2,1)}, u32[]{:S(2)}) copy-start(bf16[4,256,768]{2,1,0:T(8,128)(2,1)} %param.9) | copy-start | bytes 4718596
  25.6 17.6 %collective-permute-start.1 = (bf16[256,768]{1,0:T(8,128)(2,1)S(1)}, bf16[256,768]{1,0:T(8,128)(2,1)S(1)}, u32[]{:S(2)}, u32[]{:S(2)}) collective-permute-start(bf16[256,768]{1,0:T(8,128)(2,1)S(1)} %bitcast.15), channel_id=1, source_target_pairs={{0,64},{64,128},{128,192},{192,256},{256,320},{320,384},{384,448},... | collective-permute-start | bytes 1179656 | tf_op jit(solution)/shard_map/ppermute | solution.py:288
  29.6 16.2 %collective-permute-start = (bf16[256,768]{1,0:T(8,128)(2,1)S(1)}, bf16[256,768]{1,0:T(8,128)(2,1)S(1)}, u32[]{:S(2)}, u32[]{:S(2)}) collective-permute-start(bf16[256,768]{1,0:T(8,128)(2,1)S(1)} %bitcast.16), channel_id=1, source_target_pairs={{0,448},{64,0},{128,64},{192,128},{256,192},{320,256},{384,320},{4... | collective-permute-start | bytes 1179656 | tf_op jit(solution)/shard_map/ppermute | solution.py:287
  43.9 19.1 %collective-permute-start.3 = (bf16[128,768]{1,0:T(8,128)(2,1)}, bf16[128,768]{1,0:T(8,128)(2,1)S(1)}, u32[]{:S(2)}, u32[]{:S(2)}) collective-permute-start(bf16[128,768]{1,0:T(8,128)(2,1)} %slice.9), channel_id=1, source_target_pairs={{0,64},{64,128},{128,192},{192,256},{256,320},{320,384},{384,448},... | collective-permute-start | bytes 589832 | tf_op jit(solution)/shard_map/ppermute | solution.py:291
  46.5 18.4 %collective-permute-start.2 = (bf16[128,768]{1,0:T(8,128)(2,1)}, bf16[128,768]{1,0:T(8,128)(2,1)}, u32[]{:S(2)}, u32[]{:S(2)}) collective-permute-start(bf16[128,768]{1,0:T(8,128)(2,1)} %slice.8), channel_id=1, source_target_pairs={{0,448},{64,0},{128,64},{192,128},{256,192},{320,256},{384,320},{4... | collective-permute-start | bytes 589832 | tf_op jit(solution)/shard_map/ppermute | solution.py:290
  51.1 18.8 %collective-permute-start.4 = (bf16[256,768]{1,0:T(8,128)(2,1)S(1)}, bf16[256,768]{1,0:T(8,128)(2,1)S(1)}, u32[]{:S(2)}, u32[]{:S(2)}) collective-permute-start(bf16[256,768]{1,0:T(8,128)(2,1)S(1)} %bitcast.17), channel_id=1, source_target_pairs={{0,1},{1,0},{2,3},{3,2},{4,5},{5,4},{6,7},{7,6},{8,9},{9,8},{10,11... | collective-permute-start | bytes 1179656 | tf_op jit(solution)/shard_map/ppermute | solution.py:293
  56.7 13.2 %collective-permute-start.6 = (bf16[256,768]{1,0:T(8,128)(2,1)S(1)}, bf16[256,768]{1,0:T(8,128)(2,1)}, u32[]{:S(2)}, u32[]{:S(2)}) collective-permute-start(bf16[256,768]{1,0:T(8,128)(2,1)S(1)} %collective-permute-done.1.left), channel_id=1, source_target_pairs={{0,1},{1,0},{2,3},{3,2},{4,5},{5,4},{6,7},{7,6},{8,9},{9,8},{10,11... | collective-permute-start | bytes 1179656 | tf_op jit(solution)/shard_map/ppermute | solution.py:293
  58.6 11.3 %collective-permute-start.5 = (bf16[256,768]{1,0:T(8,128)(2,1)S(1)}, bf16[256,768]{1,0:T(8,128)(2,1)}, u32[]{:S(2)}, u32[]{:S(2)}) collective-permute-start(bf16[256,768]{1,0:T(8,128)(2,1)S(1)} %collective-permute-done.right), channel_id=1, source_target_pairs={{0,1},{1,0},{2,3},{3,2},{4,5},{5,4},{6,7},{7,6},{8,9},{9,8},{10,11... | collective-permute-start | bytes 1179656 | tf_op jit(solution)/shard_map/ppermute | solution.py:293
  62.9 7.0 %collective-permute-start.8 = (bf16[128,768]{1,0:T(8,128)(2,1)S(1)}, bf16[128,768]{1,0:T(8,128)(2,1)S(1)}, u32[]{:S(2)}, u32[]{:S(2)}) collective-permute-start(bf16[128,768]{1,0:T(8,128)(2,1)S(1)} %collective-permute-done.3.far_b), channel_id=1, source_target_pairs={{0,1},{1,0},{2,3},{3,2},{4,5},{5,4},{6,7},{7,6},{8,9},{9,8},{10,11... | collective-permute-start | bytes 589832 | tf_op jit(solution)/shard_map/ppermute | solution.py:293
  64.9 5.0 %collective-permute-start.7 = (bf16[128,768]{1,0:T(8,128)(2,1)}, bf16[128,768]{1,0:T(8,128)(2,1)S(1)}, u32[]{:S(2)}, u32[]{:S(2)}) collective-permute-start(bf16[128,768]{1,0:T(8,128)(2,1)} %collective-permute-done.2.far_a), channel_id=1, source_target_pairs={{0,1},{1,0},{2,3},{3,2},{4,5},{5,4},{6,7},{7,6},{8,9},{9,8},{10,11... | collective-permute-start | bytes 589832 | tf_op jit(solution)/shard_map/ppermute | solution.py:293
  67.3 1.1 copy-start.2
  69.0 0.8 copy-start.5
  69.9 10.3 %copy-start.4 = (s32[512]{0:T(512)S(1)}, s32[512]{0:T(512)}, u32[]{:S(2)}) copy-start(s32[512]{0:T(512)} %param.6) | copy-start | bytes 6148
  75.9 13.5 %all-to-all-start.1 = ((f32[16,16,128]{2,1,0:T(8,128)}), f32[16,16,128]{2,1,0:T(8,128)S(1)}, u32[]{:S(2)}, u32[]{:S(2)}) async-start(f32[16,16,128]{2,1,0:T(8,128)} %broadcast_in_dim.7), calls=%async_computation.1 | async-start | bytes 262144 | tf_op jit(solution)/shard_map/all_to_all | solution.py:271
  80.3 1.1 copy-start.3
  89.4 15.0 %all-to-all-start.4 = ((f32[64,1,16]{2,1,0:T(1,128)}), f32[64,1,16]{2,1,0:T(1,128)S(1)}, u32[]{:S(2)}, u32[]{:S(2)}) async-start(f32[64,1,16]{2,1,0:T(1,128)} %get-tuple-element.17), calls=%async_computation.4 | async-start | bytes 65536 | tf_op jit(solution)/shard_map/all_to_all | solution.py:271
  119.5 45.7 %all-to-all-start.3 = ((bf16[64,16,768]{2,1,0:T(8,128)(2,1)}), bf16[64,16,768]{2,1,0:T(8,128)(2,1)S(1)}, u32[]{:S(2)}, u32[]{:S(2)}) async-start(bf16[64,16,768]{2,1,0:T(8,128)(2,1)} %get-tuple-element.16), calls=%async_computation.3 | async-start | bytes 3145728 | tf_op jit(solution)/shard_map/all_to_all | solution.py:271
  165.3 1.0 copy-start.6
  171.6 1.1 copy-start.8
  172.7 0.8 copy-start.10
  173.5 15.8 %all-to-all-start.5 = ((f32[64,1,16]{2,1,0:T(1,128)}), f32[64,1,16]{2,1,0:T(1,128)S(1)}, u32[]{:S(2)}, u32[]{:S(2)}) async-start(f32[64,1,16]{2,1,0:T(1,128)} %get-tuple-element.23), calls=%async_computation.5 | async-start | bytes 65536 | tf_op jit(solution)/shard_map/all_to_all | solution.py:271
  180.0 1.6 copy-start.7
  181.6 1.4 copy-start.9
  183.0 1.0 copy-start.11

commit v2 on v0

v2 whole, which is shorter than its diff:
```python
import functools

import jax
import jax.numpy as jnp
from jax import lax
from jax.experimental import pallas as pl
from jax.experimental.pallas import tpu as pltpu
from jax.sharding import Mesh, PartitionSpec as P

sharpness = 0.0625
Z, Y, X, CORES = 8, 8, 4, 2
PLANE = ("y", "x", "c")
EVERY = ("z", "y", "x", "c")
GROUPS = Y * X
SETS = 4
LOW = 64
f32, bf16, i32 = jnp.float32, jnp.bfloat16, jnp.int32
VMEM = pl.BlockSpec(memory_space=pltpu.VMEM)
SMEM = pl.BlockSpec(memory_space=pltpu.SMEM)


def call(body, out_shape, scalars, arrays, name, flops, mib=16, scratch=()):
    return pl.pallas_call(
        body,
        out_shape=out_shape,
        in_specs=[SMEM] * len(scalars) + [VMEM] * len(arrays),
        out_specs=jax.tree.map(lambda _: VMEM, out_shape),
        scratch_shapes=scratch,
        name=name,
        compiler_params=pltpu.CompilerParams(vmem_limit_bytes=mib * 2**20),
        cost_estimate=pl.CostEstimate(flops=flops, bytes_accessed=2**20, transcendentals=0),
    )(*scalars, *arrays)


def shaped(shape, dtype):
    return jax.ShapeDtypeStruct(shape, dtype)


def iota(shape, axis):
    return lax.broadcasted_iota(i32, shape, axis)


def dot(a, b, ca, cb, precision=None):
    return lax.dot_general(
        a, b, (((ca,), (cb,)), ((), ())), preferred_element_type=f32, precision=precision
    )


def as_row(column):
    return jnp.transpose(jnp.broadcast_to(column, (column.shape[0], 128)))[0:1, :]


def row_squares(points):
    wide = points.astype(f32)
    return jnp.sum(wide * wide, axis=1, keepdims=True)


def pack_kernel(where, coarse, cell, out):
    rows, features = coarse.shape
    wide = coarse[...].astype(f32).reshape(SETS, rows // SETS, features)
    part = jnp.sum(jnp.where(iota(wide.shape, 0) == where[1], wide, 0.0), axis=0)
    ids = jnp.concatenate([cell[...] // LOW, cell[...] % LOW], axis=0).astype(f32)
    out[...] = jnp.broadcast_to(jnp.concatenate([part, ids], axis=1).astype(bf16)[None], out.shape)


def split_kernel(got, own, own_a, own_b, ids):
    features = own.shape[1]
    whole = got[...].astype(f32)
    rows = whole[:, :, :features].reshape(own.shape).astype(bf16)
    half = own.shape[0] // 2
    own[...] = rows
    own_a[...] = rows[:half]
    own_b[...] = rows[half:]
    ids[...] = whole[:, :, features:]


def prepare_kernel(owned, where, cell, table, vectors, vectors2, book, send, place, book_squares, vector_squares, wanted):
    owners, cap, _ = send.shape
    rows = vectors.shape[0]
    high, low = table.shape
    cell_of = cell[...]
    slots = table[...]
    in_high = (iota((high, rows), 0) == cell_of // low).astype(bf16)
    in_low = iota((low, rows), 0) == cell_of % low
    owner_table = ((slots // owned) % owners).astype(bf16)
    owner = jnp.sum(jnp.where(in_low, dot(owner_table, in_high, 0, 0), 0.0), axis=0, keepdims=True).astype(i32)
    at_owner = iota((owners, rows), 0) == owner
    before = (iota((rows, rows), 0) < iota((rows, rows), 1)).astype(bf16)
    earlier = dot(at_owner.astype(bf16), before, 1, 0)
    rank = jnp.sum(jnp.where(at_owner, earlier, 0.0), axis=0, keepdims=True).astype(i32)
    position = owner * cap + rank
    place[...] = position
    block = 256
    for b in range(owners * cap // block):
        pick = (iota((block, rows), 0) + b * block == position).astype(bf16)
        moved = dot(pick, vectors[...], 1, 0).astype(bf16)
        send[b * block // cap : (b + 1) * block // cap] = moved.reshape(block // cap, cap, -1)
    for b in range(book.shape[0] // block):
        at = slice(b * block, (b + 1) * block)
        book_squares[:, at] = as_row(row_squares(book[at]))
    for side, points in enumerate((vectors, vectors2)):
        for b in range(rows // block):
            at = slice(b * block, (b + 1) * block)
            vector_squares[:, side * rows + b * block : side * rows + (b + 1) * block] = as_row(row_squares(points[at]))
    base = where[0]
    cell_index = (iota((high, low), 0) * low + iota((high, low), 1)).astype(f32)
    line = iota((16, 128), 0)
    ids = jnp.full((16, 128), -1.0, f32)
    for first, start in ((0, base), (8, base ^ owned)):
        for s in range(owned):
            hit = jnp.where(slots == start + s, cell_index, 0.0)
            cell_id = jnp.sum(jnp.sum(hit, axis=1, keepdims=True), axis=0, keepdims=True)
            ids = jnp.where(line == first + s, cell_id, ids)
    wanted[...] = ids


def locals_kernel(where, ids, ids2, wanted, local):
    core = where[2]
    places = local.shape[1]
    rows = SETS * 128
    cap = places // (GROUPS * CORES)
    cells = [wanted[s : s + 1, 0:1] for s in range(SETS)]
    before = (iota((rows, rows), 0) < iota((rows, rows), 1)).astype(bf16)
    spread = (iota((cap, places), 1) % cap == iota((cap, places), 0)).astype(bf16)
    at_group = iota((GROUPS, places), 1) // (CORES * cap) == iota((GROUPS, places), 0)
    of_core = (iota((GROUPS, places), 1) // cap) % CORES
    total = jnp.zeros((1, places), f32)
    for source, side in ((ids, core), (ids2, 1 - core)):
        digits = source[...]
        codes = jnp.concatenate([digits[:, j, :] * LOW + digits[:, SETS + j, :] for j in range(SETS)], axis=1)
        found = jnp.zeros(codes.shape, f32)
        for s in range(SETS):
            found = found + jnp.where(codes == cells[s], s + 1.0, 0.0)
        earlier = dot((found > 0.0).astype(bf16), before, 1, 0)
        ranked = jnp.concatenate(
            [jnp.sum(jnp.where(earlier == float(r), found, 0.0), axis=1, keepdims=True) for r in range(cap)], axis=1
        )
        across = dot(ranked.astype(bf16), spread, 1, 0)
        total = total + jnp.sum(jnp.where(at_group & (of_core == side), across, 0.0), axis=0, keepdims=True)
    local[...] = total - 1.0


def coarse_kernel(
    where, vectors, vectors2, vector_squares, wanted, own, right, left, far_a, far_b, early, weights, told, mine, scores
):
    quarter, core = where[1], where[2]
    rows, features = vectors.shape
    cells = wanted[:, 0:1].astype(i32)
    picked = jnp.zeros((16, features), f32)
    tops = [jnp.full((1, rows), -jnp.inf, f32)] * CORES
    half = GROUPS // 2
    for chunk, step, start in zip((own, right, left, far_a, far_b), (0, 1, 3, 2, 2), (0, 0, 0, 0, half), strict=True):
        count = chunk.shape[0] // 8
        at = (quarter + step) % SETS
        points = chunk[...]
        squares = row_squares(points)
        for side, against in enumerate((vectors, vectors2)):
            across = slice(side * rows, (side + 1) * rows)
            distance = vector_squares[:, across] + squares - 2.0 * dot(points, against[...], 1, 1)
            score = -sharpness * distance
            tops[side] = jnp.maximum(tops[side], jnp.max(score, axis=0, keepdims=True))
            scores[start : start + count, at, :, across] = score.reshape(count, 8, rows)
        line = iota((16, count * 8), 1) + start * 8
        inside = (line // 8 * CORES + core) * (SETS * 8) + at * 8 + line % 8 == cells
        picked = picked + dot(inside.astype(bf16), points, 1, 0)
    mine[...] = picked[0:8]
    totals = []
    for side in range(CORES):
        across = slice(side * rows, (side + 1) * rows)
        total = jnp.zeros((1, rows), f32)
        for b in range(GROUPS // 4):
            e = jnp.exp(scores[4 * b : 4 * b + 4, :, :, across].reshape(128, rows) - tops[side])
            total = total + jnp.sum(e, axis=0, keepdims=True)
            weights[4 * b : 4 * b + 4, :, :, across] = e.reshape(4, SETS, 8, rows)
        totals.append(total)
    told[0:8, :] = jnp.broadcast_to(jnp.concatenate(tops, axis=1), (8, CORES * rows))
    told[8:16, :] = jnp.broadcast_to(jnp.concatenate(totals, axis=1), (8, CORES * rows))
    told[16:24, 0:features] = picked[8:16]
    told[16:24, features:] = jnp.zeros((8, CORES * rows - features), f32)


def share_kernel(weights, told, heard, share):
    rows = told.shape[1] // CORES

    def swapped(line):
        return jnp.concatenate([line[:, rows:], line[:, :rows]], axis=1)

    top, total = told[0:1, :], told[8:9, :]
    top2, total2 = swapped(heard[0:1, :]), swapped(heard[8:9, :])
    highest = jnp.maximum(top, top2)
    here = jnp.exp(top - highest)
    factor = here / (total * here + total2 * jnp.exp(top2 - highest))
    for b in range(GROUPS // 4):
        probs = weights[4 * b : 4 * b + 4].reshape(128, CORES * rows) * factor
        lanes = probs[:, 0:128]
        for j in range(1, CORES * rows // 128):
            lanes = lanes + probs[:, j * 128 : (j + 1) * 128]
        share[b : b + 1, :] = jnp.sum(jnp.transpose(lanes), axis=0, keepdims=True)


def fine_kernel(got, local, mine, heard, book, book_squares, spread, out, weights, residual, mass):
    owners, cap = spread.shape
    rows, features = got.shape
    fine = book.shape[0] // SETS
    centres = (mine[...] + heard[16:24, 0:features]).astype(bf16)
    squares = [
        jnp.transpose(jnp.broadcast_to(book_squares[:, s * fine : (s + 1) * fine], (128, fine)))[:, 0:1] for s in range(SETS)
    ]
    block = 256
    parts = []
    for b in range(rows // block):
        at = slice(b * block, (b + 1) * block)
        slot = local[:, at]
        inside = [slot == s for s in range(SETS)]
        chosen = (iota((8, block), 0).astype(f32) == slot).astype(bf16)
        moved = (got[at].astype(f32) - dot(chosen, centres, 0, 0)).astype(bf16)
        residual[at] = moved
        moved_squares = as_row(row_squares(moved))
        distance = jnp.zeros((fine, block), f32)
        for s in range(SETS):
            here = moved_squares + squares[s] - 2.0 * dot(book[s * fine : (s + 1) * fine], moved, 1, 1)
            distance = jnp.where(inside[s], here, distance)
        score = -sharpness * distance
        e = jnp.exp(score - jnp.max(score, axis=0, keepdims=True))
        weight = e * ((slot >= 0.0).astype(f32) / jnp.sum(e, axis=0, keepdims=True))
        parts.append(jnp.sum(weight * distance, axis=0, keepdims=True) / features)
        for s in range(SETS):
            of = slice(s * fine, (s + 1) * fine)
            only = jnp.where(inside[s], weight, 0.0)
            weights[of, at] = only.astype(bf16)
            part = jnp.sum(only, axis=1, keepdims=True)
            mass[of] = part if b == 0 else mass[of] + part
    row = jnp.concatenate(parts, axis=1)
    places = (iota((cap, rows), 1) % cap == iota((cap, rows), 0)).astype(f32)
    at_owner = iota((owners, rows), 1) // cap == iota((owners, rows), 0)
    spread[...] = dot(jnp.where(at_owner, row, 0.0), places, 1, 1, lax.Precision.HIGHEST)
    for s in range(SETS):
        of = slice(s * fine, (s + 1) * fine)
        total = dot(weights[of], residual[...], 1, 0)
        out[of] = ((book[of].astype(f32) + total) * (1.0 / (1.0 + mass[of]))).astype(bf16)


def answer_kernel(where, spread, shares, out):
    owners, cap = spread.shape
    total = jnp.sum(shares[...], axis=0).reshape(X, 2, 128)
    quarter = jnp.sum(jnp.where(iota(total.shape, 0) == where[3], total, 0.0), axis=0)
    line = jnp.concatenate([spread[...], jnp.zeros((owners, 128 - cap), f32)], axis=1)
    out[:, 0:2, :] = jnp.broadcast_to(quarter[None], (owners, 2, 128))
    out[:, 2:4, :] = jnp.broadcast_to(line[:, None, :], (owners, 2, 128))


def finish_kernel(scale, got, place, distortion, share):
    owners = got.shape[0]
    rows = place.shape[1]
    cap = 2 * rows // owners
    position = place[...]
    at_owner = (iota((owners, rows), 0) == position // cap).astype(f32)
    at_rank = iota((cap, rows), 0) == position % cap
    whole = got[...]
    returned = whole[:, 2, :][:, 0:cap]
    across = dot(returned, at_owner, 0, 0, lax.Precision.HIGHEST)
    distortion[...] = jnp.sum(jnp.where(at_rank, across, 0.0), axis=0, keepdims=True)
    quarters = jnp.sum(whole[:, 0:2, :].reshape(Y, X * CORES, 2, 128), axis=0) * scale
    halves = [jnp.concatenate([quarters[x * CORES + c] for x in range(X)], axis=0) for c in range(CORES)]
    for u in range(2):
        pieces = [
            halves[c][:, u * 64 + v * 32 : u * 64 + (v + 1) * 32] for v in range(2) for c in range(CORES)
        ]
        share[:, u, :] = jnp.concatenate(pieces, axis=1)


def exchange(x, axes):
    return lax.all_to_all(x, axes, 0, 0, tiled=True)


def from_next(x, steps):
    return lax.ppermute(x, "z", [((i + steps) % Z, i) for i in range(Z)])


def from_partner(x):
    return lax.ppermute(x, "c", [(0, 1), (1, 0)])


def on_device(vectors, cell_of, cell_slot, coarse, fine_book):
    rows, features = vectors.shape
    owned, fine, _ = fine_book.shape
    owners = GROUPS * CORES
    cap = 2 * rows // owners
    cells = cell_slot.shape[0]
    part = coarse.shape[0] // SETS
    chunk = GROUPS * part
    z, x, c = (lax.axis_index(axis) for axis in ("z", "x", "c"))
    base = lax.axis_index(EVERY) * owned
    where = jnp.stack([base, z % SETS, c, x]).astype(i32)
    book = fine_book.reshape(owned * fine, features)

    packed = call(
        pack_kernel, shaped((GROUPS, part, features + 128), bf16), [where], [coarse, cell_of.reshape(-1, 128)], "pack", 10**6
    )
    first = exchange(packed, ("y", "x"))
    vectors2 = from_partner(vectors)
    send, place, book_squares, vector_squares, wanted = call(
        functools.partial(prepare_kernel, owned),
        (
            shaped((owners, cap, features), bf16),
            shaped((1, rows), i32),
            shaped((1, owned * fine), f32),
            shaped((1, CORES * rows), f32),
            shaped((16, 128), f32),
        ),
        [where],
        [cell_of.reshape(1, rows), cell_slot.reshape(-1, LOW), vectors, vectors2, book],
        "prepare",
        10**9,
    )
    got = exchange(send, PLANE).reshape(owners * cap, features)

    own, own_a, own_b, ids = call(
        split_kernel,
        (
            shaped((chunk, features), bf16),
            shaped((chunk // 2, features), bf16),
            shaped((chunk // 2, features), bf16),
            shaped((GROUPS, part, 128), f32),
        ),
        [],
        [first],
        "split",
        10**6,
    )
    right, left = from_next(own, 1), from_next(own, -1)
    far_a, far_b = from_next(own_a, 2), from_next(own_b, -2)
    ids2 = from_partner(ids)
    local = call(locals_kernel, shaped((1, owners * cap), f32), [where], [ids, ids2, wanted], "locals", 10**9)
    weights, told, mine = call(
        coarse_kernel,
        (
            shaped((GROUPS, SETS, part, CORES * rows), f32),
            shaped((24, CORES * rows), f32),
            shaped((8, features), f32),
        ),
        [where],
        [vectors, vectors2, vector_squares, wanted, own, right, left, far_a, far_b, local],
        "coarse_part",
        2 * 10**9,
        mib=28,
        scratch=[pltpu.VMEM((GROUPS, SETS, part, CORES * rows), f32)],
    )
    heard = from_partner(told)
    share = call(share_kernel, shaped((8, 128), f32), [], [weights, told, heard], "share", 10**9)
    shares = exchange(jnp.broadcast_to(share[None], (Z * X, 8, 128)), ("z", "x"))

    spread, fine_next = call(
        fine_kernel,
        (shaped((owners, cap), f32), shaped(book.shape, bf16)),
        [],
        [got, local, mine, heard, book, book_squares],
        "fine_part",
        6 * 10**9,
        mib=24,
        scratch=[
            pltpu.VMEM((owned * fine, owners * cap), bf16),
            pltpu.VMEM((owners * cap, features), bf16),
            pltpu.VMEM((owned * fine, 1), f32),
        ],
    )
    answer = call(answer_kernel, shaped((owners, 4, 128), f32), [where], [spread, shares], "answer", 10**6)
    back = exchange(answer, PLANE)
    distortion, coarse_share = call(
        functools.partial(finish_kernel, owned / rows),
        (shaped((1, rows), f32), shaped((8, 2, 128), f32)),
        [],
        [back, place],
        "finish",
        10**8,
    )
    return (coarse_share.reshape(cells), fine_next.reshape(fine_book.shape), distortion.reshape(rows))


def solution(mesh):
    grid = Mesh(mesh.devices.reshape(Z, Y, X, CORES), EVERY)
    return jax.shard_map(
        on_device,
        mesh=grid,
        in_specs=(P(EVERY, None), P(EVERY), P(), P(PLANE, None), P(EVERY, None, None)),
        out_specs=(P(), P(EVERY, None, None), P(EVERY)),
        check_vma=False,
    )
```

time: 284 us -> 118 us (0.42)
  blocking collectives: 117 us -> 17.7 us
  waiting for transfers between devices: 76.5 us -> 14.1 us
  starting transfers between devices: 27.2 us -> 59.1 us
  other arithmetic: 23.8 us -> 0.08 us
  Pallas kernels: 0 us -> 16.8 us
  between operations: 14.2 us -> 0.82 us
  matrix products: 13 us -> 0 us
    psum x1 -> x0, blocking collectives: 117 us -> none  [on_device(): lax.psum(share_local, ('dp', 'cells')) * (cells_here / row_count)]
    all_gather x1 -> x0, waiting for transfers between devices: 72.6 us -> none  [on_device(): centres = lax.all_gather(coarse, 'cells', axis=0, tiled=True)]
    ppermute x0 -> x7, starting transfers between devices: none -> 29.1 us  [the longest x4 18.8 us: from_next(): return lax.ppermute(x, 'z', [((i + steps) % Z, i) for i in range(Z)])]
    all_to_all x0 -> x1, blocking collectives: none -> 17.7 us  [exchange(): return lax.all_to_all(x, axes, 0, 0, tiled=True)]
    pallas_call x0 -> x9, Pallas kernels: none -> 16.8 us  [call(): pl.pallas_call(body, out_shape=out_shape, in_specs=[SMEM] * len(scalars)...]
    dot_general x3 -> x0, matrix products: 13 us -> none  [the longest x2 6.76 us: distance_block(): lax.dot_general(points, centres, (((1,), (1,)), ((), ())), preferred_elem...]
    reduce_sum x9 -> x0, other arithmetic: 12 us -> none  [the longest x1 2.77 us: fine_owner(): jnp.sum(jnp.where(inside, weights * distance, 0.0), axis=1) / feature_count]
    ppermute x0 -> x7, waiting for transfers between devices: none -> 9.63 us  [the longest x4 7.38 us: from_next(): return lax.ppermute(x, 'z', [((i + steps) % Z, i) for i in range(Z)])]
  transfers between devices with their start and end apart: 4 -> 10, of which waited for: 2 -> 6; matrix products, arithmetic and copies ran while one was open for 11% -> 1% of each run, Pallas kernels for 0% -> 12%
where the time goes in v2:
time: 118 us; the launch traced here: 117 us
  starting transfers between devices  59.1 us (50%)
  blocking collectives  17.7 us (15%)
  Pallas kernels  16.8 us (14%)
  waiting for transfers between devices  14.1 us (12%)
  local copies, waits for them, and re-layouts  8.67 us (7%)
    all_to_all x3, starting transfers between devices, exchange(): return lax.all_to_all(x, axes, 0, 0, tiled=True)  30 us
    ppermute x4, starting transfers between devices, from_next(): return lax.ppermute(x, 'z', [((i + steps) % Z, i) for i in range(Z)])  18.8 us
    all_to_all x1, blocking collectives, exchange(): return lax.all_to_all(x, axes, 0, 0, tiled=True)  17.7 us
    pallas_call x9, Pallas kernels, call(): pl.pallas_call(body, out_shape=out_shape, in_specs=[SMEM] * len(scalars)...  16.8 us
    ppermute x3, starting transfers between devices, from_partner(): return lax.ppermute(x, 'c', [(0, 1), (1, 0)])  10.4 us
    ppermute x4, waiting for transfers between devices, from_next(): return lax.ppermute(x, 'z', [((i + steps) % Z, i) for i in range(Z)])  7.38 us
    unnamed x16, local copies, waits for them, and re-layouts  7.25 us
    all_to_all x3, waiting for transfers between devices, exchange(): return lax.all_to_all(x, axes, 0, 0, tiled=True)  4.5 us
  transfers between devices with their start and end apart: 10, of which 6 were waited for; matrix products, arithmetic and copies ran while one was open for 1% of the time, Pallas kernels for 12%

profile of v2, /device:TPU:1, one launch (start us, length us, event | category | flops | bytes accessed | tf_op | source)
XLA Modules:
  0.0 117.2 jit_solution(2942941183042716706)
XLA Ops:
  0.6 0.1 pad_add_fusion.where
  0.7 0.0 copy-start.1
  0.7 0.8 copy-done.1
  1.5 0.0 copy-start.2
  1.5 0.7 copy-done.2
  2.2 1.4 %pack.1 = bf16[32,8,896]{2,1,0:T(8,128)(2,1)} custom-call(s32[4]{0:T(128)S(1)} %pad_add_fusion.where, bf16[32,768]{1,0:T(8,128)(2,1)S(1)} %copy-done.1, s32[4,128]{1,0:T(4,128)S(1)} %bitcast.12), custom_call_target="tpu_custom_call" | custom-call | flops 1000000 | bytes 1048576 | tf_op jit(solution)/shard_map/pack/pallas_call | solution.py:23
  3.6 10.5 %all-to-all-start.1 = ((bf16[32,8,896]{2,1,0:T(8,128)(2,1)}), bf16[32,8,896]{2,1,0:T(8,128)(2,1)S(1)}, u32[]{:S(2)}, u32[]{:S(2)}) async-start(bf16[32,8,896]{2,1,0:T(8,128)(2,1)} %pack.1), calls=%async_computation.1 | async-start | bytes 917504 | tf_op jit(solution)/shard_map/all_to_all | solution.py:273
  14.1 2.9 %collective-permute-start = (bf16[512,768]{1,0:T(8,128)(2,1)}, bf16[512,768]{1,0:T(8,128)(2,1)S(1)}, u32[]{:S(2)}, u32[]{:S(2)}) collective-permute-start(bf16[512,768]{1,0:T(8,128)(2,1)} %vectors.3), channel_id=1, source_target_pairs={{0,1},{1,0},{2,3},{3,2},{4,5},{5,4},{6,7},{7,6},{8,9},{9,8},{10,11... | collective-permute-start | bytes 2359304 | tf_op jit(solution)/shard_map/ppermute | solution.py:281
  16.9 0.8 reshape.32.table
  17.7 1.3 %collective-permute-done.vectors2 = bf16[512,768]{1,0:T(8,128)(2,1)S(1)} collective-permute-done((bf16[512,768]{1,0:T(8,128)(2,1)}, bf16[512,768]{1,0:T(8,128)(2,1)S(1)}, u32[]{:S(2)}, u32[]{:S(2)}) %collective-permute-start) | collective-permute-done | bytes 786464 | tf_op jit(solution)/shard_map/ppermute | solution.py:281
  19.0 0.0 copy-start.3
  19.0 0.7 copy-done.3
  19.7 0.0 copy-start.4
  19.7 1.4 %copy-done.4 = bf16[4,256,768]{2,1,0:T(8,128)(2,1)S(1)} copy-done((bf16[4,256,768]{2,1,0:T(8,128)(2,1)S(1)}, bf16[4,256,768]{2,1,0:T(8,128)(2,1)}, u32[]{:S(2)}) %copy-start.4) | copy-done | bytes 1572888
  21.1 0.0 copy-start.6
  21.1 1.1 copy-done.6
  22.3 2.2 %prepare.1 = (bf16[64,16,768]{2,1,0:T(8,128)(2,1)S(1)}, s32[1,512]{1,0:T(1,128)S(1)}, f32[1,1024]{1,0:T(1,128)S(1)}, f32[1,1024]{1,0:T(1,128)S(1)}, f32[16,128]{1,0:T(8,128)S(1)}) custom-call(s32[4]{0:T(128)S(1)} %pad_add_fusion.where, s32[1,512]{1,0:T(1,128)S(1)} %bitcast.13, s32[32,64]{1,0:T(8,128)S(1)} %reshape.32.table, bf16[512,768]{1,0:T(8,128)(2,1)S(1)} %copy-done.6, ...), custom_call_target="tpu_custom_call" | custom-call | flops 1000000000 | bytes 1048576 | tf_op jit(solution)/shard_map/prepare/pallas_call | solution.py:23
  24.5 0.0 copy-start
  24.5 1.1 copy-done
  25.6 2.9 %all-to-all-done.1.got = bf16[32,8,896]{2,1,0:T(8,128)(2,1)S(1)} async-done(((bf16[32,8,896]{2,1,0:T(8,128)(2,1)}), bf16[32,8,896]{2,1,0:T(8,128)(2,1)S(1)}, u32[]{:S(2)}, u32[]{:S(2)}) %all-to-all-start.1) | async-done | bytes 458784 | tf_op jit(solution)/shard_map/all_to_all | solution.py:273
  28.5 7.7 %all-to-all-start = ((bf16[64,16,768]{2,1,0:T(8,128)(2,1)}), bf16[64,16,768]{2,1,0:T(8,128)(2,1)S(1)}, u32[]{:S(2)}, u32[]{:S(2)}) async-start(bf16[64,16,768]{2,1,0:T(8,128)(2,1)} %copy-done), calls=%async_computation | async-start | bytes 3145728 | tf_op jit(solution)/shard_map/all_to_all | solution.py:273
  36.2 0.1 split.1
  36.3 4.0 %collective-permute-start.3 = (bf16[256,768]{1,0:T(8,128)(2,1)S(1)}, bf16[256,768]{1,0:T(8,128)(2,1)S(1)}, u32[]{:S(2)}, u32[]{:S(2)}) collective-permute-start(bf16[256,768]{1,0:T(8,128)(2,1)S(1)} %get-tuple-element.23.own), channel_id=1, source_target_pairs={{448,0},{0,64},{64,128},{128,192},{192,256},{256,320},{320,384},{3... | collective-permute-start | bytes 1179656 | tf_op jit(solution)/shard_map/ppermute | solution.py:277
  40.3 8.6 %collective-permute-start.2 = (bf16[256,768]{1,0:T(8,128)(2,1)S(1)}, bf16[256,768]{1,0:T(8,128)(2,1)S(1)}, u32[]{:S(2)}, u32[]{:S(2)}) collective-permute-start(bf16[256,768]{1,0:T(8,128)(2,1)S(1)} %get-tuple-element.23.own), channel_id=1, source_target_pairs={{64,0},{128,64},{192,128},{256,192},{320,256},{384,320},{448,384},... | collective-permute-start | bytes 1179656 | tf_op jit(solution)/shard_map/ppermute | solution.py:277
  48.9 2.6 %collective-permute-start.1 = (f32[32,8,128]{2,1,0:T(8,128)S(1)}, f32[32,8,128]{2,1,0:T(8,128)S(1)}, u32[]{:S(2)}, u32[]{:S(2)}) collective-permute-start(f32[32,8,128]{2,1,0:T(8,128)S(1)} %get-tuple-element.20.ids), channel_id=1, source_target_pairs={{0,1},{1,0},{2,3},{3,2},{4,5},{5,4},{6,7},{7,6},{8,9},{9,8},{10,11... | collective-permute-start | bytes 393224 | tf_op jit(solution)/shard_map/ppermute | solution.py:281
  51.5 3.6 %collective-permute-start.4 = (bf16[128,768]{1,0:T(8,128)(2,1)S(1)}, bf16[128,768]{1,0:T(8,128)(2,1)S(1)}, u32[]{:S(2)}, u32[]{:S(2)}) collective-permute-start(bf16[128,768]{1,0:T(8,128)(2,1)S(1)} %get-tuple-element.24), channel_id=1, source_target_pairs={{128,0},{192,64},{256,128},{320,192},{384,256},{448,320},{0,384},{... | collective-permute-start | bytes 589832 | tf_op jit(solution)/shard_map/ppermute | solution.py:277
  55.2 2.5 %collective-permute-start.5 = (bf16[128,768]{1,0:T(8,128)(2,1)S(1)}, bf16[128,768]{1,0:T(8,128)(2,1)S(1)}, u32[]{:S(2)}, u32[]{:S(2)}) collective-permute-start(bf16[128,768]{1,0:T(8,128)(2,1)S(1)} %get-tuple-element.25), channel_id=1, source_target_pairs={{384,0},{448,64},{0,128},{64,192},{128,256},{192,320},{256,384},{3... | collective-permute-start | bytes 589832 | tf_op jit(solution)/shard_map/ppermute | solution.py:277
  57.7 0.0 collective-permute-done.1.ids2
  57.7 0.0 copy-start.7
  57.7 1.4 %locals.1.early.local = f32[1,1024]{1,0:T(1,128)S(1)} custom-call(s32[4]{0:T(128)S(1)} %pad_add_fusion.where, f32[32,8,128]{2,1,0:T(8,128)S(1)} %get-tuple-element.20.ids, f32[32,8,128]{2,1,0:T(8,128)S(1)} %collective-permute-done.1.ids2, f32[16,128]{1,0:T(8,128)S(1)} %get-tuple-element.21.wanted), custom_call_target="tpu_custom_call" | custom-call | flops 1000000000 | bytes 1048576 | tf_op jit(solution)/shard_map/locals/pallas_call | solution.py:23
  59.2 6.1 %collective-permute-done.4.far_a = bf16[128,768]{1,0:T(8,128)(2,1)S(1)} collective-permute-done((bf16[128,768]{1,0:T(8,128)(2,1)S(1)}, bf16[128,768]{1,0:T(8,128)(2,1)S(1)}, u32[]{:S(2)}, u32[]{:S(2)}) %collective-permute-start.4) | collective-permute-done | bytes 196640 | tf_op jit(solution)/shard_map/ppermute | solution.py:277
  65.3 1.2 %collective-permute-done.5.far_b = bf16[128,768]{1,0:T(8,128)(2,1)S(1)} collective-permute-done((bf16[128,768]{1,0:T(8,128)(2,1)S(1)}, bf16[128,768]{1,0:T(8,128)(2,1)S(1)}, u32[]{:S(2)}, u32[]{:S(2)}) %collective-permute-start.5) | collective-permute-done | bytes 196640 | tf_op jit(solution)/shard_map/ppermute | solution.py:277
  66.6 0.0 collective-permute-done.3.left
  66.6 0.0 collective-permute-done.2.right
  66.6 0.0 copy-done.7
  66.6 3.8 %coarse_part.1 = (f32[32,4,8,1024]{3,2,1,0:T(8,128)S(1)}, f32[24,1024]{1,0:T(8,128)S(1)}, f32[8,768]{1,0:T(8,128)S(1)}) custom-call(s32[4]{0:T(128)S(1)} %pad_add_fusion.where, bf16[512,768]{1,0:T(8,128)(2,1)S(1)} %copy-done.7, bf16[512,768]{1,0:T(8,128)(2,1)S(1)} %collective-permute-done.vectors2, f32[1,1024]{1,0:T(1,128)S(1)} %get-tuple-element.22.vector_squares, ...), custom_call_target="tpu_custom_call" | custom-call | flops 2000000000 | bytes 1048576 | tf_op jit(solution)/shard_map/coarse_part/pallas_call | solution.py:23
  70.4 4.8 %collective-permute-start.6 = (f32[24,1024]{1,0:T(8,128)S(1)}, f32[24,1024]{1,0:T(8,128)S(1)}, u32[]{:S(2)}, u32[]{:S(2)}) collective-permute-start(f32[24,1024]{1,0:T(8,128)S(1)} %get-tuple-element.27.told), channel_id=1, source_target_pairs={{0,1},{1,0},{2,3},{3,2},{4,5},{5,4},{6,7},{7,6},{8,9},{9,8},{10,11... | collective-permute-start | bytes 294920 | tf_op jit(solution)/shard_map/ppermute | solution.py:281
  75.2 0.9 collective-permute-done.6.heard
  76.1 0.4 share.1
  76.5 0.0 all-to-all-done
  76.5 0.6 broadcast_in_dim.2
  77.2 11.8 %all-to-all-start.2 = ((f32[32,8,128]{2,1,0:T(8,128)}), f32[32,8,128]{2,1,0:T(8,128)S(1)}, u32[]{:S(2)}, u32[]{:S(2)}) async-start(f32[32,8,128]{2,1,0:T(8,128)} %broadcast_in_dim.2), calls=%async_computation.2 | async-start | bytes 262144 | tf_op jit(solution)/shard_map/all_to_all | solution.py:273
  88.9 0.0 copy-start.5
  88.9 1.4 %copy-done.5 = bf16[4,256,768]{2,1,0:T(8,128)(2,1)S(1)} copy-done((bf16[4,256,768]{2,1,0:T(8,128)(2,1)S(1)}, bf16[4,256,768]{2,1,0:T(8,128)(2,1)}, u32[]{:S(2)}) %copy-start.5) | copy-done | bytes 1572888
  90.3 6.1 %fine_part.1 = (f32[64,16]{1,0:T(8,128)S(1)}, bf16[1024,768]{1,0:T(8,128)(2,1)}) custom-call(bf16[1024,768]{1,0:T(8,128)(2,1)S(1)} %bitcast.11, f32[1,1024]{1,0:T(1,128)S(1)} %locals.1.early.local, f32[8,768]{1,0:T(8,128)S(1)} %get-tuple-element.26.mine, f32[24,1024]{1,0:T(8,128)S(1)} %collective-permute-done.6.heard, bf16[1024,768]{1,0:T(8,128)(2,1)S(1)} %bitcast.15, ...), custom_call_target="tpu_custom_call" | custom-call | flops 6000000000 | bytes 1048576 | tf_op jit(solution)/shard_map/fine_part/pallas_call | solution.py:23
  96.5 1.6 %all-to-all-done.2.shares = f32[32,8,128]{2,1,0:T(8,128)S(1)} async-done(((f32[32,8,128]{2,1,0:T(8,128)}), f32[32,8,128]{2,1,0:T(8,128)S(1)}, u32[]{:S(2)}, u32[]{:S(2)}) %all-to-all-start.2) | async-done | bytes 131104 | tf_op jit(solution)/shard_map/all_to_all | solution.py:273
  98.1 0.6 answer.1
  98.7 17.7 %all_to_all.20.got = f32[64,4,128]{2,1,0:T(4,128)S(1)} all-to-all(f32[64,4,128]{2,1,0:T(4,128)S(1)} %answer.1), channel_id=1, replica_groups=mesh['z'=8,'y'=8,'x'=4,'c'=2] {'y','x','c'}, dimensions={0} | all-to-all | bytes 262144 | tf_op jit(solution)/shard_map/all_to_all | solution.py:273
  116.4 0.8 finish.1
Async XLA Ops:
  0.7 0.8 copy-start.1
  1.5 0.7 copy-start.2
  3.6 24.9 %all-to-all-start.1 = ((bf16[32,8,896]{2,1,0:T(8,128)(2,1)}), bf16[32,8,896]{2,1,0:T(8,128)(2,1)S(1)}, u32[]{:S(2)}, u32[]{:S(2)}) async-start(bf16[32,8,896]{2,1,0:T(8,128)(2,1)} %pack.1), calls=%async_computation.1 | async-start | bytes 917504 | tf_op jit(solution)/shard_map/all_to_all | solution.py:273
  14.1 5.0 %collective-permute-start = (bf16[512,768]{1,0:T(8,128)(2,1)}, bf16[512,768]{1,0:T(8,128)(2,1)S(1)}, u32[]{:S(2)}, u32[]{:S(2)}) collective-permute-start(bf16[512,768]{1,0:T(8,128)(2,1)} %vectors.3), channel_id=1, source_target_pairs={{0,1},{1,0},{2,3},{3,2},{4,5},{5,4},{6,7},{7,6},{8,9},{9,8},{10,11... | collective-permute-start | bytes 2359304 | tf_op jit(solution)/shard_map/ppermute | solution.py:281
  19.0 0.7 copy-start.3
  19.7 1.4 %copy-start.4 = (bf16[4,256,768]{2,1,0:T(8,128)(2,1)S(1)}, bf16[4,256,768]{2,1,0:T(8,128)(2,1)}, u32[]{:S(2)}) copy-start(bf16[4,256,768]{2,1,0:T(8,128)(2,1)} %param.9) | copy-start | bytes 4718596
  21.1 1.1 copy-start.6
  24.5 1.1 copy-start
  28.5 48.0 %all-to-all-start = ((bf16[64,16,768]{2,1,0:T(8,128)(2,1)}), bf16[64,16,768]{2,1,0:T(8,128)(2,1)S(1)}, u32[]{:S(2)}, u32[]{:S(2)}) async-start(bf16[64,16,768]{2,1,0:T(8,128)(2,1)} %copy-done), calls=%async_computation | async-start | bytes 3145728 | tf_op jit(solution)/shard_map/all_to_all | solution.py:273
  36.3 30.3 %collective-permute-start.3 = (bf16[256,768]{1,0:T(8,128)(2,1)S(1)}, bf16[256,768]{1,0:T(8,128)(2,1)S(1)}, u32[]{:S(2)}, u32[]{:S(2)}) collective-permute-start(bf16[256,768]{1,0:T(8,128)(2,1)S(1)} %get-tuple-element.23.own), channel_id=1, source_target_pairs={{448,0},{0,64},{64,128},{128,192},{192,256},{256,320},{320,384},{3... | collective-permute-start | bytes 1179656 | tf_op jit(solution)/shard_map/ppermute | solution.py:277
  40.3 26.3 %collective-permute-start.2 = (bf16[256,768]{1,0:T(8,128)(2,1)S(1)}, bf16[256,768]{1,0:T(8,128)(2,1)S(1)}, u32[]{:S(2)}, u32[]{:S(2)}) collective-permute-start(bf16[256,768]{1,0:T(8,128)(2,1)S(1)} %get-tuple-element.23.own), channel_id=1, source_target_pairs={{64,0},{128,64},{192,128},{256,192},{320,256},{384,320},{448,384},... | collective-permute-start | bytes 1179656 | tf_op jit(solution)/shard_map/ppermute | solution.py:277
  48.9 8.9 %collective-permute-start.1 = (f32[32,8,128]{2,1,0:T(8,128)S(1)}, f32[32,8,128]{2,1,0:T(8,128)S(1)}, u32[]{:S(2)}, u32[]{:S(2)}) collective-permute-start(f32[32,8,128]{2,1,0:T(8,128)S(1)} %get-tuple-element.20.ids), channel_id=1, source_target_pairs={{0,1},{1,0},{2,3},{3,2},{4,5},{5,4},{6,7},{7,6},{8,9},{9,8},{10,11... | collective-permute-start | bytes 393224 | tf_op jit(solution)/shard_map/ppermute | solution.py:281
  51.5 13.8 %collective-permute-start.4 = (bf16[128,768]{1,0:T(8,128)(2,1)S(1)}, bf16[128,768]{1,0:T(8,128)(2,1)S(1)}, u32[]{:S(2)}, u32[]{:S(2)}) collective-permute-start(bf16[128,768]{1,0:T(8,128)(2,1)S(1)} %get-tuple-element.24), channel_id=1, source_target_pairs={{128,0},{192,64},{256,128},{320,192},{384,256},{448,320},{0,384},{... | collective-permute-start | bytes 589832 | tf_op jit(solution)/shard_map/ppermute | solution.py:277
  55.2 11.4 %collective-permute-start.5 = (bf16[128,768]{1,0:T(8,128)(2,1)S(1)}, bf16[128,768]{1,0:T(8,128)(2,1)S(1)}, u32[]{:S(2)}, u32[]{:S(2)}) collective-permute-start(bf16[128,768]{1,0:T(8,128)(2,1)S(1)} %get-tuple-element.25), channel_id=1, source_target_pairs={{384,0},{448,64},{0,128},{64,192},{128,256},{192,320},{256,384},{3... | collective-permute-start | bytes 589832 | tf_op jit(solution)/shard_map/ppermute | solution.py:277
  57.7 8.8 %copy-start.7 = (bf16[512,768]{1,0:T(8,128)(2,1)S(1)}, bf16[512,768]{1,0:T(8,128)(2,1)}, u32[]{:S(2)}) copy-start(bf16[512,768]{1,0:T(8,128)(2,1)} %vectors.3) | copy-start | bytes 2359300
  70.4 5.8 %collective-permute-start.6 = (f32[24,1024]{1,0:T(8,128)S(1)}, f32[24,1024]{1,0:T(8,128)S(1)}, u32[]{:S(2)}, u32[]{:S(2)}) collective-permute-start(f32[24,1024]{1,0:T(8,128)S(1)} %get-tuple-element.27.told), channel_id=1, source_target_pairs={{0,1},{1,0},{2,3},{3,2},{4,5},{5,4},{6,7},{7,6},{8,9},{9,8},{10,11... | collective-permute-start | bytes 294920 | tf_op jit(solution)/shard_map/ppermute | solution.py:281
  77.2 20.9 %all-to-all-start.2 = ((f32[32,8,128]{2,1,0:T(8,128)}), f32[32,8,128]{2,1,0:T(8,128)S(1)}, u32[]{:S(2)}, u32[]{:S(2)}) async-start(f32[32,8,128]{2,1,0:T(8,128)} %broadcast_in_dim.2), calls=%async_computation.2 | async-start | bytes 262144 | tf_op jit(solution)/shard_map/all_to_all | solution.py:273
  88.9 1.4 %copy-start.5 = (bf16[4,256,768]{2,1,0:T(8,128)(2,1)S(1)}, bf16[4,256,768]{2,1,0:T(8,128)(2,1)}, u32[]{:S(2)}) copy-start(bf16[4,256,768]{2,1,0:T(8,128)(2,1)} %param.9) | copy-start | bytes 4718596

commit v3 on v2

v3 whole, which is shorter than its diff:
```python
import functools

import jax
import jax.numpy as jnp
from jax import lax
from jax.experimental import pallas as pl
from jax.experimental.pallas import tpu as pltpu
from jax.sharding import Mesh, PartitionSpec as P

sharpness = 0.0625
Z, Y, X, CORES = 8, 8, 4, 2
PLANE = ("y", "x", "c")
EVERY = ("zh", "zl", "y", "x", "c")
FOUR = ("zl", "c")
GROUPS = Y * X
PAIR = 2
TEAM = PAIR * CORES
SLOTS = 4
LOW = 128
f32, bf16, i32 = jnp.float32, jnp.bfloat16, jnp.int32
VMEM = pl.BlockSpec(memory_space=pltpu.VMEM)
SMEM = pl.BlockSpec(memory_space=pltpu.SMEM)
ANY = pl.BlockSpec(memory_space=pl.ANY)
FAR = pl.BlockSpec(memory_space=pltpu.HBM)


def call(body, out_shape, scalars, arrays, name, flops, mib=16, scratch=(), far_in=(), far_out=(), loose=()):
    specs = [ANY if i in loose else FAR if i in far_in else VMEM for i in range(len(arrays))]
    many = isinstance(out_shape, tuple)
    return pl.pallas_call(
        body,
        out_shape=out_shape,
        in_specs=[SMEM] * len(scalars) + specs,
        out_specs=tuple(FAR if i in far_out else VMEM for i in range(len(out_shape))) if many else FAR if far_out else VMEM,
        scratch_shapes=scratch,
        name=name,
        compiler_params=pltpu.CompilerParams(vmem_limit_bytes=mib * 2**20),
        cost_estimate=pl.CostEstimate(flops=flops, bytes_accessed=2**20, transcendentals=0),
    )(*scalars, *arrays)


def shaped(shape, dtype):
    return jax.ShapeDtypeStruct(shape, dtype)


def iota(shape, axis):
    return lax.broadcasted_iota(i32, shape, axis)


def dot(a, b, ca, cb, precision=None):
    return lax.dot_general(
        a, b, (((ca,), (cb,)), ((), ())), preferred_element_type=f32, precision=precision
    )


def as_row(column):
    return jnp.transpose(jnp.broadcast_to(column, (column.shape[0], 128)))[0:1, :]


def row_squares(points):
    wide = points.astype(f32)
    return jnp.sum(wide * wide, axis=1, keepdims=True)


def pack_kernel(coarse, cell, out, coarse_in, cell_in, line, in_sem, out_sem):
    half, features = coarse_in.shape
    fetches = [
        pltpu.make_async_copy(coarse.at[pl.ds(pl.multiple_of(lax.axis_index("zl") * half, half), half)], coarse_in, in_sem.at[0]),
        pltpu.make_async_copy(cell, cell_in, in_sem.at[1]),
    ]
    for fetch in fetches:
        fetch.start()
    for fetch in fetches:
        fetch.wait()
    digits = [cell_in[...] // LOW, cell_in[...] % LOW]
    ids = jnp.concatenate([*digits, jnp.zeros((half - 2 * cell.shape[0], 128), i32)], axis=0).astype(f32)
    line[:, 0:features] = coarse_in[...]
    line[:, features:] = ids.astype(bf16)
    stores = [pltpu.make_async_copy(line, out.at[y], out_sem.at[y]) for y in range(Y)]
    for store in stores:
        store.start()
    for store in stores:
        store.wait()


def route_kernel(
    owned, cell, table, vectors, book, early, send, place, book_squares, wanted,
    cell_in, table_in, rows_in, book_in, rows_out, in_sem, out_sem,
):
    owners, cap, _ = send.shape
    rows = vectors.shape[0]
    pairs = ((cell, cell_in), (table, table_in), (vectors, rows_in), (book, book_in))
    fetches = [pltpu.make_async_copy(source, target, in_sem.at[i]) for i, (source, target) in enumerate(pairs)]
    for fetch in fetches:
        fetch.start()
    fetches[0].wait()
    fetches[1].wait()
    high, low = table.shape
    cell_of = cell_in[...]
    slots = table_in[...]
    in_high = (iota((high, rows), 0) == cell_of // low).astype(bf16)
    in_low = iota((low, rows), 0) == cell_of % low
    owner_table = ((slots // owned) % owners).astype(bf16)
    owner = jnp.sum(jnp.where(in_low, dot(owner_table, in_high, 0, 0), 0.0), axis=0, keepdims=True).astype(i32)
    at_owner = iota((owners, rows), 0) == owner
    before = (iota((rows, rows), 0) < iota((rows, rows), 1)).astype(bf16)
    earlier = dot(at_owner.astype(bf16), before, 1, 0)
    rank = jnp.sum(jnp.where(at_owner, earlier, 0.0), axis=0, keepdims=True).astype(i32)
    position = owner * cap + rank
    place[...] = position
    fetches[2].wait()
    block = 256
    count = block // cap
    stores = []
    for b in range(owners // count):
        pick = (iota((block, rows), 0) + b * block == position).astype(bf16)
        moved = dot(pick, rows_in[...], 1, 0).astype(bf16)
        rows_out[b * count : (b + 1) * count] = moved.reshape(count, cap, -1)
        at = pl.ds(b * count, count)
        store = pltpu.make_async_copy(rows_out.at[at], send.at[at], out_sem.at[b])
        store.start()
        stores.append(store)
    cell_index = (iota((high, low), 0) * low + iota((high, low), 1)).astype(f32)
    line = iota((TEAM * owned, 128), 0)
    ids = jnp.full(line.shape, -1.0, f32)
    for member in range(TEAM):
        start = (lax.axis_index(EVERY) ^ (member % CORES + member // CORES * GROUPS * CORES)) * owned
        for s in range(owned):
            hit = jnp.where(slots == start + s, cell_index, 0.0)
            cell_id = jnp.sum(jnp.sum(hit, axis=1, keepdims=True), axis=0, keepdims=True)
            ids = jnp.where(line == member * owned + s, cell_id, ids)
    wanted[...] = ids
    fetches[3].wait()
    for b in range(book.shape[0] // block):
        at = slice(b * block, (b + 1) * block)
        book_squares[:, at] = as_row(row_squares(book_in[at]))
    for store in stores:
        store.wait()


def coarse_kernel(
    cap, vectors, vectors2, vectors3, vectors4, wanted, gathered, weights, told, scores
):
    parity, core = lax.axis_index("zl"), lax.axis_index("c")
    rows, features = vectors.shape
    part = scores.shape[2]
    slab = Y * part
    cells = wanted[:, 0:1].astype(i32)
    points = gathered[:, 0:features]
    squares = -sharpness * row_squares(points)
    told[...] = jnp.zeros(told.shape, f32)
    tops = []
    for side, against in enumerate((vectors, vectors2, vectors3, vectors4)):
        across = slice(side * rows, (side + 1) * rows)
        vector_squares = -sharpness * as_row(row_squares(against[...]))
        score = (vector_squares + squares) + (2.0 * sharpness) * dot(points, against[...], 1, 1)
        tops.append(jnp.max(score, axis=0, keepdims=True))
        for x in range(X):
            scores[:, x, :, across] = score[x * slab : (x + 1) * slab].reshape(Y, part, rows)
    line = iota((TEAM * SLOTS, X * slab), 1)
    group = line // part % Y * X + line // slab
    inside = (group * CORES + core) * (PAIR * part) + parity * part + line % part == cells
    told[8:24, :] = dot(inside.astype(bf16), points, 1, 0)
    for side in range(TEAM):
        across = slice(side * rows, (side + 1) * rows)
        total = jnp.zeros((1, rows), f32)
        for y in range(Y):
            e = jnp.exp(scores[y, :, :, across].reshape(X * part, rows) - tops[side])
            total = total + jnp.sum(e, axis=0, keepdims=True)
            weights[y, :, :, across] = e.reshape(X, part, rows)
        told[side : side + 1, 0:rows] = tops[side]
        told[4 + side : 5 + side, 0:rows] = total
    ids = gathered[:, features:].astype(f32).reshape(GROUPS, part, 128)
    codes = jnp.concatenate([ids[:, j, :] * LOW + ids[:, 4 + j, :] for j in range(4)], axis=1)
    places = GROUPS * CORES * cap
    before = (iota((rows, rows), 0) < iota((rows, rows), 1)).astype(bf16)
    spread = (iota((cap, places), 1) % cap == iota((cap, places), 0)).astype(bf16)
    source = iota((GROUPS, places), 0)
    target = iota((GROUPS, places), 1) // cap
    filled = (source % Y * X + source // Y) * CORES + core == target
    for member in range(CORES):
        found = jnp.zeros(codes.shape, f32)
        for s in range(SLOTS):
            at = member * SLOTS + s
            found = found + jnp.where(codes == wanted[at : at + 1, 0:1], s + 1.0, 0.0)
        earlier = dot((found > 0.0).astype(bf16), before, 1, 0)
        ranked = jnp.concatenate(
            [jnp.sum(jnp.where(earlier == float(r), found, 0.0), axis=1, keepdims=True) for r in range(cap)], axis=1
        )
        across = dot(ranked.astype(bf16), spread, 1, 0)
        row = jnp.sum(jnp.where(filled, across, 0.0), axis=0, keepdims=True)
        for half in range(2):
            at = 24 + 2 * member + half
            told[at : at + 1, 0 : places // 2] = row[:, half * places // 2 : (half + 1) * places // 2]


def share_kernel(rows, weights, heard, shares):
    me = lax.axis_index(FOUR)
    factors = []
    for side in range(TEAM):
        tops = [heard[me ^ t, t ^ side : (t ^ side) + 1, 0:rows] for t in range(TEAM)]
        totals = [heard[me ^ t, 4 + (t ^ side) : 5 + (t ^ side), 0:rows] for t in range(TEAM)]
        highest = functools.reduce(jnp.maximum, tops)
        total = sum(n * jnp.exp(top - highest) for n, top in zip(totals, tops, strict=True))
        factors.append(jnp.exp(tops[0] - highest) / total)
    factor = jnp.concatenate(factors, axis=1)
    for b in range(Y // 2):
        probs = weights[2 * b : 2 * b + 2].reshape(128, TEAM * rows) * factor
        lanes = probs[:, 0:128]
        for j in range(1, TEAM * rows // 128):
            lanes = lanes + probs[:, j * 128 : (j + 1) * 128]
        share = jnp.sum(jnp.transpose(lanes), axis=0, keepdims=True)
        shares[:, b : b + 1, :] = jnp.broadcast_to(share[None], (shares.shape[0], 1, 128))


def fine_kernel(
    got, heard, book, book_squares, spread, out, weights, residual
):
    owners, cap = spread.shape
    rows, features = got.shape
    fine = book.shape[0] // SLOTS
    me = lax.axis_index(FOUR)
    centres = sum(heard[me ^ t, 8 + t * SLOTS : 8 + (t + 1) * SLOTS, :] for t in range(TEAM))
    centres = jnp.concatenate([centres, jnp.zeros(centres.shape, f32)], axis=0).astype(bf16)
    halves = [heard[me, 24 + h : 25 + h, 0 : rows // 2] + heard[me ^ 1, 26 + h : 27 + h, 0 : rows // 2] for h in range(2)]
    local = jnp.concatenate(halves, axis=1) - 1.0
    squares = [
        jnp.transpose(jnp.broadcast_to(book_squares[:, s * fine : (s + 1) * fine], (128, fine)))[:, 0:1] for s in range(SLOTS)
    ]
    block = 256
    moved_squares = []
    for b in range(rows // block):
        at = slice(b * block, (b + 1) * block)
        chosen = (iota((8, block), 0).astype(f32) == local[:, at]).astype(bf16)
        moved = (got[at].astype(f32) - dot(chosen, centres, 0, 0)).astype(bf16)
        residual[at] = moved
        moved_squares.append(as_row(row_squares(moved)))
    parts = []
    masses = [jnp.zeros((fine, 1), f32)] * SLOTS
    for b in range(rows // block):
        at = slice(b * block, (b + 1) * block)
        slot = local[:, at]
        inside = [slot == s for s in range(SLOTS)]
        distance = jnp.zeros((fine, block), f32)
        for s in range(SLOTS):
            products = dot(book[s * fine : (s + 1) * fine], residual[at], 1, 1)
            distance = jnp.where(inside[s], moved_squares[b] + squares[s] - 2.0 * products, distance)
        score = -sharpness * distance
        e = jnp.exp(score - jnp.max(score, axis=0, keepdims=True))
        weight = e * ((slot >= 0.0).astype(f32) / jnp.sum(e, axis=0, keepdims=True))
        parts.append(jnp.sum(weight * distance, axis=0, keepdims=True) / features)
        for s in range(SLOTS):
            only = jnp.where(inside[s], weight, 0.0)
            weights[s * fine : (s + 1) * fine, at] = only.astype(bf16)
            masses[s] = masses[s] + jnp.sum(only, axis=1, keepdims=True)
    row = jnp.concatenate(parts, axis=1)
    places = (iota((cap, rows), 1) % cap == iota((cap, rows), 0)).astype(f32)
    at_owner = iota((owners, rows), 1) // cap == iota((owners, rows), 0)
    spread[...] = dot(jnp.where(at_owner, row, 0.0), places, 1, 1, lax.Precision.HIGHEST)
    for s in range(SLOTS):
        at = slice(s * fine, (s + 1) * fine)
        total = dot(weights[at], residual[...], 1, 0)
        out[at] = ((book[at].astype(f32) + total) * (1.0 / (1.0 + masses[s]))).astype(bf16)


def answer_kernel(spread, shares, out):
    owners, cap = spread.shape
    total = jnp.sum(jnp.sum(shares[...].reshape(Z // PAIR, PAIR, X, 4, 128), axis=2), axis=0).reshape(X, 2, 128)
    quarter = jnp.sum(jnp.where(iota(total.shape, 0) == lax.axis_index("x"), total, 0.0), axis=0)
    line = jnp.concatenate([spread[...], jnp.zeros((owners, 128 - cap), f32)], axis=1)
    out[:, 0:2, :] = jnp.broadcast_to(quarter[None], (owners, 2, 128))
    out[:, 2:4, :] = jnp.broadcast_to(line[:, None, :], (owners, 2, 128))


def finish_kernel(scale, got, place, distortion, share):
    owners = got.shape[0]
    rows = place.shape[1]
    cap = 2 * rows // owners
    position = place[...]
    at_owner = (iota((owners, rows), 0) == position // cap).astype(f32)
    at_rank = iota((cap, rows), 0) == position % cap
    whole = got[...]
    returned = whole[:, 2, :][:, 0:cap]
    across = dot(returned, at_owner, 0, 0, lax.Precision.HIGHEST)
    distortion[...] = jnp.sum(jnp.where(at_rank, across, 0.0), axis=0, keepdims=True)
    quarters = jnp.sum(whole[:, 0:2, :].reshape(Y, X * CORES, 2, 128), axis=0) * scale
    halves = [jnp.concatenate([quarters[x * CORES + c] for x in range(X)], axis=0) for c in range(CORES)]
    for yl in range(2):
        for xh in range(2):
            pieces = [
                halves[c][p * 4 : p * 4 + 4, yl * 64 + (2 * xh + xl) * 16 : yl * 64 + (2 * xh + xl + 1) * 16]
                for xl in range(2)
                for c in range(CORES)
                for p in range(PAIR)
            ]
            share[:, 2 * yl + xh, :] = jnp.concatenate(pieces, axis=1)


def after(x, *others):
    return pl.pallas_call(
        lambda *refs: None,
        out_shape=shaped(x.shape, x.dtype),
        in_specs=[ANY] * (1 + len(others)),
        out_specs=ANY,
        input_output_aliases={0: 0},
        name="after",
        compiler_params=pltpu.CompilerParams(vmem_limit_bytes=2**20),
    )(x, *others)


def exchange(x, axes):
    return lax.all_to_all(x, axes, 0, 0, tiled=True)


def from_neighbour(x):
    return lax.ppermute(x, "zl", [(0, 1), (1, 0)])


def from_partner(x):
    return lax.ppermute(x, "c", [(0, 1), (1, 0)])


def on_device(vectors, cell_of, cell_slot, coarse, fine_book):
    rows, features = vectors.shape
    owned, fine, _ = fine_book.shape
    owners = GROUPS * CORES
    cap = 2 * rows // owners
    cells = cell_slot.shape[0]
    part = coarse.shape[0] // PAIR
    book = fine_book.reshape(owned * fine, features)
    table = cell_slot.reshape(-1, LOW)

    packed = call(
        pack_kernel,
        shaped((Y, part, features + 128), bf16),
        [],
        [coarse, cell_of.reshape(-1, 128)],
        "pack",
        10**6,
        mib=60,
        far_in=(0, 1),
        far_out=(0,),
        scratch=[
            pltpu.VMEM((part, features), bf16),
            pltpu.VMEM((rows // 128, 128), i32),
            pltpu.VMEM((part, features + 128), bf16),
            pltpu.SemaphoreType.DMA((2,)),
            pltpu.SemaphoreType.DMA((Y,)),
        ],
    )
    first = exchange(packed, ("y",)).reshape(Y * part, features + 128)
    vectors2 = from_partner(vectors)
    send, place, book_squares, wanted = call(
        functools.partial(route_kernel, owned),
        (
            shaped((owners, cap, features), bf16),
            shaped((1, rows), i32),
            shaped((1, owned * fine), f32),
            shaped((TEAM * owned, 128), f32),
        ),
        [],
        [cell_of.reshape(1, rows), table, vectors, book, vectors2],
        "route",
        10**9,
        mib=60,
        far_in=(0, 1, 2, 3),
        far_out=(0,),
        loose=(4,),
        scratch=[
            pltpu.VMEM((1, rows), i32),
            pltpu.VMEM(table.shape, i32),
            pltpu.VMEM((rows, features), bf16),
            pltpu.VMEM(book.shape, bf16),
            pltpu.VMEM((owners, cap, features), bf16),
            pltpu.SemaphoreType.DMA((4,)),
            pltpu.SemaphoreType.DMA((owners * cap // 256,)),
        ],
    )
    got = exchange(send, PLANE).reshape(owners * cap, features)

    gathered = lax.all_gather(first, "x", axis=0, tiled=True)
    vectors3 = after(from_neighbour(vectors), gathered)
    vectors4 = from_partner(vectors3)
    weights, told = call(
        functools.partial(coarse_kernel, cap),
        (shaped((Y, X, part, TEAM * rows), f32), shaped((32, features), f32)),
        [],
        [vectors, vectors2, vectors3, vectors4, wanted, gathered],
        "coarse_part",
        2 * 10**9,
        mib=28,
        scratch=[pltpu.VMEM((Y, X, part, TEAM * rows), f32)],
    )
    heard = lax.all_gather(told, FOUR, axis=0)
    shares = call(
        functools.partial(share_kernel, rows), shaped((Z * X, 4, 128), f32), [], [weights, heard], "share", 10**9
    )
    shares = exchange(shares, ("zh", "zl", "x"))

    spread, fine_next = call(
        fine_kernel,
        (shaped((owners, cap), f32), shaped(book.shape, bf16)),
        [],
        [got, heard, book, book_squares],
        "fine_part",
        3 * 10**9,
        mib=24,
        scratch=[
            pltpu.VMEM((owned * fine, owners * cap), bf16),
            pltpu.VMEM((owners * cap, features), bf16),
        ],
    )
    answer = call(answer_kernel, shaped((owners, 4, 128), f32), [], [spread, shares], "answer", 10**6)
    back = exchange(answer, PLANE)
    distortion, coarse_share = call(
        functools.partial(finish_kernel, owned / rows),
        (shaped((1, rows), f32), shaped((4, 4, 128), f32)),
        [],
        [back, place],
        "finish",
        10**8,
    )
    return (coarse_share.reshape(cells), fine_next.reshape(fine_book.shape), distortion.reshape(rows))


def solution(mesh):
    grid = Mesh(mesh.devices.reshape(Z // PAIR, PAIR, Y, X, CORES), EVERY)
    return jax.shard_map(
        on_device,
        mesh=grid,
        in_specs=(P(EVERY, None), P(EVERY), P(), P(PLANE, None), P(EVERY, None, None)),
        out_specs=(P(), P(EVERY, None, None), P(EVERY)),
        check_vma=False,
    )
```

time: 118 us -> 112 us (0.949)
  blocking collectives: 17.7 us -> 45.3 us
  starting transfers between devices: 59.1 us -> 35.8 us
  local copies, waits for them, and re-layouts: 8.67 us -> 2.3 us
  waiting for transfers between devices: 14.1 us -> 10.7 us
    all_gather x0 -> x2, blocking collectives: none -> 24.7 us  [the longest x1 18.1 us: on_device(): gathered = lax.all_gather(first, 'x', axis=0, tiled=True)]
    ppermute x4 -> x1, starting transfers between devices: 18.8 us -> 2.88 us  [from_neighbour(): return lax.ppermute(x, 'zl', [(0, 1), (1, 0)])]
    all_to_all x3, starting transfers between devices: 30 us -> 19.9 us  [exchange(): return lax.all_to_all(x, axes, 0, 0, tiled=True)]
    ppermute x4 -> x1, waiting for transfers between devices: 7.38 us -> 0.01 us  [from_neighbour(): return lax.ppermute(x, 'zl', [(0, 1), (1, 0)])]
    unnamed x16 -> x14, local copies, waits for them, and re-layouts: 7.25 us -> 2.3 us
    all_to_all x3, waiting for transfers between devices: 4.5 us -> 8.81 us  [exchange(): return lax.all_to_all(x, axes, 0, 0, tiled=True)]
    all_to_all x1, blocking collectives: 17.7 us -> 20.6 us  [exchange(): return lax.all_to_all(x, axes, 0, 0, tiled=True)]
    ppermute x3 -> x2, starting transfers between devices: 10.4 us -> 13 us  [from_partner(): return lax.ppermute(x, 'c', [(0, 1), (1, 0)])]
  transfers between devices with their start and end apart: 10 -> 6, of which waited for: 6 -> 4; matrix products, arithmetic and copies ran while one was open for 1% -> 0% of each run, Pallas kernels for 12% -> 14%
where the time goes in v3:
time: 112 us
  blocking collectives  45.3 us (40%)
  starting transfers between devices  35.8 us (32%)
  Pallas kernels  16.9 us (15%)
  waiting for transfers between devices  10.7 us (10%)
  local copies, waits for them, and re-layouts  2.3 us (2%)
    all_to_all x1, blocking collectives, exchange(): return lax.all_to_all(x, axes, 0, 0, tiled=True)  20.6 us
    all_to_all x3, starting transfers between devices, exchange(): return lax.all_to_all(x, axes, 0, 0, tiled=True)  19.9 us
    all_gather x1, blocking collectives, on_device(): gathered = lax.all_gather(first, 'x', axis=0, tiled=True)  18.1 us
    pallas_call x7, Pallas kernels, call(): pl.pallas_call(body, out_shape=out_shape, in_specs=[SMEM] * len(scalars)...  16.9 us
    ppermute x2, starting transfers between devices, from_partner(): return lax.ppermute(x, 'c', [(0, 1), (1, 0)])  13 us
    all_to_all x3, waiting for transfers between devices, exchange(): return lax.all_to_all(x, axes, 0, 0, tiled=True)  8.81 us
    all_gather x1, blocking collectives, on_device(): heard = lax.all_gather(told, FOUR, axis=0)  6.58 us
    ppermute x1, starting transfers between devices, from_neighbour(): return lax.ppermute(x, 'zl', [(0, 1), (1, 0)])  2.88 us
  transfers between devices with their start and end apart: 6, of which 4 were waited for; matrix products, arithmetic and copies ran while one was open for 0% of the time, Pallas kernels for 14%

profile of v3, /device:TPU:1, one launch (start us, length us, event | category | flops | bytes accessed | tf_op | source)
XLA Modules:
  0.0 111.8 jit_solution(12137727748832888438)
XLA Ops:
  0.6 8.8 %collective-permute-start = (bf16[512,768]{1,0:T(8,128)(2,1)}, bf16[512,768]{1,0:T(8,128)(2,1)S(1)}, u32[]{:S(2)}, u32[]{:S(2)}) collective-permute-start(bf16[512,768]{1,0:T(8,128)(2,1)} %vectors.3), channel_id=1, source_target_pairs={{0,1},{1,0},{2,3},{3,2},{4,5},{5,4},{6,7},{7,6},{8,9},{9,8},{10,11... | collective-permute-start | bytes 2359304 | tf_op jit(solution)/shard_map/ppermute | solution.py:320
  9.4 1.5 %pack.1 = bf16[8,16,896]{2,1,0:T(8,128)(2,1)} custom-call(bf16[32,768]{1,0:T(8,128)(2,1)} %coarse.1, s32[4,128]{1,0:T(4,128)} %bitcast.16), custom_call_target="tpu_custom_call" | custom-call | flops 1000000 | bytes 1048576 | tf_op jit(solution)/shard_map/pack/pallas_call | solution.py:30
  11.0 3.4 %all-to-all-start.1 = ((bf16[8,16,896]{2,1,0:T(8,128)(2,1)}), bf16[8,16,896]{2,1,0:T(8,128)(2,1)S(1)}, u32[]{:S(2)}, u32[]{:S(2)}) async-start(bf16[8,16,896]{2,1,0:T(8,128)(2,1)} %pack.1), calls=%async_computation.1 | async-start | bytes 458752 | tf_op jit(solution)/shard_map/all_to_all | solution.py:312
  14.4 0.0 collective-permute-done.early.vectors2
  14.4 0.0 copy-start.2
  14.4 0.9 copy-done.2
  15.3 3.6 %route.1 = (bf16[64,16,768]{2,1,0:T(8,128)(2,1)}, s32[1,512]{1,0:T(1,128)}, f32[1,1024]{1,0:T(1,128)}, f32[16,128]{1,0:T(8,128)}) custom-call(s32[1,512]{1,0:T(1,128)} %bitcast.17, s32[16,128]{1,0:T(8,128)} %bitcast.18, bf16[512,768]{1,0:T(8,128)(2,1)} %vectors.3, bf16[1024,768]{1,0:T(8,128)(2,1)} %bitcast.13, bf16[512,768]{1,0:T(8,128)(2,1)} %copy-done.2), custom_call_target="tpu_custom_call" | custom-call | flops 1000000000 | bytes 1048576 | tf_op jit(solution)/shard_map/route/pallas_call | solution.py:30
  18.9 7.1 %all-to-all-done.1 = bf16[8,16,896]{2,1,0:T(8,128)(2,1)S(1)} async-done(((bf16[8,16,896]{2,1,0:T(8,128)(2,1)}), bf16[8,16,896]{2,1,0:T(8,128)(2,1)S(1)}, u32[]{:S(2)}, u32[]{:S(2)}) %all-to-all-start.1) | async-done | bytes 229408 | tf_op jit(solution)/shard_map/all_to_all | solution.py:312
  26.0 0.0 copy-start.1
  26.0 4.7 %all-to-all-start = ((bf16[64,16,768]{2,1,0:T(8,128)(2,1)}), bf16[64,16,768]{2,1,0:T(8,128)(2,1)S(1)}, u32[]{:S(2)}, u32[]{:S(2)}) async-start(bf16[64,16,768]{2,1,0:T(8,128)(2,1)} %get-tuple-element.13), calls=%async_computation | async-start | bytes 3145728 | tf_op jit(solution)/shard_map/all_to_all | solution.py:312
  30.7 0.0 copy-done.1
  30.7 2.9 %collective-permute-start.1 = (bf16[512,768]{1,0:T(8,128)(2,1)S(1)}, bf16[512,768]{1,0:T(8,128)(2,1)S(1)}, u32[]{:S(2)}, u32[]{:S(2)}) collective-permute-start(bf16[512,768]{1,0:T(8,128)(2,1)S(1)} %copy-done.1), channel_id=1, source_target_pairs={{0,64},{64,0},{1,65},{65,1},{2,66},{66,2},{3,67},{67,3},{4,68},{68... | collective-permute-start | bytes 2359304 | tf_op jit(solution)/shard_map/ppermute | solution.py:316
  33.6 0.0 copy-start.3
  33.6 0.0 copy-start.5
  33.6 18.1 %all_gather.9.refs_1_.gathered = bf16[512,896]{1,0:T(8,128)(2,1)S(1)} all-gather(bf16[128,896]{1,0:T(8,128)(2,1)S(1)} %bitcast.15), channel_id=1, replica_groups=mesh['zh'=4,'zl'=2,'y'=8,'x'=4,'c'=2] {'x'}, dimensions={0}, use_global_device_ids=true | all-gather | bytes 1146880 | tf_op jit(solution)/shard_map/all_gather | solution.py:381
  51.7 0.0 collective-permute-done.1.refs_0_
  51.7 4.2 %collective-permute-start.2 = (bf16[512,768]{1,0:T(8,128)(2,1)S(1)}, bf16[512,768]{1,0:T(8,128)(2,1)S(1)}, u32[]{:S(2)}, u32[]{:S(2)}) collective-permute-start(bf16[512,768]{1,0:T(8,128)(2,1)S(1)} %after.1.vectors3), channel_id=1, source_target_pairs={{0,1},{1,0},{2,3},{3,2},{4,5},{5,4},{6,7},{7,6},{8,9},{9,8},{10,11... | collective-permute-start | bytes 2359304 | tf_op jit(solution)/shard_map/ppermute | solution.py:320
  56.0 1.9 %collective-permute-done.2.vectors4 = bf16[512,768]{1,0:T(8,128)(2,1)S(1)} collective-permute-done((bf16[512,768]{1,0:T(8,128)(2,1)S(1)}, bf16[512,768]{1,0:T(8,128)(2,1)S(1)}, u32[]{:S(2)}, u32[]{:S(2)}) %collective-permute-start.2) | collective-permute-done | bytes 786464 | tf_op jit(solution)/shard_map/ppermute | solution.py:320
  57.9 0.0 copy-done.3
  57.9 0.0 copy-done.5
  57.9 4.1 %coarse_part.1 = (f32[8,4,16,2048]{3,2,1,0:T(8,128)S(1)}, f32[32,768]{1,0:T(8,128)S(1)}) custom-call(bf16[512,768]{1,0:T(8,128)(2,1)S(1)} %copy-done.1, bf16[512,768]{1,0:T(8,128)(2,1)S(1)} %copy-done.3, bf16[512,768]{1,0:T(8,128)(2,1)S(1)} %after.1.vectors3, bf16[512,768]{1,0:T(8,128)(2,1)S(1)} %collective-permute-done.2.vectors4, f32[16,128]{1,0:T(8,128)S(1)} %copy-done.5, ...), custom_call_target="tpu_custom_call" | custom-call | flops 2000000000 | bytes 1048576 | tf_op jit(solution)/shard_map/coarse_part/pallas_call | solution.py:30
  62.0 6.6 %all-gather = f32[128,768]{1,0:T(8,128)S(1)} all-gather(f32[32,768]{1,0:T(8,128)S(1)} %get-tuple-element.15), channel_id=2, replica_groups=mesh['zh'=4,'zl'=2,'y'=8,'x'=4,'c'=2] {'zl','c'}, dimensions={0}, use_global_device_ids=true | all-gather | bytes 491520 | tf_op jit(solution)/shard_map/all_gather | solution.py:394
  68.6 0.0 copy-start.6
  68.6 1.0 share.1
  69.6 0.2 all-to-all-done
  69.8 11.8 %all-to-all-start.2 = ((f32[32,4,128]{2,1,0:T(4,128)}), f32[32,4,128]{2,1,0:T(4,128)S(1)}, u32[]{:S(2)}, u32[]{:S(2)}) async-start(f32[32,4,128]{2,1,0:T(4,128)} %share.1), calls=%async_computation.2 | async-start | bytes 131072 | tf_op jit(solution)/shard_map/all_to_all | solution.py:312
  81.7 0.0 copy-done.6
  81.7 0.0 copy-start
  81.7 1.4 %copy-done = bf16[4,256,768]{2,1,0:T(8,128)(2,1)S(1)} copy-done((bf16[4,256,768]{2,1,0:T(8,128)(2,1)S(1)}, bf16[4,256,768]{2,1,0:T(8,128)(2,1)}, u32[]{:S(2)}) %copy-start) | copy-done | bytes 1572888
  83.1 0.0 copy-start.4
  83.1 5.7 %fine_part.1 = (f32[64,16]{1,0:T(8,128)S(1)}, bf16[1024,768]{1,0:T(8,128)(2,1)}) custom-call(bf16[1024,768]{1,0:T(8,128)(2,1)S(1)} %bitcast.10, f32[4,32,768]{2,1,0:T(8,128)S(1)} %bitcast.12, bf16[1024,768]{1,0:T(8,128)(2,1)S(1)} %bitcast.14, f32[1,1024]{1,0:T(1,128)S(1)} %copy-done.6), custom_call_target="tpu_custom_call" | custom-call | flops 3000000000 | bytes 1048576 | tf_op jit(solution)/shard_map/fine_part/pallas_call | solution.py:30
  88.8 1.5 %all-to-all-done.2.shares = f32[32,4,128]{2,1,0:T(4,128)S(1)} async-done(((f32[32,4,128]{2,1,0:T(4,128)}), f32[32,4,128]{2,1,0:T(4,128)S(1)}, u32[]{:S(2)}, u32[]{:S(2)}) %all-to-all-start.2) | async-done | bytes 65568 | tf_op jit(solution)/shard_map/all_to_all | solution.py:312
  90.3 0.1 answer.1
  90.4 20.6 %all_to_all.20.got = f32[64,4,128]{2,1,0:T(4,128)S(1)} all-to-all(f32[64,4,128]{2,1,0:T(4,128)S(1)} %answer.1), channel_id=1, replica_groups=mesh['zh'=4,'zl'=2,'y'=8,'x'=4,'c'=2] {'y','x','c'}, dimensions={0} | all-to-all | bytes 262144 | tf_op jit(solution)/shard_map/all_to_all | solution.py:312
  110.9 0.0 copy-done.4
  110.9 0.8 finish.1
  (1 shorter events, 0.0 us)
Async XLA Ops:
  0.6 13.8 %collective-permute-start = (bf16[512,768]{1,0:T(8,128)(2,1)}, bf16[512,768]{1,0:T(8,128)(2,1)S(1)}, u32[]{:S(2)}, u32[]{:S(2)}) collective-permute-start(bf16[512,768]{1,0:T(8,128)(2,1)} %vectors.3), channel_id=1, source_target_pairs={{0,1},{1,0},{2,3},{3,2},{4,5},{5,4},{6,7},{7,6},{8,9},{9,8},{10,11... | collective-permute-start | bytes 2359304 | tf_op jit(solution)/shard_map/ppermute | solution.py:320
  11.0 15.0 %all-to-all-start.1 = ((bf16[8,16,896]{2,1,0:T(8,128)(2,1)}), bf16[8,16,896]{2,1,0:T(8,128)(2,1)S(1)}, u32[]{:S(2)}, u32[]{:S(2)}) async-start(bf16[8,16,896]{2,1,0:T(8,128)(2,1)} %pack.1), calls=%async_computation.1 | async-start | bytes 458752 | tf_op jit(solution)/shard_map/all_to_all | solution.py:312
  14.4 0.9 copy-start.2
  26.0 4.7 %copy-start.1 = (bf16[512,768]{1,0:T(8,128)(2,1)S(1)}, bf16[512,768]{1,0:T(8,128)(2,1)}, u32[]{:S(2)}) copy-start(bf16[512,768]{1,0:T(8,128)(2,1)} %vectors.3) | copy-start | bytes 2359300
  26.0 43.8 %all-to-all-start = ((bf16[64,16,768]{2,1,0:T(8,128)(2,1)}), bf16[64,16,768]{2,1,0:T(8,128)(2,1)S(1)}, u32[]{:S(2)}, u32[]{:S(2)}) async-start(bf16[64,16,768]{2,1,0:T(8,128)(2,1)} %get-tuple-element.13), calls=%async_computation | async-start | bytes 3145728 | tf_op jit(solution)/shard_map/all_to_all | solution.py:312
  30.7 21.0 %collective-permute-start.1 = (bf16[512,768]{1,0:T(8,128)(2,1)S(1)}, bf16[512,768]{1,0:T(8,128)(2,1)S(1)}, u32[]{:S(2)}, u32[]{:S(2)}) collective-permute-start(bf16[512,768]{1,0:T(8,128)(2,1)S(1)} %copy-done.1), channel_id=1, source_target_pairs={{0,64},{64,0},{1,65},{65,1},{2,66},{66,2},{3,67},{67,3},{4,68},{68... | collective-permute-start | bytes 2359304 | tf_op jit(solution)/shard_map/ppermute | solution.py:316
  33.6 24.3 %copy-start.3 = (bf16[512,768]{1,0:T(8,128)(2,1)S(1)}, bf16[512,768]{1,0:T(8,128)(2,1)}, u32[]{:S(2)}) copy-start(bf16[512,768]{1,0:T(8,128)(2,1)} %copy-done.2) | copy-start | bytes 2359300
  33.6 24.3 %copy-start.5 = (f32[16,128]{1,0:T(8,128)S(1)}, f32[16,128]{1,0:T(8,128)}, u32[]{:S(2)}) copy-start(f32[16,128]{1,0:T(8,128)} %get-tuple-element.14.wanted) | copy-start | bytes 24580
  51.7 6.1 %collective-permute-start.2 = (bf16[512,768]{1,0:T(8,128)(2,1)S(1)}, bf16[512,768]{1,0:T(8,128)(2,1)S(1)}, u32[]{:S(2)}, u32[]{:S(2)}) collective-permute-start(bf16[512,768]{1,0:T(8,128)(2,1)S(1)} %after.1.vectors3), channel_id=1, source_target_pairs={{0,1},{1,0},{2,3},{3,2},{4,5},{5,4},{6,7},{7,6},{8,9},{9,8},{10,11... | collective-permute-start | bytes 2359304 | tf_op jit(solution)/shard_map/ppermute | solution.py:320
  68.6 13.1 %copy-start.6 = (f32[1,1024]{1,0:T(1,128)S(1)}, f32[1,1024]{1,0:T(1,128)}, u32[]{:S(2)}) copy-start(f32[1,1024]{1,0:T(1,128)} %get-tuple-element.16.book_squares) | copy-start | bytes 12292
  69.8 20.5 %all-to-all-start.2 = ((f32[32,4,128]{2,1,0:T(4,128)}), f32[32,4,128]{2,1,0:T(4,128)S(1)}, u32[]{:S(2)}, u32[]{:S(2)}) async-start(f32[32,4,128]{2,1,0:T(4,128)} %share.1), calls=%async_computation.2 | async-start | bytes 131072 | tf_op jit(solution)/shard_map/all_to_all | solution.py:312
  81.7 1.4 %copy-start = (bf16[4,256,768]{2,1,0:T(8,128)(2,1)S(1)}, bf16[4,256,768]{2,1,0:T(8,128)(2,1)}, u32[]{:S(2)}) copy-start(bf16[4,256,768]{2,1,0:T(8,128)(2,1)} %param.9) | copy-start | bytes 4718596
  83.1 27.8 %copy-start.4 = (s32[1,512]{1,0:T(1,128)S(1)}, s32[1,512]{1,0:T(1,128)}, u32[]{:S(2)}) copy-start(s32[1,512]{1,0:T(1,128)} %get-tuple-element.19.place) | copy-start | bytes 6148

commit v4 on v3

--- a/solution.py
+++ b/solution.py
@@ -138,9 +138,31 @@
         store.wait()
 
 
-def coarse_kernel(
-    cap, vectors, vectors2, vectors3, vectors4, wanted, gathered, weights, told, scores
-):
+def quarter_weights(points, squares, against, scores, weights, across):
+    part, rows = scores.shape[2], against.shape[0]
+    slab = Y * part
+    vector_squares = -sharpness * as_row(row_squares(against[...]))
+    score = (vector_squares + squares) + (2.0 * sharpness) * dot(points, against[...], 1, 1)
+    for x in range(X):
+        scores[:, x, :, across] = score[x * slab : (x + 1) * slab].reshape(Y, part, rows)
+    top = jnp.max(score, axis=0, keepdims=True).astype(bf16).astype(f32)
+    total = jnp.zeros((1, rows), f32)
+    for y in range(Y):
+        e = jnp.exp(scores[y, :, :, across].reshape(X * part, rows) - top)
+        total = total + jnp.sum(e, axis=0, keepdims=True)
+        weights[y, :, :, across] = e.reshape(X, part, rows)
+    return top, total
+
+
+def note_sums(told, side, top, total):
+    rows = top.shape[1]
+    upper = total.astype(bf16).astype(f32)
+    told[side : side + 1, 0:rows] = top
+    told[4 + side : 5 + side, 0:rows] = upper
+    told[8 + side : 9 + side, 0:rows] = total - upper
+
+
+def coarse_kernel(cap, vectors, vectors2, vectors3, wanted, gathered, weights, told, scores):
     parity, core = lax.axis_index("zl"), lax.axis_index("c")
     rows, features = vectors.shape
     part = scores.shape[2]
@@ -149,27 +171,13 @@
     points = gathered[:, 0:features]
     squares = -sharpness * row_squares(points)
     told[...] = jnp.zeros(told.shape, f32)
-    tops = []
-    for side, against in enumerate((vectors, vectors2, vectors3, vectors4)):
+    for side, against in enumerate((vectors, vectors2, vectors3)):
         across = slice(side * rows, (side + 1) * rows)
-        vector_squares = -sharpness * as_row(row_squares(against[...]))
-        score = (vector_squares + squares) + (2.0 * sharpness) * dot(points, against[...], 1, 1)
-        tops.append(jnp.max(score, axis=0, keepdims=True))
-        for x in range(X):
-            scores[:, x, :, across] = score[x * slab : (x + 1) * slab].reshape(Y, part, rows)
+        note_sums(told, side, *quarter_weights(points, squares, against, scores, weights, across))
     line = iota((TEAM * SLOTS, X * slab), 1)
     group = line // part % Y * X + line // slab
     inside = (group * CORES + core) * (PAIR * part) + parity * part + line % part == cells
-    told[8:24, :] = dot(inside.astype(bf16), points, 1, 0)
-    for side in range(TEAM):
-        across = slice(side * rows, (side + 1) * rows)
-        total = jnp.zeros((1, rows), f32)
-        for y in range(Y):
-            e = jnp.exp(scores[y, :, :, across].reshape(X * part, rows) - tops[side])
-            total = total + jnp.sum(e, axis=0, keepdims=True)
-            weights[y, :, :, across] = e.reshape(X, part, rows)
-        told[side : side + 1, 0:rows] = tops[side]
-        told[4 + side : 5 + side, 0:rows] = total
+    told[12:28, :] = dot(inside.astype(bf16), points, 1, 0)
     ids = gathered[:, features:].astype(f32).reshape(GROUPS, part, 128)
     codes = jnp.concatenate([ids[:, j, :] * LOW + ids[:, 4 + j, :] for j in range(4)], axis=1)
     places = GROUPS * CORES * cap
@@ -190,25 +198,38 @@
         across = dot(ranked.astype(bf16), spread, 1, 0)
         row = jnp.sum(jnp.where(filled, across, 0.0), axis=0, keepdims=True)
         for half in range(2):
-            at = 24 + 2 * member + half
+            at = 28 + 2 * member + half
             told[at : at + 1, 0 : places // 2] = row[:, half * places // 2 : (half + 1) * places // 2]
 
 
-def share_kernel(rows, weights, heard, shares):
+def last_kernel(vectors, gathered, so_far, weights, told, scores, notes):
+    features = vectors.shape[1]
+    points = gathered[:, 0:features]
+    notes[...] = so_far[...]
+    across = slice(0, vectors.shape[0])
+    top, total = quarter_weights(points, -sharpness * row_squares(points), vectors, scores, weights, across)
+    note_sums(notes, TEAM - 1, top, total)
+    told[...] = notes[...].astype(bf16)
+
+
+def share_kernel(rows, weights, weights2, heard, shares):
     me = lax.axis_index(FOUR)
+    words = [heard[me ^ t].astype(f32) for t in range(TEAM)]
     factors = []
     for side in range(TEAM):
-        tops = [heard[me ^ t, t ^ side : (t ^ side) + 1, 0:rows] for t in range(TEAM)]
-        totals = [heard[me ^ t, 4 + (t ^ side) : 5 + (t ^ side), 0:rows] for t in range(TEAM)]
+        at = [t ^ side for t in range(TEAM)]
+        tops = [words[t][at[t] : at[t] + 1, 0:rows] for t in range(TEAM)]
+        totals = [words[t][4 + at[t] : 5 + at[t], 0:rows] + words[t][8 + at[t] : 9 + at[t], 0:rows] for t in range(TEAM)]
         highest = functools.reduce(jnp.maximum, tops)
         total = sum(n * jnp.exp(top - highest) for n, top in zip(totals, tops, strict=True))
         factors.append(jnp.exp(tops[0] - highest) / total)
-    factor = jnp.concatenate(factors, axis=1)
     for b in range(Y // 2):
-        probs = weights[2 * b : 2 * b + 2].reshape(128, TEAM * rows) * factor
-        lanes = probs[:, 0:128]
-        for j in range(1, TEAM * rows // 128):
-            lanes = lanes + probs[:, j * 128 : (j + 1) * 128]
+        lanes = jnp.zeros((128, 128), f32)
+        for side, factor in enumerate(factors):
+            source, first = (weights, side * rows) if side < TEAM - 1 else (weights2, 0)
+            probs = source[2 * b : 2 * b + 2, :, :, first : first + rows].reshape(128, rows) * factor
+            for j in range(rows // 128):
+                lanes = lanes + probs[:, j * 128 : (j + 1) * 128]
         share = jnp.sum(jnp.transpose(lanes), axis=0, keepdims=True)
         shares[:, b : b + 1, :] = jnp.broadcast_to(share[None], (shares.shape[0], 1, 128))
 
@@ -220,9 +241,10 @@
     rows, features = got.shape
     fine = book.shape[0] // SLOTS
     me = lax.axis_index(FOUR)
-    centres = sum(heard[me ^ t, 8 + t * SLOTS : 8 + (t + 1) * SLOTS, :] for t in range(TEAM))
+    words = [heard[me ^ t].astype(f32) for t in range(TEAM)]
+    centres = sum(words[t][12 + t * SLOTS : 12 + (t + 1) * SLOTS, :] for t in range(TEAM))
     centres = jnp.concatenate([centres, jnp.zeros(centres.shape, f32)], axis=0).astype(bf16)
-    halves = [heard[me, 24 + h : 25 + h, 0 : rows // 2] + heard[me ^ 1, 26 + h : 27 + h, 0 : rows // 2] for h in range(2)]
+    halves = [words[0][28 + h : 29 + h, 0 : rows // 2] + words[1][30 + h : 31 + h, 0 : rows // 2] for h in range(2)]
     local = jnp.concatenate(halves, axis=1) - 1.0
     squares = [
         jnp.transpose(jnp.broadcast_to(book_squares[:, s * fine : (s + 1) * fine], (128, fine)))[:, 0:1] for s in range(SLOTS)
@@ -267,9 +289,10 @@
     owners, cap = spread.shape
     total = jnp.sum(jnp.sum(shares[...].reshape(Z // PAIR, PAIR, X, 4, 128), axis=2), axis=0).reshape(X, 2, 128)
     quarter = jnp.sum(jnp.where(iota(total.shape, 0) == lax.axis_index("x"), total, 0.0), axis=0)
-    line = jnp.concatenate([spread[...], jnp.zeros((owners, 128 - cap), f32)], axis=1)
-    out[:, 0:2, :] = jnp.broadcast_to(quarter[None], (owners, 2, 128))
-    out[:, 2:4, :] = jnp.broadcast_to(line[:, None, :], (owners, 2, 128))
+    upper = spread[...].astype(bf16).astype(f32)
+    line = jnp.concatenate([upper, spread[...] - upper, jnp.zeros((owners, 128 - 2 * cap), f32)], axis=1)
+    top = jnp.broadcast_to(quarter[None], (owners, 2, 128))
+    out[...] = jnp.concatenate([top, jnp.broadcast_to(line[:, None, :], (owners, 2, 128))], axis=1).astype(bf16)
 
 
 def finish_kernel(scale, got, place, distortion, share):
@@ -279,8 +302,9 @@
     position = place[...]
     at_owner = (iota((owners, rows), 0) == position // cap).astype(f32)
     at_rank = iota((cap, rows), 0) == position % cap
-    whole = got[...]
-    returned = whole[:, 2, :][:, 0:cap]
+    whole = got[...].astype(f32)
+    line = whole[:, 2, :]
+    returned = line[:, 0:cap] + line[:, cap : 2 * cap]
     across = dot(returned, at_owner, 0, 0, lax.Precision.HIGHEST)
     distortion[...] = jnp.sum(jnp.where(at_rank, across, 0.0), axis=0, keepdims=True)
     quarters = jnp.sum(whole[:, 0:2, :].reshape(Y, X * CORES, 2, 128), axis=0) * scale
@@ -383,17 +407,31 @@
     vectors4 = from_partner(vectors3)
     weights, told = call(
         functools.partial(coarse_kernel, cap),
-        (shaped((Y, X, part, TEAM * rows), f32), shaped((32, features), f32)),
-        [],
-        [vectors, vectors2, vectors3, vectors4, wanted, gathered],
+        (shaped((Y, X, part, (TEAM - 1) * rows), f32), shaped((32, features), f32)),
+        [],
+        [vectors, vectors2, vectors3, wanted, gathered],
         "coarse_part",
         2 * 10**9,
         mib=28,
-        scratch=[pltpu.VMEM((Y, X, part, TEAM * rows), f32)],
+        scratch=[pltpu.VMEM((Y, X, part, (TEAM - 1) * rows), f32)],
+    )
+    weights2, told = call(
+        last_kernel,
+        (shaped((Y, X, part, rows), f32), shaped((32, features), bf16)),
+        [],
+        [vectors4, gathered, told],
+        "last_part",
+        10**9,
+        scratch=[pltpu.VMEM((Y, X, part, rows), f32), pltpu.VMEM((32, features), f32)],
     )
     heard = lax.all_gather(told, FOUR, axis=0)
     shares = call(
-        functools.partial(share_kernel, rows), shaped((Z * X, 4, 128), f32), [], [weights, heard], "share", 10**9
+        functools.partial(share_kernel, rows),
+        shaped((Z * X, 4, 128), f32),
+        [],
+        [weights, weights2, heard],
+        "share",
+        10**9,
     )
     shares = exchange(shares, ("zh", "zl", "x"))
 
@@ -410,7 +448,7 @@
             pltpu.VMEM((owners * cap, features), bf16),
         ],
     )
-    answer = call(answer_kernel, shaped((owners, 4, 128), f32), [], [spread, shares], "answer", 10**6)
+    answer = call(answer_kernel, shaped((owners, 4, 128), bf16), [], [spread, shares], "answer", 10**6)
     back = exchange(answer, PLANE)
     distortion, coarse_share = call(
         functools.partial(finish_kernel, owned / rows),

time: 112 us -> 109 us (0.973)
  blocking collectives: 45.3 us -> 40.5 us
  waiting for transfers between devices: 10.7 us -> 12.9 us
  local copies, waits for them, and re-layouts: 2.3 us -> 0.9 us
    all_to_all x3, waiting for transfers between devices: 8.81 us -> 12.9 us  [exchange(): return lax.all_to_all(x, axes, 0, 0, tiled=True)]
    all_to_all x1, blocking collectives: 20.6 us -> 16.8 us  [exchange(): return lax.all_to_all(x, axes, 0, 0, tiled=True)]
    ppermute x2, waiting for transfers between devices: 1.89 us -> 0.01 us  [from_partner(): return lax.ppermute(x, 'c', [(0, 1), (1, 0)])]
    unnamed x14, local copies, waits for them, and re-layouts: 2.3 us -> 0.9 us
    pallas_call x7 -> x8, Pallas kernels: 16.9 us -> 17.2 us  [call(): pl.pallas_call(body, out_shape=out_shape, in_specs=[SMEM] * len(scalars)...]
  transfers between devices with their start and end apart: 6 -> 6, of which waited for: 4 -> 3; matrix products, arithmetic and copies ran while one was open for 0% -> 0% of each run, Pallas kernels for 14% -> 15%
where the time goes in v4:
time: 109 us; the launch traced here: 108 us
  blocking collectives  40.5 us (37%)
  starting transfers between devices  35.8 us (33%)
  Pallas kernels  17.2 us (16%)
  waiting for transfers between devices  12.9 us (12%)
    all_to_all x3, starting transfers between devices, exchange(): return lax.all_to_all(x, axes, 0, 0, tiled=True)  19.9 us
    all_gather x1, blocking collectives, on_device(): gathered = lax.all_gather(first, 'x', axis=0, tiled=True)  18.1 us
    pallas_call x8, Pallas kernels, call(): pl.pallas_call(body, out_shape=out_shape, in_specs=[SMEM] * len(scalars)...  17.2 us
    all_to_all x1, blocking collectives, exchange(): return lax.all_to_all(x, axes, 0, 0, tiled=True)  16.8 us
    ppermute x2, starting transfers between devices, from_partner(): return lax.ppermute(x, 'c', [(0, 1), (1, 0)])  13 us
    all_to_all x3, waiting for transfers between devices, exchange(): return lax.all_to_all(x, axes, 0, 0, tiled=True)  12.9 us
    all_gather x1, blocking collectives, on_device(): heard = lax.all_gather(told, FOUR, axis=0)  5.51 us
    ppermute x1, starting transfers between devices, from_neighbour(): return lax.ppermute(x, 'zl', [(0, 1), (1, 0)])  2.88 us
  transfers between devices with their start and end apart: 6, of which 3 were waited for; matrix products, arithmetic and copies ran while one was open for 0% of the time, Pallas kernels for 15%

profile of v4, /device:TPU:1, one launch (start us, length us, event | category | flops | bytes accessed | tf_op | source)
XLA Modules:
  0.0 108.2 jit_solution(5700128561364037639)
XLA Ops:
  0.6 8.8 %collective-permute-start = (bf16[512,768]{1,0:T(8,128)(2,1)}, bf16[512,768]{1,0:T(8,128)(2,1)S(1)}, u32[]{:S(2)}, u32[]{:S(2)}) collective-permute-start(bf16[512,768]{1,0:T(8,128)(2,1)} %vectors.3), channel_id=1, source_target_pairs={{0,1},{1,0},{2,3},{3,2},{4,5},{5,4},{6,7},{7,6},{8,9},{9,8},{10,11... | collective-permute-start | bytes 2359304 | tf_op jit(solution)/shard_map/ppermute | solution.py:344
  9.4 1.5 %pack.1 = bf16[8,16,896]{2,1,0:T(8,128)(2,1)} custom-call(bf16[32,768]{1,0:T(8,128)(2,1)} %coarse.1, s32[4,128]{1,0:T(4,128)} %bitcast.16), custom_call_target="tpu_custom_call" | custom-call | flops 1000000 | bytes 1048576 | tf_op jit(solution)/shard_map/pack/pallas_call | solution.py:30
  11.0 3.4 %all-to-all-start.1 = ((bf16[8,16,896]{2,1,0:T(8,128)(2,1)}), bf16[8,16,896]{2,1,0:T(8,128)(2,1)S(1)}, u32[]{:S(2)}, u32[]{:S(2)}) async-start(bf16[8,16,896]{2,1,0:T(8,128)(2,1)} %pack.1), calls=%async_computation.1 | async-start | bytes 458752 | tf_op jit(solution)/shard_map/all_to_all | solution.py:336
  14.4 0.0 collective-permute-done.early.vectors2
  14.4 0.0 copy-start.2
  14.4 0.9 copy-done.2
  15.3 3.6 %route.1 = (bf16[64,16,768]{2,1,0:T(8,128)(2,1)}, s32[1,512]{1,0:T(1,128)}, f32[1,1024]{1,0:T(1,128)}, f32[16,128]{1,0:T(8,128)}) custom-call(s32[1,512]{1,0:T(1,128)} %bitcast.17, s32[16,128]{1,0:T(8,128)} %bitcast.18, bf16[512,768]{1,0:T(8,128)(2,1)} %vectors.3, bf16[1024,768]{1,0:T(8,128)(2,1)} %bitcast.13, bf16[512,768]{1,0:T(8,128)(2,1)} %copy-done.2), custom_call_target="tpu_custom_call" | custom-call | flops 1000000000 | bytes 1048576 | tf_op jit(solution)/shard_map/route/pallas_call | solution.py:30
  18.9 7.1 %all-to-all-done.1 = bf16[8,16,896]{2,1,0:T(8,128)(2,1)S(1)} async-done(((bf16[8,16,896]{2,1,0:T(8,128)(2,1)}), bf16[8,16,896]{2,1,0:T(8,128)(2,1)S(1)}, u32[]{:S(2)}, u32[]{:S(2)}) %all-to-all-start.1) | async-done | bytes 229408 | tf_op jit(solution)/shard_map/all_to_all | solution.py:336
  26.0 0.0 copy-start.1
  26.0 4.7 %all-to-all-start = ((bf16[64,16,768]{2,1,0:T(8,128)(2,1)}), bf16[64,16,768]{2,1,0:T(8,128)(2,1)S(1)}, u32[]{:S(2)}, u32[]{:S(2)}) async-start(bf16[64,16,768]{2,1,0:T(8,128)(2,1)} %get-tuple-element.15), calls=%async_computation | async-start | bytes 3145728 | tf_op jit(solution)/shard_map/all_to_all | solution.py:336
  30.7 0.0 copy-done.1
  30.7 2.9 %collective-permute-start.1 = (bf16[512,768]{1,0:T(8,128)(2,1)S(1)}, bf16[512,768]{1,0:T(8,128)(2,1)S(1)}, u32[]{:S(2)}, u32[]{:S(2)}) collective-permute-start(bf16[512,768]{1,0:T(8,128)(2,1)S(1)} %copy-done.1), channel_id=1, source_target_pairs={{0,64},{64,0},{1,65},{65,1},{2,66},{66,2},{3,67},{67,3},{4,68},{68... | collective-permute-start | bytes 2359304 | tf_op jit(solution)/shard_map/ppermute | solution.py:340
  33.6 0.0 copy-start.3
  33.6 0.0 copy-start.4
  33.6 18.1 %all_gather.9.refs_1_.gathered = bf16[512,896]{1,0:T(8,128)(2,1)S(1)} all-gather(bf16[128,896]{1,0:T(8,128)(2,1)S(1)} %bitcast.15), channel_id=1, replica_groups=mesh['zh'=4,'zl'=2,'y'=8,'x'=4,'c'=2] {'x'}, dimensions={0}, use_global_device_ids=true | all-gather | bytes 1146880 | tf_op jit(solution)/shard_map/all_gather | solution.py:405
  51.7 0.0 collective-permute-done.1.refs_0_
  51.7 4.2 %collective-permute-start.2 = (bf16[512,768]{1,0:T(8,128)(2,1)S(1)}, bf16[512,768]{1,0:T(8,128)(2,1)S(1)}, u32[]{:S(2)}, u32[]{:S(2)}) collective-permute-start(bf16[512,768]{1,0:T(8,128)(2,1)S(1)} %after.1.vectors3), channel_id=1, source_target_pairs={{0,1},{1,0},{2,3},{3,2},{4,5},{5,4},{6,7},{7,6},{8,9},{9,8},{10,11... | collective-permute-start | bytes 2359304 | tf_op jit(solution)/shard_map/ppermute | solution.py:344
  56.0 0.0 copy-done.3
  56.0 0.0 copy-done.4
  56.0 3.4 %coarse_part.1 = (f32[8,4,16,1536]{3,2,1,0:T(8,128)S(1)}, f32[32,768]{1,0:T(8,128)S(1)}) custom-call(bf16[512,768]{1,0:T(8,128)(2,1)S(1)} %copy-done.1, bf16[512,768]{1,0:T(8,128)(2,1)S(1)} %copy-done.3, bf16[512,768]{1,0:T(8,128)(2,1)S(1)} %after.1.vectors3, f32[16,128]{1,0:T(8,128)S(1)} %copy-done.4, bf16[512,896]{1,0:T(8,128)(2,1)S(1)} %all_gather.9.refs_1_.gathered), custom_call_target="tpu_custom_call" | custom-call | flops 2000000000 | bytes 1048576 | tf_op jit(solution)/shard_map/coarse_part/pallas_call | solution.py:30
  59.4 0.0 collective-permute-done.2.vectors
  59.4 0.9 last_part.1
  60.3 5.5 %all-gather = bf16[128,768]{1,0:T(8,128)(2,1)S(1)} all-gather(bf16[32,768]{1,0:T(8,128)(2,1)S(1)} %get-tuple-element.18), channel_id=2, replica_groups=mesh['zh'=4,'zl'=2,'y'=8,'x'=4,'c'=2] {'zl','c'}, dimensions={0}, use_global_device_ids=true | all-gather | bytes 245760 | tf_op jit(solution)/shard_map/all_gather | solution.py:427
  65.8 0.0 copy-start
  65.8 0.0 copy-start.6
  65.8 1.1 share.1
  66.9 2.9 %all-to-all-done = bf16[64,16,768]{2,1,0:T(8,128)(2,1)S(1)} async-done(((bf16[64,16,768]{2,1,0:T(8,128)(2,1)}), bf16[64,16,768]{2,1,0:T(8,128)(2,1)S(1)}, u32[]{:S(2)}, u32[]{:S(2)}) %all-to-all-start) | async-done | bytes 1572896 | tf_op jit(solution)/shard_map/all_to_all | solution.py:336
  69.8 11.8 %all-to-all-start.2 = ((f32[32,4,128]{2,1,0:T(4,128)}), f32[32,4,128]{2,1,0:T(4,128)S(1)}, u32[]{:S(2)}, u32[]{:S(2)}) async-start(f32[32,4,128]{2,1,0:T(4,128)} %share.1), calls=%async_computation.2 | async-start | bytes 131072 | tf_op jit(solution)/shard_map/all_to_all | solution.py:336
  81.7 0.0 copy-done
  81.7 0.0 copy-done.6
  81.7 0.0 copy-start.5
  81.7 5.7 %fine_part.1 = (f32[64,16]{1,0:T(8,128)S(1)}, bf16[1024,768]{1,0:T(8,128)(2,1)}) custom-call(bf16[1024,768]{1,0:T(8,128)(2,1)S(1)} %bitcast.10, bf16[4,32,768]{2,1,0:T(8,128)(2,1)S(1)} %bitcast.12, bf16[1024,768]{1,0:T(8,128)(2,1)S(1)} %bitcast.14, f32[1,1024]{1,0:T(1,128)S(1)} %copy-done.6), custom_call_target="tpu_custom_call" | custom-call | flops 3000000000 | bytes 1048576 | tf_op jit(solution)/shard_map/fine_part/pallas_call | solution.py:30
  87.4 2.9 %all-to-all-done.2.shares = f32[32,4,128]{2,1,0:T(4,128)S(1)} async-done(((f32[32,4,128]{2,1,0:T(4,128)}), f32[32,4,128]{2,1,0:T(4,128)S(1)}, u32[]{:S(2)}, u32[]{:S(2)}) %all-to-all-start.2) | async-done | bytes 65568 | tf_op jit(solution)/shard_map/all_to_all | solution.py:336
  90.3 0.1 answer.1
  90.4 16.8 %all_to_all.20.got = bf16[64,4,128]{2,1,0:T(4,128)(2,1)S(1)} all-to-all(bf16[64,4,128]{2,1,0:T(4,128)(2,1)S(1)} %answer.1), channel_id=1, replica_groups=mesh['zh'=4,'zl'=2,'y'=8,'x'=4,'c'=2] {'y','x','c'}, dimensions={0} | all-to-all | bytes 131072 | tf_op jit(solution)/shard_map/all_to_all | solution.py:336
  107.2 0.0 copy-done.5
  107.3 0.9 finish.1
  (1 shorter events, 0.0 us)
Async XLA Ops:
  0.6 13.8 %collective-permute-start = (bf16[512,768]{1,0:T(8,128)(2,1)}, bf16[512,768]{1,0:T(8,128)(2,1)S(1)}, u32[]{:S(2)}, u32[]{:S(2)}) collective-permute-start(bf16[512,768]{1,0:T(8,128)(2,1)} %vectors.3), channel_id=1, source_target_pairs={{0,1},{1,0},{2,3},{3,2},{4,5},{5,4},{6,7},{7,6},{8,9},{9,8},{10,11... | collective-permute-start | bytes 2359304 | tf_op jit(solution)/shard_map/ppermute | solution.py:344
  11.0 15.0 %all-to-all-start.1 = ((bf16[8,16,896]{2,1,0:T(8,128)(2,1)}), bf16[8,16,896]{2,1,0:T(8,128)(2,1)S(1)}, u32[]{:S(2)}, u32[]{:S(2)}) async-start(bf16[8,16,896]{2,1,0:T(8,128)(2,1)} %pack.1), calls=%async_computation.1 | async-start | bytes 458752 | tf_op jit(solution)/shard_map/all_to_all | solution.py:336
  14.4 0.9 copy-start.2
  26.0 4.7 %copy-start.1 = (bf16[512,768]{1,0:T(8,128)(2,1)S(1)}, bf16[512,768]{1,0:T(8,128)(2,1)}, u32[]{:S(2)}) copy-start(bf16[512,768]{1,0:T(8,128)(2,1)} %vectors.3) | copy-start | bytes 2359300
  26.0 43.8 %all-to-all-start = ((bf16[64,16,768]{2,1,0:T(8,128)(2,1)}), bf16[64,16,768]{2,1,0:T(8,128)(2,1)S(1)}, u32[]{:S(2)}, u32[]{:S(2)}) async-start(bf16[64,16,768]{2,1,0:T(8,128)(2,1)} %get-tuple-element.15), calls=%async_computation | async-start | bytes 3145728 | tf_op jit(solution)/shard_map/all_to_all | solution.py:336
  30.7 21.0 %collective-permute-start.1 = (bf16[512,768]{1,0:T(8,128)(2,1)S(1)}, bf16[512,768]{1,0:T(8,128)(2,1)S(1)}, u32[]{:S(2)}, u32[]{:S(2)}) collective-permute-start(bf16[512,768]{1,0:T(8,128)(2,1)S(1)} %copy-done.1), channel_id=1, source_target_pairs={{0,64},{64,0},{1,65},{65,1},{2,66},{66,2},{3,67},{67,3},{4,68},{68... | collective-permute-start | bytes 2359304 | tf_op jit(solution)/shard_map/ppermute | solution.py:340
  33.6 22.4 %copy-start.3 = (bf16[512,768]{1,0:T(8,128)(2,1)S(1)}, bf16[512,768]{1,0:T(8,128)(2,1)}, u32[]{:S(2)}) copy-start(bf16[512,768]{1,0:T(8,128)(2,1)} %copy-done.2) | copy-start | bytes 2359300
  33.6 22.4 %copy-start.4 = (f32[16,128]{1,0:T(8,128)S(1)}, f32[16,128]{1,0:T(8,128)}, u32[]{:S(2)}) copy-start(f32[16,128]{1,0:T(8,128)} %get-tuple-element.16.wanted) | copy-start | bytes 24580
  51.7 7.6 %collective-permute-start.2 = (bf16[512,768]{1,0:T(8,128)(2,1)S(1)}, bf16[512,768]{1,0:T(8,128)(2,1)S(1)}, u32[]{:S(2)}, u32[]{:S(2)}) collective-permute-start(bf16[512,768]{1,0:T(8,128)(2,1)S(1)} %after.1.vectors3), channel_id=1, source_target_pairs={{0,1},{1,0},{2,3},{3,2},{4,5},{5,4},{6,7},{7,6},{8,9},{9,8},{10,11... | collective-permute-start | bytes 2359304 | tf_op jit(solution)/shard_map/ppermute | solution.py:344
  65.8 15.8 %copy-start = (bf16[4,256,768]{2,1,0:T(8,128)(2,1)S(1)}, bf16[4,256,768]{2,1,0:T(8,128)(2,1)}, u32[]{:S(2)}) copy-start(bf16[4,256,768]{2,1,0:T(8,128)(2,1)} %param.9) | copy-start | bytes 4718596
  65.8 15.8 %copy-start.6 = (f32[1,1024]{1,0:T(1,128)S(1)}, f32[1,1024]{1,0:T(1,128)}, u32[]{:S(2)}) copy-start(f32[1,1024]{1,0:T(1,128)} %get-tuple-element.19.book_squares) | copy-start | bytes 12292
  69.8 20.5 %all-to-all-start.2 = ((f32[32,4,128]{2,1,0:T(4,128)}), f32[32,4,128]{2,1,0:T(4,128)S(1)}, u32[]{:S(2)}, u32[]{:S(2)}) async-start(f32[32,4,128]{2,1,0:T(4,128)} %share.1), calls=%async_computation.2 | async-start | bytes 131072 | tf_op jit(solution)/shard_map/all_to_all | solution.py:336
  81.7 25.6 %copy-start.5 = (s32[1,512]{1,0:T(1,128)S(1)}, s32[1,512]{1,0:T(1,128)}, u32[]{:S(2)}) copy-start(s32[1,512]{1,0:T(1,128)} %get-tuple-element.23.place) | copy-start | bytes 6148

commit v5 on v4

--- a/solution.py
+++ b/solution.py
@@ -24,8 +24,8 @@
 FAR = pl.BlockSpec(memory_space=pltpu.HBM)
 
 
-def call(body, out_shape, scalars, arrays, name, flops, mib=16, scratch=(), far_in=(), far_out=(), loose=()):
-    specs = [ANY if i in loose else FAR if i in far_in else VMEM for i in range(len(arrays))]
+def call(body, out_shape, scalars, arrays, name, flops, mib=16, scratch=(), far_in=(), far_out=()):
+    specs = [FAR if i in far_in else VMEM for i in range(len(arrays))]
     many = isinstance(out_shape, tuple)
     return pl.pallas_call(
         body,
@@ -47,10 +47,8 @@
     return lax.broadcasted_iota(i32, shape, axis)
 
 
-def dot(a, b, ca, cb, precision=None):
-    return lax.dot_general(
-        a, b, (((ca,), (cb,)), ((), ())), preferred_element_type=f32, precision=precision
-    )
+def dot(a, b, ca, cb):
+    return lax.dot_general(a, b, (((ca,), (cb,)), ((), ())), preferred_element_type=f32)
 
 
 def as_row(column):
@@ -84,7 +82,7 @@
 
 
 def route_kernel(
-    owned, cell, table, vectors, book, early, send, place, book_squares, wanted,
+    owned, cell, table, vectors, book, send, place, book_squares, wanted,
     cell_in, table_in, rows_in, book_in, rows_out, in_sem, out_sem,
 ):
     owners, cap, _ = send.shape
@@ -162,7 +160,7 @@
     told[8 + side : 9 + side, 0:rows] = total - upper
 
 
-def coarse_kernel(cap, vectors, vectors2, vectors3, wanted, gathered, weights, told, scores):
+def coarse_kernel(cap, vectors, vectors3, wanted, gathered, weights, told, scores):
     parity, core = lax.axis_index("zl"), lax.axis_index("c")
     rows, features = vectors.shape
     part = scores.shape[2]
@@ -171,8 +169,8 @@
     points = gathered[:, 0:features]
     squares = -sharpness * row_squares(points)
     told[...] = jnp.zeros(told.shape, f32)
-    for side, against in enumerate((vectors, vectors2, vectors3)):
-        across = slice(side * rows, (side + 1) * rows)
+    for place, (side, against) in enumerate(((0, vectors), (2, vectors3))):
+        across = slice(place * rows, (place + 1) * rows)
         note_sums(told, side, *quarter_weights(points, squares, against, scores, weights, across))
     line = iota((TEAM * SLOTS, X * slab), 1)
     group = line // part % Y * X + line // slab
@@ -202,13 +200,14 @@
             told[at : at + 1, 0 : places // 2] = row[:, half * places // 2 : (half + 1) * places // 2]
 
 
-def last_kernel(vectors, gathered, so_far, weights, told, scores, notes):
-    features = vectors.shape[1]
+def last_kernel(vectors2, vectors4, gathered, so_far, weights, told, scores, notes):
+    rows, features = vectors2.shape
     points = gathered[:, 0:features]
+    squares = -sharpness * row_squares(points)
     notes[...] = so_far[...]
-    across = slice(0, vectors.shape[0])
-    top, total = quarter_weights(points, -sharpness * row_squares(points), vectors, scores, weights, across)
-    note_sums(notes, TEAM - 1, top, total)
+    for place, (side, against) in enumerate(((1, vectors2), (3, vectors4))):
+        across = slice(place * rows, (place + 1) * rows)
+        note_sums(notes, side, *quarter_weights(points, squares, against, scores, weights, across))
     told[...] = notes[...].astype(bf16)
 
 
@@ -226,7 +225,7 @@
     for b in range(Y // 2):
         lanes = jnp.zeros((128, 128), f32)
         for side, factor in enumerate(factors):
-            source, first = (weights, side * rows) if side < TEAM - 1 else (weights2, 0)
+            source, first = (weights2 if side % CORES else weights), side // CORES * rows
             probs = source[2 * b : 2 * b + 2, :, :, first : first + rows].reshape(128, rows) * factor
             for j in range(rows // 128):
                 lanes = lanes + probs[:, j * 128 : (j + 1) * 128]
@@ -237,7 +236,7 @@
 def fine_kernel(
     got, heard, book, book_squares, spread, out, weights, residual
 ):
-    owners, cap = spread.shape
+    owners, cap = spread.shape[0], spread.shape[1] // 2
     rows, features = got.shape
     fine = book.shape[0] // SLOTS
     me = lax.axis_index(FOUR)
@@ -276,9 +275,11 @@
             weights[s * fine : (s + 1) * fine, at] = only.astype(bf16)
             masses[s] = masses[s] + jnp.sum(only, axis=1, keepdims=True)
     row = jnp.concatenate(parts, axis=1)
-    places = (iota((cap, rows), 1) % cap == iota((cap, rows), 0)).astype(f32)
+    places = (iota((cap, rows), 1) % cap == iota((cap, rows), 0)).astype(bf16)
     at_owner = iota((owners, rows), 1) // cap == iota((owners, rows), 0)
-    spread[...] = dot(jnp.where(at_owner, row, 0.0), places, 1, 1, lax.Precision.HIGHEST)
+    upper = row.astype(bf16).astype(f32)
+    for part, values in enumerate((upper, row - upper)):
+        spread[:, part * cap : (part + 1) * cap] = dot(jnp.where(at_owner, values, 0.0).astype(bf16), places, 1, 1)
     for s in range(SLOTS):
         at = slice(s * fine, (s + 1) * fine)
         total = dot(weights[at], residual[...], 1, 0)
@@ -286,11 +287,10 @@
 
 
 def answer_kernel(spread, shares, out):
-    owners, cap = spread.shape
+    owners, width = spread.shape
     total = jnp.sum(jnp.sum(shares[...].reshape(Z // PAIR, PAIR, X, 4, 128), axis=2), axis=0).reshape(X, 2, 128)
     quarter = jnp.sum(jnp.where(iota(total.shape, 0) == lax.axis_index("x"), total, 0.0), axis=0)
-    upper = spread[...].astype(bf16).astype(f32)
-    line = jnp.concatenate([upper, spread[...] - upper, jnp.zeros((owners, 128 - 2 * cap), f32)], axis=1)
+    line = jnp.concatenate([spread[...], jnp.zeros((owners, 128 - width), f32)], axis=1)
     top = jnp.broadcast_to(quarter[None], (owners, 2, 128))
     out[...] = jnp.concatenate([top, jnp.broadcast_to(line[:, None, :], (owners, 2, 128))], axis=1).astype(bf16)
 
@@ -300,12 +300,11 @@
     rows = place.shape[1]
     cap = 2 * rows // owners
     position = place[...]
-    at_owner = (iota((owners, rows), 0) == position // cap).astype(f32)
+    at_owner = (iota((owners, rows), 0) == position // cap).astype(bf16)
     at_rank = iota((cap, rows), 0) == position % cap
     whole = got[...].astype(f32)
-    line = whole[:, 2, :]
-    returned = line[:, 0:cap] + line[:, cap : 2 * cap]
-    across = dot(returned, at_owner, 0, 0, lax.Precision.HIGHEST)
+    line = whole[:, 2, :].astype(bf16)
+    across = dot(line[:, 0:cap], at_owner, 0, 0) + dot(line[:, cap : 2 * cap], at_owner, 0, 0)
     distortion[...] = jnp.sum(jnp.where(at_rank, across, 0.0), axis=0, keepdims=True)
     quarters = jnp.sum(whole[:, 0:2, :].reshape(Y, X * CORES, 2, 128), axis=0) * scale
     halves = [jnp.concatenate([quarters[x * CORES + c] for x in range(X)], axis=0) for c in range(CORES)]
@@ -373,7 +372,6 @@
         ],
     )
     first = exchange(packed, ("y",)).reshape(Y * part, features + 128)
-    vectors2 = from_partner(vectors)
     send, place, book_squares, wanted = call(
         functools.partial(route_kernel, owned),
         (
@@ -383,13 +381,12 @@
             shaped((TEAM * owned, 128), f32),
         ),
         [],
-        [cell_of.reshape(1, rows), table, vectors, book, vectors2],
+        [cell_of.reshape(1, rows), table, vectors, book],
         "route",
         10**9,
         mib=60,
         far_in=(0, 1, 2, 3),
         far_out=(0,),
-        loose=(4,),
         scratch=[
             pltpu.VMEM((1, rows), i32),
             pltpu.VMEM(table.shape, i32),
@@ -404,25 +401,26 @@
 
     gathered = lax.all_gather(first, "x", axis=0, tiled=True)
     vectors3 = after(from_neighbour(vectors), gathered)
-    vectors4 = from_partner(vectors3)
+    vectors2, vectors4 = from_partner(vectors), from_partner(vectors3)
     weights, told = call(
         functools.partial(coarse_kernel, cap),
-        (shaped((Y, X, part, (TEAM - 1) * rows), f32), shaped((32, features), f32)),
-        [],
-        [vectors, vectors2, vectors3, wanted, gathered],
+        (shaped((Y, X, part, PAIR * rows), f32), shaped((32, features), f32)),
+        [],
+        [vectors, vectors3, wanted, gathered],
         "coarse_part",
         2 * 10**9,
         mib=28,
-        scratch=[pltpu.VMEM((Y, X, part, (TEAM - 1) * rows), f32)],
+        scratch=[pltpu.VMEM((Y, X, part, PAIR * rows), f32)],
     )
     weights2, told = call(
         last_kernel,
-        (shaped((Y, X, part, rows), f32), shaped((32, features), bf16)),
-        [],
-        [vectors4, gathered, told],
+        (shaped((Y, X, part, PAIR * rows), f32), shaped((32, features), bf16)),
+        [],
+        [vectors2, vectors4, gathered, told],
         "last_part",
         10**9,
-        scratch=[pltpu.VMEM((Y, X, part, rows), f32), pltpu.VMEM((32, features), f32)],
+        mib=28,
+        scratch=[pltpu.VMEM((Y, X, part, PAIR * rows), f32), pltpu.VMEM((32, features), f32)],
     )
     heard = lax.all_gather(told, FOUR, axis=0)
     shares = call(
@@ -437,7 +435,7 @@
 
     spread, fine_next = call(
         fine_kernel,
-        (shaped((owners, cap), f32), shaped(book.shape, bf16)),
+        (shaped((owners, 2 * cap), f32), shaped(book.shape, bf16)),
         [],
         [got, heard, book, book_squares],
         "fine_part",

time: 109 us -> 108 us (level)
  waiting for transfers between devices: 12.9 us -> 8.44 us
  starting transfers between devices: 35.8 us -> 38.9 us
  blocking collectives: 40.5 us -> 42.2 us
    all_to_all x3, starting transfers between devices: 19.9 us -> 28.9 us  [exchange(): return lax.all_to_all(x, axes, 0, 0, tiled=True)]
    ppermute x2, starting transfers between devices: 13 us -> 6 us  [from_partner(): return lax.ppermute(x, 'c', [(0, 1), (1, 0)])]
    all_to_all x3, waiting for transfers between devices: 12.9 us -> 8.43 us  [exchange(): return lax.all_to_all(x, axes, 0, 0, tiled=True)]
    all_to_all x1, blocking collectives: 16.8 us -> 18.8 us  [exchange(): return lax.all_to_all(x, axes, 0, 0, tiled=True)]
    ppermute x1, starting transfers between devices: 2.88 us -> 4 us  [from_neighbour(): return lax.ppermute(x, 'zl', [(0, 1), (1, 0)])]
  transfers between devices with their start and end apart: 6 -> 6, of which waited for: 3 -> 3; matrix products, arithmetic and copies ran while one was open for 0% -> 0% of each run, Pallas kernels for 15% -> 14%
where the time goes in v5:
time: 108 us; the launch traced here: 107 us
  blocking collectives  42.2 us (39%)
  starting transfers between devices  38.9 us (36%)
  Pallas kernels  17.2 us (16%)
  waiting for transfers between devices  8.44 us (8%)
    all_to_all x3, starting transfers between devices, exchange(): return lax.all_to_all(x, axes, 0, 0, tiled=True)  28.9 us
    all_to_all x1, blocking collectives, exchange(): return lax.all_to_all(x, axes, 0, 0, tiled=True)  18.8 us
    all_gather x1, blocking collectives, on_device(): gathered = lax.all_gather(first, 'x', axis=0, tiled=True)  17.9 us
    pallas_call x8, Pallas kernels, call(): pl.pallas_call(body, out_shape=out_shape, in_specs=[SMEM] * len(scalars)...  17.2 us
    all_to_all x3, waiting for transfers between devices, exchange(): return lax.all_to_all(x, axes, 0, 0, tiled=True)  8.43 us
    ppermute x2, starting transfers between devices, from_partner(): return lax.ppermute(x, 'c', [(0, 1), (1, 0)])  6 us
    all_gather x1, blocking collectives, on_device(): heard = lax.all_gather(told, FOUR, axis=0)  5.51 us
    ppermute x1, starting transfers between devices, from_neighbour(): return lax.ppermute(x, 'zl', [(0, 1), (1, 0)])  4 us
  transfers between devices with their start and end apart: 6, of which 3 were waited for; matrix products, arithmetic and copies ran while one was open for 0% of the time, Pallas kernels for 14%

profile of v5, /device:TPU:1, one launch (start us, length us, event | category | flops | bytes accessed | tf_op | source)
XLA Modules:
  0.0 107.5 jit_solution(15280547325061411823)
XLA Ops:
  0.6 1.5 %pack.1 = bf16[8,16,896]{2,1,0:T(8,128)(2,1)} custom-call(bf16[32,768]{1,0:T(8,128)(2,1)} %coarse.1, s32[4,128]{1,0:T(4,128)} %bitcast.16), custom_call_target="tpu_custom_call" | custom-call | flops 1000000 | bytes 1048576 | tf_op jit(solution)/shard_map/pack/pallas_call | solution.py:30
  2.2 7.7 %all-to-all-start.1 = ((bf16[8,16,896]{2,1,0:T(8,128)(2,1)}), bf16[8,16,896]{2,1,0:T(8,128)(2,1)S(1)}, u32[]{:S(2)}, u32[]{:S(2)}) async-start(bf16[8,16,896]{2,1,0:T(8,128)(2,1)} %pack.1), calls=%async_computation.1 | async-start | bytes 458752 | tf_op jit(solution)/shard_map/all_to_all | solution.py:335
  9.8 3.6 %route.1 = (bf16[64,16,768]{2,1,0:T(8,128)(2,1)}, s32[1,512]{1,0:T(1,128)}, f32[1,1024]{1,0:T(1,128)}, f32[16,128]{1,0:T(8,128)}) custom-call(s32[1,512]{1,0:T(1,128)} %bitcast.17, s32[16,128]{1,0:T(8,128)} %bitcast.18, bf16[512,768]{1,0:T(8,128)(2,1)} %vectors.3, bf16[1024,768]{1,0:T(8,128)(2,1)} %bitcast.13), custom_call_target="tpu_custom_call" | custom-call | flops 1000000000 | bytes 1048576 | tf_op jit(solution)/shard_map/route/pallas_call | solution.py:30
  13.4 5.4 %all-to-all-done.1 = bf16[8,16,896]{2,1,0:T(8,128)(2,1)S(1)} async-done(((bf16[8,16,896]{2,1,0:T(8,128)(2,1)}), bf16[8,16,896]{2,1,0:T(8,128)(2,1)S(1)}, u32[]{:S(2)}, u32[]{:S(2)}) %all-to-all-start.1) | async-done | bytes 229408 | tf_op jit(solution)/shard_map/all_to_all | solution.py:335
  18.9 0.0 copy-start.1
  18.9 8.1 %all-to-all-start = ((bf16[64,16,768]{2,1,0:T(8,128)(2,1)}), bf16[64,16,768]{2,1,0:T(8,128)(2,1)S(1)}, u32[]{:S(2)}, u32[]{:S(2)}) async-start(bf16[64,16,768]{2,1,0:T(8,128)(2,1)} %get-tuple-element.15), calls=%async_computation | async-start | bytes 3145728 | tf_op jit(solution)/shard_map/all_to_all | solution.py:335
  27.0 0.0 copy-done.1
  27.0 4.0 %collective-permute-start.1 = (bf16[512,768]{1,0:T(8,128)(2,1)S(1)}, bf16[512,768]{1,0:T(8,128)(2,1)S(1)}, u32[]{:S(2)}, u32[]{:S(2)}) collective-permute-start(bf16[512,768]{1,0:T(8,128)(2,1)S(1)} %copy-done.1), channel_id=1, source_target_pairs={{0,64},{64,0},{1,65},{65,1},{2,66},{66,2},{3,67},{67,3},{4,68},{68... | collective-permute-start | bytes 2359304 | tf_op jit(solution)/shard_map/ppermute | solution.py:339
  31.0 2.6 %collective-permute-start = (bf16[512,768]{1,0:T(8,128)(2,1)S(1)}, bf16[512,768]{1,0:T(8,128)(2,1)S(1)}, u32[]{:S(2)}, u32[]{:S(2)}) collective-permute-start(bf16[512,768]{1,0:T(8,128)(2,1)S(1)} %copy-done.1), channel_id=1, source_target_pairs={{0,1},{1,0},{2,3},{3,2},{4,5},{5,4},{6,7},{7,6},{8,9},{9,8},{10,11... | collective-permute-start | bytes 2359304 | tf_op jit(solution)/shard_map/ppermute | solution.py:343
  33.6 0.0 copy-start.3
  33.7 17.9 %all_gather.9.refs_1_.gathered = bf16[512,896]{1,0:T(8,128)(2,1)S(1)} all-gather(bf16[128,896]{1,0:T(8,128)(2,1)S(1)} %bitcast.15), channel_id=1, replica_groups=mesh['zh'=4,'zl'=2,'y'=8,'x'=4,'c'=2] {'x'}, dimensions={0}, use_global_device_ids=true | all-gather | bytes 1146880 | tf_op jit(solution)/shard_map/all_gather | solution.py:402
  51.5 0.0 collective-permute-done.1.refs_0_
  51.5 3.4 %collective-permute-start.2 = (bf16[512,768]{1,0:T(8,128)(2,1)S(1)}, bf16[512,768]{1,0:T(8,128)(2,1)S(1)}, u32[]{:S(2)}, u32[]{:S(2)}) collective-permute-start(bf16[512,768]{1,0:T(8,128)(2,1)S(1)} %after.1.vectors3), channel_id=1, source_target_pairs={{0,1},{1,0},{2,3},{3,2},{4,5},{5,4},{6,7},{7,6},{8,9},{9,8},{10,11... | collective-permute-start | bytes 2359304 | tf_op jit(solution)/shard_map/ppermute | solution.py:343
  54.9 0.0 copy-done.3
  54.9 2.7 %coarse_part.1 = (f32[8,4,16,1024]{3,2,1,0:T(8,128)S(1)}, f32[32,768]{1,0:T(8,128)S(1)}) custom-call(bf16[512,768]{1,0:T(8,128)(2,1)S(1)} %copy-done.1, bf16[512,768]{1,0:T(8,128)(2,1)S(1)} %after.1.vectors3, f32[16,128]{1,0:T(8,128)S(1)} %copy-done.3, bf16[512,896]{1,0:T(8,128)(2,1)S(1)} %all_gather.9.refs_1_.gathered), custom_call_target="tpu_custom_call" | custom-call | flops 2000000000 | bytes 1048576 | tf_op jit(solution)/shard_map/coarse_part/pallas_call | solution.py:30
  57.6 0.0 collective-permute-done.vectors2
  57.6 0.0 collective-permute-done.2.vectors4
  57.6 1.6 %last_part.1 = (f32[8,4,16,1024]{3,2,1,0:T(8,128)S(1)}, bf16[32,768]{1,0:T(8,128)(2,1)S(1)}) custom-call(bf16[512,768]{1,0:T(8,128)(2,1)S(1)} %collective-permute-done.vectors2, bf16[512,768]{1,0:T(8,128)(2,1)S(1)} %collective-permute-done.2.vectors4, bf16[512,896]{1,0:T(8,128)(2,1)S(1)} %all_gather.9.refs_1_.gathered, f32[32,768]{1,0:T(8,128)S(1)} %get-tuple-element.17.so_far), custom_call_target="tpu_custom_call" | custom-call | flops 1000000000 | bytes 1048576 | tf_op jit(solution)/shard_map/last_part/pallas_call | solution.py:30
  59.3 5.5 %all-gather = bf16[128,768]{1,0:T(8,128)(2,1)S(1)} all-gather(bf16[32,768]{1,0:T(8,128)(2,1)S(1)} %get-tuple-element.18), channel_id=2, replica_groups=mesh['zh'=4,'zl'=2,'y'=8,'x'=4,'c'=2] {'zl','c'}, dimensions={0}, use_global_device_ids=true | all-gather | bytes 245760 | tf_op jit(solution)/shard_map/all_gather | solution.py:425
  64.8 0.0 copy-start
  64.8 0.0 copy-start.4
  64.8 1.1 %share.1 = f32[32,4,128]{2,1,0:T(4,128)} custom-call(f32[8,4,16,1024]{3,2,1,0:T(8,128)S(1)} %get-tuple-element.21.weights, f32[8,4,16,1024]{3,2,1,0:T(8,128)S(1)} %get-tuple-element.22.weights2, bf16[4,32,768]{2,1,0:T(8,128)(2,1)S(1)} %bitcast.11), custom_call_target="tpu_custom_call" | custom-call | flops 1000000000 | bytes 1048576 | tf_op jit(solution)/shard_map/share/pallas_call | solution.py:30
  65.8 0.1 all-to-all-done
  66.0 13.1 %all-to-all-start.2 = ((f32[32,4,128]{2,1,0:T(4,128)}), f32[32,4,128]{2,1,0:T(4,128)S(1)}, u32[]{:S(2)}, u32[]{:S(2)}) async-start(f32[32,4,128]{2,1,0:T(4,128)} %share.1), calls=%async_computation.2 | async-start | bytes 131072 | tf_op jit(solution)/shard_map/all_to_all | solution.py:335
  79.1 0.0 copy-done
  79.1 0.0 copy-done.4
  79.1 0.0 copy-start.2
  79.1 5.7 %fine_part.1 = (f32[64,32]{1,0:T(8,128)S(1)}, bf16[1024,768]{1,0:T(8,128)(2,1)}) custom-call(bf16[1024,768]{1,0:T(8,128)(2,1)S(1)} %bitcast.10, bf16[4,32,768]{2,1,0:T(8,128)(2,1)S(1)} %bitcast.12, bf16[1024,768]{1,0:T(8,128)(2,1)S(1)} %bitcast.14, f32[1,1024]{1,0:T(1,128)S(1)} %copy-done.4), custom_call_target="tpu_custom_call" | custom-call | flops 3000000000 | bytes 1048576 | tf_op jit(solution)/shard_map/fine_part/pallas_call | solution.py:30
  84.8 2.9 %all-to-all-done.2.shares = f32[32,4,128]{2,1,0:T(4,128)S(1)} async-done(((f32[32,4,128]{2,1,0:T(4,128)}), f32[32,4,128]{2,1,0:T(4,128)S(1)}, u32[]{:S(2)}, u32[]{:S(2)}) %all-to-all-start.2) | async-done | bytes 65568 | tf_op jit(solution)/shard_map/all_to_all | solution.py:335
  87.7 0.1 answer.1
  87.8 18.8 %all_to_all.20.got = bf16[64,4,128]{2,1,0:T(4,128)(2,1)S(1)} all-to-all(bf16[64,4,128]{2,1,0:T(4,128)(2,1)S(1)} %answer.1), channel_id=1, replica_groups=mesh['zh'=4,'zl'=2,'y'=8,'x'=4,'c'=2] {'y','x','c'}, dimensions={0} | all-to-all | bytes 131072 | tf_op jit(solution)/shard_map/all_to_all | solution.py:335
  106.6 0.0 copy-done.2
  106.6 0.9 finish.1
  (1 shorter events, 0.0 us)
Async XLA Ops:
  2.2 16.7 %all-to-all-start.1 = ((bf16[8,16,896]{2,1,0:T(8,128)(2,1)}), bf16[8,16,896]{2,1,0:T(8,128)(2,1)S(1)}, u32[]{:S(2)}, u32[]{:S(2)}) async-start(bf16[8,16,896]{2,1,0:T(8,128)(2,1)} %pack.1), calls=%async_computation.1 | async-start | bytes 458752 | tf_op jit(solution)/shard_map/all_to_all | solution.py:335
  18.9 8.1 %copy-start.1 = (bf16[512,768]{1,0:T(8,128)(2,1)S(1)}, bf16[512,768]{1,0:T(8,128)(2,1)}, u32[]{:S(2)}) copy-start(bf16[512,768]{1,0:T(8,128)(2,1)} %vectors.3) | copy-start | bytes 2359300
  18.9 47.1 %all-to-all-start = ((bf16[64,16,768]{2,1,0:T(8,128)(2,1)}), bf16[64,16,768]{2,1,0:T(8,128)(2,1)S(1)}, u32[]{:S(2)}, u32[]{:S(2)}) async-start(bf16[64,16,768]{2,1,0:T(8,128)(2,1)} %get-tuple-element.15), calls=%async_computation | async-start | bytes 3145728 | tf_op jit(solution)/shard_map/all_to_all | solution.py:335
  27.0 24.5 %collective-permute-start.1 = (bf16[512,768]{1,0:T(8,128)(2,1)S(1)}, bf16[512,768]{1,0:T(8,128)(2,1)S(1)}, u32[]{:S(2)}, u32[]{:S(2)}) collective-permute-start(bf16[512,768]{1,0:T(8,128)(2,1)S(1)} %copy-done.1), channel_id=1, source_target_pairs={{0,64},{64,0},{1,65},{65,1},{2,66},{66,2},{3,67},{67,3},{4,68},{68... | collective-permute-start | bytes 2359304 | tf_op jit(solution)/shard_map/ppermute | solution.py:339
  31.0 26.6 %collective-permute-start = (bf16[512,768]{1,0:T(8,128)(2,1)S(1)}, bf16[512,768]{1,0:T(8,128)(2,1)S(1)}, u32[]{:S(2)}, u32[]{:S(2)}) collective-permute-start(bf16[512,768]{1,0:T(8,128)(2,1)S(1)} %copy-done.1), channel_id=1, source_target_pairs={{0,1},{1,0},{2,3},{3,2},{4,5},{5,4},{6,7},{7,6},{8,9},{9,8},{10,11... | collective-permute-start | bytes 2359304 | tf_op jit(solution)/shard_map/ppermute | solution.py:343
  33.6 21.2 %copy-start.3 = (f32[16,128]{1,0:T(8,128)S(1)}, f32[16,128]{1,0:T(8,128)}, u32[]{:S(2)}) copy-start(f32[16,128]{1,0:T(8,128)} %get-tuple-element.16.wanted) | copy-start | bytes 24580
  51.5 6.1 %collective-permute-start.2 = (bf16[512,768]{1,0:T(8,128)(2,1)S(1)}, bf16[512,768]{1,0:T(8,128)(2,1)S(1)}, u32[]{:S(2)}, u32[]{:S(2)}) collective-permute-start(bf16[512,768]{1,0:T(8,128)(2,1)S(1)} %after.1.vectors3), channel_id=1, source_target_pairs={{0,1},{1,0},{2,3},{3,2},{4,5},{5,4},{6,7},{7,6},{8,9},{9,8},{10,11... | collective-permute-start | bytes 2359304 | tf_op jit(solution)/shard_map/ppermute | solution.py:343
  64.8 14.3 %copy-start = (bf16[4,256,768]{2,1,0:T(8,128)(2,1)S(1)}, bf16[4,256,768]{2,1,0:T(8,128)(2,1)}, u32[]{:S(2)}) copy-start(bf16[4,256,768]{2,1,0:T(8,128)(2,1)} %param.9) | copy-start | bytes 4718596
  64.8 14.3 %copy-start.4 = (f32[1,1024]{1,0:T(1,128)S(1)}, f32[1,1024]{1,0:T(1,128)}, u32[]{:S(2)}) copy-start(f32[1,1024]{1,0:T(1,128)} %get-tuple-element.19.book_squares) | copy-start | bytes 12292
  66.0 21.7 %all-to-all-start.2 = ((f32[32,4,128]{2,1,0:T(4,128)}), f32[32,4,128]{2,1,0:T(4,128)S(1)}, u32[]{:S(2)}, u32[]{:S(2)}) async-start(f32[32,4,128]{2,1,0:T(4,128)} %share.1), calls=%async_computation.2 | async-start | bytes 131072 | tf_op jit(solution)/shard_map/all_to_all | solution.py:335
  79.1 27.5 %copy-start.2 = (s32[1,512]{1,0:T(1,128)S(1)}, s32[1,512]{1,0:T(1,128)}, u32[]{:S(2)}) copy-start(s32[1,512]{1,0:T(1,128)} %get-tuple-element.23.place) | copy-start | bytes 6148

commit v6 on v5

--- a/solution.py
+++ b/solution.py
@@ -222,6 +222,7 @@
         highest = functools.reduce(jnp.maximum, tops)
         total = sum(n * jnp.exp(top - highest) for n, top in zip(totals, tops, strict=True))
         factors.append(jnp.exp(tops[0] - highest) / total)
+    lines = []
     for b in range(Y // 2):
         lanes = jnp.zeros((128, 128), f32)
         for side, factor in enumerate(factors):
@@ -229,8 +230,8 @@
             probs = source[2 * b : 2 * b + 2, :, :, first : first + rows].reshape(128, rows) * factor
             for j in range(rows // 128):
                 lanes = lanes + probs[:, j * 128 : (j + 1) * 128]
-        share = jnp.sum(jnp.transpose(lanes), axis=0, keepdims=True)
-        shares[:, b : b + 1, :] = jnp.broadcast_to(share[None], (shares.shape[0], 1, 128))
+        lines.append(jnp.sum(jnp.transpose(lanes), axis=0, keepdims=True))
+    shares[...] = jnp.broadcast_to(jnp.concatenate(lines, axis=0)[None], shares.shape).astype(bf16)
 
 
 def fine_kernel(
@@ -257,15 +258,16 @@
         residual[at] = moved
         moved_squares.append(as_row(row_squares(moved)))
     parts = []
-    masses = [jnp.zeros((fine, 1), f32)] * SLOTS
+    masses = [jnp.zeros((fine, 128), f32)] * SLOTS
     for b in range(rows // block):
         at = slice(b * block, (b + 1) * block)
         slot = local[:, at]
         inside = [slot == s for s in range(SLOTS)]
-        distance = jnp.zeros((fine, block), f32)
-        for s in range(SLOTS):
-            products = dot(book[s * fine : (s + 1) * fine], residual[at], 1, 1)
-            distance = jnp.where(inside[s], moved_squares[b] + squares[s] - 2.0 * products, distance)
+        distance = squares[0] - 2.0 * dot(book[0:fine], residual[at], 1, 1)
+        for s in range(1, SLOTS):
+            here = squares[s] - 2.0 * dot(book[s * fine : (s + 1) * fine], residual[at], 1, 1)
+            distance = jnp.where(inside[s], here, distance)
+        distance = moved_squares[b] + distance
         score = -sharpness * distance
         e = jnp.exp(score - jnp.max(score, axis=0, keepdims=True))
         weight = e * ((slot >= 0.0).astype(f32) / jnp.sum(e, axis=0, keepdims=True))
@@ -273,7 +275,8 @@
         for s in range(SLOTS):
             only = jnp.where(inside[s], weight, 0.0)
             weights[s * fine : (s + 1) * fine, at] = only.astype(bf16)
-            masses[s] = masses[s] + jnp.sum(only, axis=1, keepdims=True)
+            masses[s] = masses[s] + only[:, :128] + only[:, 128:]
+    masses = [jnp.sum(lanes, axis=1, keepdims=True) for lanes in masses]
     row = jnp.concatenate(parts, axis=1)
     places = (iota((cap, rows), 1) % cap == iota((cap, rows), 0)).astype(bf16)
     at_owner = iota((owners, rows), 1) // cap == iota((owners, rows), 0)
@@ -288,7 +291,7 @@
 
 def answer_kernel(spread, shares, out):
     owners, width = spread.shape
-    total = jnp.sum(jnp.sum(shares[...].reshape(Z // PAIR, PAIR, X, 4, 128), axis=2), axis=0).reshape(X, 2, 128)
+    total = jnp.sum(jnp.sum(shares[...].astype(f32).reshape(Z // PAIR, PAIR, X, 4, 128), axis=2), axis=0).reshape(X, 2, 128)
     quarter = jnp.sum(jnp.where(iota(total.shape, 0) == lax.axis_index("x"), total, 0.0), axis=0)
     line = jnp.concatenate([spread[...], jnp.zeros((owners, 128 - width), f32)], axis=1)
     top = jnp.broadcast_to(quarter[None], (owners, 2, 128))
@@ -425,7 +428,7 @@
     heard = lax.all_gather(told, FOUR, axis=0)
     shares = call(
         functools.partial(share_kernel, rows),
-        shaped((Z * X, 4, 128), f32),
+        shaped((Z * X, 4, 128), bf16),
         [],
         [weights, weights2, heard],
         "share",

time: 108 us -> 108 us (level)
  transfers between devices with their start and end apart: 6 -> 6, of which waited for: 3 -> 3; matrix products, arithmetic and copies ran while one was open for 0% -> 0% of each run, Pallas kernels for 14% -> 13%
where the time goes in v6:
time: 108 us; the launch traced here: 107 us
  blocking collectives  42 us (39%)
  starting transfers between devices  38.9 us (36%)
  Pallas kernels  17 us (16%)
  waiting for transfers between devices  8.57 us (8%)
    all_to_all x3, starting transfers between devices, exchange(): return lax.all_to_all(x, axes, 0, 0, tiled=True)  28.9 us
    all_to_all x1, blocking collectives, exchange(): return lax.all_to_all(x, axes, 0, 0, tiled=True)  18.6 us
    all_gather x1, blocking collectives, on_device(): gathered = lax.all_gather(first, 'x', axis=0, tiled=True)  17.9 us
    pallas_call x8, Pallas kernels, call(): pl.pallas_call(body, out_shape=out_shape, in_specs=[SMEM] * len(scalars)...  17 us
    all_to_all x3, waiting for transfers between devices, exchange(): return lax.all_to_all(x, axes, 0, 0, tiled=True)  8.57 us
    ppermute x2, starting transfers between devices, from_partner(): return lax.ppermute(x, 'c', [(0, 1), (1, 0)])  6 us
    all_gather x1, blocking collectives, on_device(): heard = lax.all_gather(told, FOUR, axis=0)  5.51 us
    ppermute x1, starting transfers between devices, from_neighbour(): return lax.ppermute(x, 'zl', [(0, 1), (1, 0)])  4 us
  transfers between devices with their start and end apart: 6, of which 3 were waited for; matrix products, arithmetic and copies ran while one was open for 0% of the time, Pallas kernels for 13%

profile of v6, /device:TPU:1, one launch (start us, length us, event | category | flops | bytes accessed | tf_op | source)
XLA Modules:
  0.0 107.2 jit_solution(8387448306532342222)
XLA Ops:
  0.6 1.5 %pack.1 = bf16[8,16,896]{2,1,0:T(8,128)(2,1)} custom-call(bf16[32,768]{1,0:T(8,128)(2,1)} %coarse.1, s32[4,128]{1,0:T(4,128)} %bitcast.16), custom_call_target="tpu_custom_call" | custom-call | flops 1000000 | bytes 1048576 | tf_op jit(solution)/shard_map/pack/pallas_call | solution.py:30
  2.2 7.7 %all-to-all-start.1 = ((bf16[8,16,896]{2,1,0:T(8,128)(2,1)}), bf16[8,16,896]{2,1,0:T(8,128)(2,1)S(1)}, u32[]{:S(2)}, u32[]{:S(2)}) async-start(bf16[8,16,896]{2,1,0:T(8,128)(2,1)} %pack.1), calls=%async_computation.1 | async-start | bytes 458752 | tf_op jit(solution)/shard_map/all_to_all | solution.py:338
  9.8 3.6 %route.1 = (bf16[64,16,768]{2,1,0:T(8,128)(2,1)}, s32[1,512]{1,0:T(1,128)}, f32[1,1024]{1,0:T(1,128)}, f32[16,128]{1,0:T(8,128)}) custom-call(s32[1,512]{1,0:T(1,128)} %bitcast.17, s32[16,128]{1,0:T(8,128)} %bitcast.18, bf16[512,768]{1,0:T(8,128)(2,1)} %vectors.3, bf16[1024,768]{1,0:T(8,128)(2,1)} %bitcast.13), custom_call_target="tpu_custom_call" | custom-call | flops 1000000000 | bytes 1048576 | tf_op jit(solution)/shard_map/route/pallas_call | solution.py:30
  13.4 5.4 %all-to-all-done.1 = bf16[8,16,896]{2,1,0:T(8,128)(2,1)S(1)} async-done(((bf16[8,16,896]{2,1,0:T(8,128)(2,1)}), bf16[8,16,896]{2,1,0:T(8,128)(2,1)S(1)}, u32[]{:S(2)}, u32[]{:S(2)}) %all-to-all-start.1) | async-done | bytes 229408 | tf_op jit(solution)/shard_map/all_to_all | solution.py:338
  18.9 0.0 copy-start.1
  18.9 8.1 %all-to-all-start = ((bf16[64,16,768]{2,1,0:T(8,128)(2,1)}), bf16[64,16,768]{2,1,0:T(8,128)(2,1)S(1)}, u32[]{:S(2)}, u32[]{:S(2)}) async-start(bf16[64,16,768]{2,1,0:T(8,128)(2,1)} %get-tuple-element.15), calls=%async_computation | async-start | bytes 3145728 | tf_op jit(solution)/shard_map/all_to_all | solution.py:338
  27.0 0.0 copy-done.1
  27.0 4.0 %collective-permute-start.1 = (bf16[512,768]{1,0:T(8,128)(2,1)S(1)}, bf16[512,768]{1,0:T(8,128)(2,1)S(1)}, u32[]{:S(2)}, u32[]{:S(2)}) collective-permute-start(bf16[512,768]{1,0:T(8,128)(2,1)S(1)} %copy-done.1), channel_id=1, source_target_pairs={{0,64},{64,0},{1,65},{65,1},{2,66},{66,2},{3,67},{67,3},{4,68},{68... | collective-permute-start | bytes 2359304 | tf_op jit(solution)/shard_map/ppermute | solution.py:342
  31.0 2.6 %collective-permute-start = (bf16[512,768]{1,0:T(8,128)(2,1)S(1)}, bf16[512,768]{1,0:T(8,128)(2,1)S(1)}, u32[]{:S(2)}, u32[]{:S(2)}) collective-permute-start(bf16[512,768]{1,0:T(8,128)(2,1)S(1)} %copy-done.1), channel_id=1, source_target_pairs={{0,1},{1,0},{2,3},{3,2},{4,5},{5,4},{6,7},{7,6},{8,9},{9,8},{10,11... | collective-permute-start | bytes 2359304 | tf_op jit(solution)/shard_map/ppermute | solution.py:346
  33.6 0.0 copy-start.3
  33.7 17.9 %all_gather.9.refs_1_.gathered = bf16[512,896]{1,0:T(8,128)(2,1)S(1)} all-gather(bf16[128,896]{1,0:T(8,128)(2,1)S(1)} %bitcast.15), channel_id=1, replica_groups=mesh['zh'=4,'zl'=2,'y'=8,'x'=4,'c'=2] {'x'}, dimensions={0}, use_global_device_ids=true | all-gather | bytes 1146880 | tf_op jit(solution)/shard_map/all_gather | solution.py:405
  51.5 0.0 collective-permute-done.1.refs_0_
  51.5 3.4 %collective-permute-start.2 = (bf16[512,768]{1,0:T(8,128)(2,1)S(1)}, bf16[512,768]{1,0:T(8,128)(2,1)S(1)}, u32[]{:S(2)}, u32[]{:S(2)}) collective-permute-start(bf16[512,768]{1,0:T(8,128)(2,1)S(1)} %after.1.vectors3), channel_id=1, source_target_pairs={{0,1},{1,0},{2,3},{3,2},{4,5},{5,4},{6,7},{7,6},{8,9},{9,8},{10,11... | collective-permute-start | bytes 2359304 | tf_op jit(solution)/shard_map/ppermute | solution.py:346
  54.9 0.0 copy-done.3
  54.9 2.7 %coarse_part.1 = (f32[8,4,16,1024]{3,2,1,0:T(8,128)S(1)}, f32[32,768]{1,0:T(8,128)S(1)}) custom-call(bf16[512,768]{1,0:T(8,128)(2,1)S(1)} %copy-done.1, bf16[512,768]{1,0:T(8,128)(2,1)S(1)} %after.1.vectors3, f32[16,128]{1,0:T(8,128)S(1)} %copy-done.3, bf16[512,896]{1,0:T(8,128)(2,1)S(1)} %all_gather.9.refs_1_.gathered), custom_call_target="tpu_custom_call" | custom-call | flops 2000000000 | bytes 1048576 | tf_op jit(solution)/shard_map/coarse_part/pallas_call | solution.py:30
  57.6 0.0 collective-permute-done.vectors2
  57.6 0.0 collective-permute-done.2.vectors4
  57.6 1.6 %last_part.1 = (f32[8,4,16,1024]{3,2,1,0:T(8,128)S(1)}, bf16[32,768]{1,0:T(8,128)(2,1)S(1)}) custom-call(bf16[512,768]{1,0:T(8,128)(2,1)S(1)} %collective-permute-done.vectors2, bf16[512,768]{1,0:T(8,128)(2,1)S(1)} %collective-permute-done.2.vectors4, bf16[512,896]{1,0:T(8,128)(2,1)S(1)} %all_gather.9.refs_1_.gathered, f32[32,768]{1,0:T(8,128)S(1)} %get-tuple-element.17.so_far), custom_call_target="tpu_custom_call" | custom-call | flops 1000000000 | bytes 1048576 | tf_op jit(solution)/shard_map/last_part/pallas_call | solution.py:30
  59.3 5.5 %all-gather = bf16[128,768]{1,0:T(8,128)(2,1)S(1)} all-gather(bf16[32,768]{1,0:T(8,128)(2,1)S(1)} %get-tuple-element.18), channel_id=2, replica_groups=mesh['zh'=4,'zl'=2,'y'=8,'x'=4,'c'=2] {'zl','c'}, dimensions={0}, use_global_device_ids=true | all-gather | bytes 245760 | tf_op jit(solution)/shard_map/all_gather | solution.py:428
  64.8 0.0 copy-start
  64.8 0.0 copy-start.4
  64.8 1.1 share.1
  65.8 0.1 all-to-all-done
  66.0 13.1 %all-to-all-start.2 = ((bf16[32,4,128]{2,1,0:T(4,128)(2,1)}), bf16[32,4,128]{2,1,0:T(4,128)(2,1)S(1)}, u32[]{:S(2)}, u32[]{:S(2)}) async-start(bf16[32,4,128]{2,1,0:T(4,128)(2,1)} %share.1), calls=%async_computation.2 | async-start | bytes 65536 | tf_op jit(solution)/shard_map/all_to_all | solution.py:338
  79.1 0.0 copy-done
  79.1 0.0 copy-done.4
  79.1 0.0 copy-start.2
  79.1 5.5 %fine_part.1 = (f32[64,32]{1,0:T(8,128)S(1)}, bf16[1024,768]{1,0:T(8,128)(2,1)}) custom-call(bf16[1024,768]{1,0:T(8,128)(2,1)S(1)} %bitcast.10, bf16[4,32,768]{2,1,0:T(8,128)(2,1)S(1)} %bitcast.12, bf16[1024,768]{1,0:T(8,128)(2,1)S(1)} %bitcast.14, f32[1,1024]{1,0:T(1,128)S(1)} %copy-done.4), custom_call_target="tpu_custom_call" | custom-call | flops 3000000000 | bytes 1048576 | tf_op jit(solution)/shard_map/fine_part/pallas_call | solution.py:30
  84.6 3.0 %all-to-all-done.2.shares = bf16[32,4,128]{2,1,0:T(4,128)(2,1)S(1)} async-done(((bf16[32,4,128]{2,1,0:T(4,128)(2,1)}), bf16[32,4,128]{2,1,0:T(4,128)(2,1)S(1)}, u32[]{:S(2)}, u32[]{:S(2)}) %all-to-all-start.2) | async-done | bytes 32800 | tf_op jit(solution)/shard_map/all_to_all | solution.py:338
  87.6 0.1 answer.1
  87.6 18.6 %all_to_all.20.got = bf16[64,4,128]{2,1,0:T(4,128)(2,1)S(1)} all-to-all(bf16[64,4,128]{2,1,0:T(4,128)(2,1)S(1)} %answer.1), channel_id=1, replica_groups=mesh['zh'=4,'zl'=2,'y'=8,'x'=4,'c'=2] {'y','x','c'}, dimensions={0} | all-to-all | bytes 131072 | tf_op jit(solution)/shard_map/all_to_all | solution.py:338
  106.3 0.0 copy-done.2
  106.3 0.9 finish.1
  (1 shorter events, 0.0 us)
Async XLA Ops:
  2.2 16.7 %all-to-all-start.1 = ((bf16[8,16,896]{2,1,0:T(8,128)(2,1)}), bf16[8,16,896]{2,1,0:T(8,128)(2,1)S(1)}, u32[]{:S(2)}, u32[]{:S(2)}) async-start(bf16[8,16,896]{2,1,0:T(8,128)(2,1)} %pack.1), calls=%async_computation.1 | async-start | bytes 458752 | tf_op jit(solution)/shard_map/all_to_all | solution.py:338
  18.9 8.1 %copy-start.1 = (bf16[512,768]{1,0:T(8,128)(2,1)S(1)}, bf16[512,768]{1,0:T(8,128)(2,1)}, u32[]{:S(2)}) copy-start(bf16[512,768]{1,0:T(8,128)(2,1)} %vectors.3) | copy-start | bytes 2359300
  18.9 47.1 %all-to-all-start = ((bf16[64,16,768]{2,1,0:T(8,128)(2,1)}), bf16[64,16,768]{2,1,0:T(8,128)(2,1)S(1)}, u32[]{:S(2)}, u32[]{:S(2)}) async-start(bf16[64,16,768]{2,1,0:T(8,128)(2,1)} %get-tuple-element.15), calls=%async_computation | async-start | bytes 3145728 | tf_op jit(solution)/shard_map/all_to_all | solution.py:338
  27.0 24.5 %collective-permute-start.1 = (bf16[512,768]{1,0:T(8,128)(2,1)S(1)}, bf16[512,768]{1,0:T(8,128)(2,1)S(1)}, u32[]{:S(2)}, u32[]{:S(2)}) collective-permute-start(bf16[512,768]{1,0:T(8,128)(2,1)S(1)} %copy-done.1), channel_id=1, source_target_pairs={{0,64},{64,0},{1,65},{65,1},{2,66},{66,2},{3,67},{67,3},{4,68},{68... | collective-permute-start | bytes 2359304 | tf_op jit(solution)/shard_map/ppermute | solution.py:342
  31.0 26.6 %collective-permute-start = (bf16[512,768]{1,0:T(8,128)(2,1)S(1)}, bf16[512,768]{1,0:T(8,128)(2,1)S(1)}, u32[]{:S(2)}, u32[]{:S(2)}) collective-permute-start(bf16[512,768]{1,0:T(8,128)(2,1)S(1)} %copy-done.1), channel_id=1, source_target_pairs={{0,1},{1,0},{2,3},{3,2},{4,5},{5,4},{6,7},{7,6},{8,9},{9,8},{10,11... | collective-permute-start | bytes 2359304 | tf_op jit(solution)/shard_map/ppermute | solution.py:346
  33.6 21.2 %copy-start.3 = (f32[16,128]{1,0:T(8,128)S(1)}, f32[16,128]{1,0:T(8,128)}, u32[]{:S(2)}) copy-start(f32[16,128]{1,0:T(8,128)} %get-tuple-element.16.wanted) | copy-start | bytes 24580
  51.5 6.1 %collective-permute-start.2 = (bf16[512,768]{1,0:T(8,128)(2,1)S(1)}, bf16[512,768]{1,0:T(8,128)(2,1)S(1)}, u32[]{:S(2)}, u32[]{:S(2)}) collective-permute-start(bf16[512,768]{1,0:T(8,128)(2,1)S(1)} %after.1.vectors3), channel_id=1, source_target_pairs={{0,1},{1,0},{2,3},{3,2},{4,5},{5,4},{6,7},{7,6},{8,9},{9,8},{10,11... | collective-permute-start | bytes 2359304 | tf_op jit(solution)/shard_map/ppermute | solution.py:346
  64.8 14.3 %copy-start = (bf16[4,256,768]{2,1,0:T(8,128)(2,1)S(1)}, bf16[4,256,768]{2,1,0:T(8,128)(2,1)}, u32[]{:S(2)}) copy-start(bf16[4,256,768]{2,1,0:T(8,128)(2,1)} %param.9) | copy-start | bytes 4718596
  64.8 14.3 %copy-start.4 = (f32[1,1024]{1,0:T(1,128)S(1)}, f32[1,1024]{1,0:T(1,128)}, u32[]{:S(2)}) copy-start(f32[1,1024]{1,0:T(1,128)} %get-tuple-element.19.book_squares) | copy-start | bytes 12292
  66.0 21.6 %all-to-all-start.2 = ((bf16[32,4,128]{2,1,0:T(4,128)(2,1)}), bf16[32,4,128]{2,1,0:T(4,128)(2,1)S(1)}, u32[]{:S(2)}, u32[]{:S(2)}) async-start(bf16[32,4,128]{2,1,0:T(4,128)(2,1)} %share.1), calls=%async_computation.2 | async-start | bytes 65536 | tf_op jit(solution)/shard_map/all_to_all | solution.py:338
  79.1 27.2 %copy-start.2 = (s32[1,512]{1,0:T(1,128)S(1)}, s32[1,512]{1,0:T(1,128)}, u32[]{:S(2)}) copy-start(s32[1,512]{1,0:T(1,128)} %get-tuple-element.23.place) | copy-start | bytes 6148
